TPU v7x, 32 devices: a whole 2x2x4 slice. The times are simulated.
32 devices in a mesh: dp: 16 (over z, y, x), tensor: 2 (over core).
Axes of the slice: x: 2, y: 2, z: 4, core: 2. Of those that a mesh axis runs over, the one named last changes fastest.
Arguments:
- tokens: bfloat16 [16384, 1024], P(('dp', 'tensor')), may hold values from -6 to 6
- cotangent: bfloat16 [16384, 1024], P(('dp', 'tensor')), may hold values from -6 to 6
- species_ids: int32 [16], P('dp'), may hold values from 0 to 849, as said below
- species_counts: int32 [850], replicated, may hold values from 1000 to 15992
- norm1_gain: float32 [1024], replicated, may hold values from 0.1 to 1.9
- norm1_bias: float32 [1024], replicated, may hold values from -3 to 3
- w_query: bfloat16 [1024, 1024], P(None, 'tensor'), may hold values from -0.1875 to 0.1875
- w_key: bfloat16 [1024, 1024], P(None, 'tensor'), may hold values from -0.1875 to 0.1875
- w_value: bfloat16 [1024, 1024], P(None, 'tensor'), may hold values from -0.1875 to 0.1875
- w_out: bfloat16 [1024, 1024], P('tensor'), may hold values from -4 to 4
- norm2_gain: float32 [1024], replicated, may hold values from 0.1 to 1.9
- norm2_bias: float32 [1024], replicated, may hold values from -3 to 3
- w_gate: bfloat16 [1024, 4096], P(None, 'tensor'), may hold values from -0.1875 to 0.1875
- w_up: bfloat16 [1024, 4096], P(None, 'tensor'), may hold values from -0.1875 to 0.1875
- w_down: bfloat16 [4096, 1024], P('tensor'), may hold values from -0.09375 to 0.09375
Outputs:
- output: bfloat16 [16384, 1024], P(('dp', 'tensor'))
- input_grad: float32 [16384, 1024], P(('dp', 'tensor'))
- grad_norm1_gain: float32 [1024], replicated
- grad_norm1_bias: float32 [1024], replicated
- grad_query: float32 [1024, 1024], P(None, 'tensor')
- grad_key: float32 [1024, 1024], P(None, 'tensor')
- grad_value: float32 [1024, 1024], P(None, 'tensor')
- grad_out: float32 [1024, 1024], P('tensor')
- grad_norm2_gain: float32 [1024], replicated
- grad_norm2_bias: float32 [1024], replicated
- grad_gate: float32 [1024, 4096], P(None, 'tensor')
- grad_up: float32 [1024, 4096], P(None, 'tensor')
- grad_down: float32 [4096, 1024], P('tensor')
Inputs may be any that keep to these rules, and one draw needn't show every extreme that they name: `species_ids`: each window's species, an index into species_counts; 0 and 849 are named in every draw.
All inputs are finite; a program needn't handle non-finite values.
Results may differ from a plain program's by a relative error of at most 0.02.
Values may be sent and summed in bfloat16 or wider, within the bound.
No kernel may reach another device: no remote copies, remote signals or barrier semaphores. Data moves between devices by JAX's collectives and lax.ppermute only.
A program may use at most 256 MiB of HBM per device.

v0:
```python
import jax
import jax.numpy as jnp
from jax import lax
from jax.sharding import PartitionSpec as P

HD = 64
LEN = 1024
QBLOCK = 512
SPECIES = 850
WIN_DEV = 1


eps_norm = 1e-05


def row_norm(values):
    center = values - jnp.mean(values, axis=-1, keepdims=True)
    inv_std = lax.rsqrt(jnp.mean(center * center, axis=-1, keepdims=True) + eps_norm)
    return (center * inv_std, inv_std)


def norm_back(upstream, normed, inv_std, gain_vec):
    scaled_up = upstream * gain_vec
    mean_one = jnp.mean(scaled_up, axis=-1, keepdims=True)
    mean_two = jnp.mean(scaled_up * normed, axis=-1, keepdims=True)
    return inv_std * (scaled_up - mean_one - normed * mean_two)


def turn_half(values, head_count):
    dims_in = values.shape
    pieces = values.reshape(dims_in[:-1] + (head_count, 2, dims_in[-1] // (2 * head_count)))
    turned = jnp.concatenate([-pieces[..., 1:, :], pieces[..., :1, :]], axis=-2)
    return turned.reshape(dims_in)


def rotary_tables(head_count):
    half_dim = HD // 2
    inv_freq = 1.0 / 10000.0 ** (jnp.arange(half_dim, dtype=jnp.float32) * 2.0 / HD)
    angles = jnp.arange(LEN, dtype=jnp.float32)[:, None] * inv_freq[None, :]
    angles = jnp.concatenate([angles, angles], axis=1)
    angles = jnp.tile(angles, (1, head_count))
    return (jnp.cos(angles), jnp.sin(angles))


def inner_rows(left_mat, right_mat):
    return lax.dot_general(
        left_mat, right_mat, (((0,), (0,)), ((), ())), preferred_element_type=jnp.float32
    )


def times_transposed(left_mat, right_mat):
    return lax.dot_general(
        left_mat, right_mat, (((1,), (1,)), ((), ())), preferred_element_type=jnp.float32
    )


def per_device(
    tokens,
    cotangent,
    species_ids,
    species_counts,
    norm1_gain,
    norm1_bias,
    w_query,
    w_key,
    w_value,
    w_out,
    norm2_gain,
    norm2_bias,
    w_gate,
    w_up,
    w_down,
):
    own_count = tokens.shape[0]
    group_size = lax.axis_size("tensor")
    group_index = lax.axis_index("tensor")
    all_count = own_count * group_size
    head_cols = w_query.shape[1]
    heads_here = head_cols // HD
    blocks_per = LEN // QBLOCK
    block_total = WIN_DEV * blocks_per
    score_scale = HD ** (-0.5)

    def own_slice(values):
        return lax.dynamic_slice_in_dim(values, group_index * own_count, own_count, 0)

    tok_all = lax.all_gather(tokens, "tensor", axis=0, tiled=True).astype(jnp.float32)
    normed1_all, inv1_all = row_norm(tok_all)
    normed_in = (normed1_all * norm1_gain + norm1_bias).astype(jnp.bfloat16)
    normed1 = own_slice(normed1_all)
    inv1 = own_slice(inv1_all)
    cos_tab, sin_tab = rotary_tables(heads_here)

    def rotate(values):
        shaped = values.reshape(WIN_DEV, LEN, head_cols)
        return shaped * cos_tab + turn_half(shaped, heads_here) * sin_tab

    def unrotate(grads):
        return grads * cos_tab - turn_half(grads * sin_tab, heads_here)

    query_low = rotate(jnp.dot(normed_in, w_query, preferred_element_type=jnp.float32)).astype(
        jnp.bfloat16
    )
    key_low = rotate(jnp.dot(normed_in, w_key, preferred_element_type=jnp.float32)).astype(
        jnp.bfloat16
    )
    value_low = jnp.dot(normed_in, w_value, preferred_element_type=jnp.float32).astype(jnp.bfloat16)
    q_blocks = query_low.reshape(block_total, QBLOCK, heads_here, HD)
    key_blocks = key_low.reshape(WIN_DEV, LEN, heads_here, HD)
    value_blocks = value_low.reshape(WIN_DEV, LEN, heads_here, HD)
    block_window = jnp.arange(block_total, dtype=jnp.int32) // blocks_per

    def attend(block_item):
        q_block, window = block_item
        k_win = lax.dynamic_index_in_dim(key_blocks, window, 0, keepdims=False)
        v_win = lax.dynamic_index_in_dim(value_blocks, window, 0, keepdims=False)
        scores = (
            jnp.einsum("qhd,khd->hqk", q_block, k_win, preferred_element_type=jnp.float32)
            * score_scale
        )
        row_max = jnp.max(scores, axis=-1, keepdims=True)
        exp_scores = jnp.exp(scores - row_max)
        row_total = jnp.sum(exp_scores, axis=-1, keepdims=True)
        prob_low = (exp_scores / row_total).astype(jnp.bfloat16)
        context_blk = jnp.einsum(
            "hqk,khd->qhd", prob_low, v_win, preferred_element_type=jnp.float32
        )
        return (context_blk.astype(jnp.bfloat16), row_max[..., 0] + jnp.log(row_total[..., 0]))

    context_blocks, log_totals = lax.map(attend, (q_blocks, block_window))
    context = context_blocks.reshape(all_count, head_cols)
    branch_all = lax.psum(
        jnp.dot(context, w_out, preferred_element_type=jnp.float32).astype(jnp.bfloat16), "tensor"
    ).astype(jnp.float32)
    mixed_all = tok_all + branch_all
    normed2_all, inv2_all = row_norm(mixed_all)
    normed_mid = (normed2_all * norm2_gain + norm2_bias).astype(jnp.bfloat16)
    mixed_own = own_slice(mixed_all)
    normed2 = own_slice(normed2_all)
    inv2 = own_slice(inv2_all)
    gate_pre = jnp.dot(normed_mid, w_gate, preferred_element_type=jnp.float32)
    up_pre = jnp.dot(normed_mid, w_up, preferred_element_type=jnp.float32)
    sigmoid_gate = 1.0 / (1.0 + jnp.exp(-gate_pre))
    silu_gate = gate_pre * sigmoid_gate
    hidden = (silu_gate * up_pre).astype(jnp.bfloat16)
    output = (
        mixed_own
        + lax.psum_scatter(
            jnp.dot(hidden, w_down, preferred_element_type=jnp.float32).astype(jnp.bfloat16),
            "tensor",
            scatter_dimension=0,
            tiled=True,
        ).astype(jnp.float32)
    ).astype(jnp.bfloat16)
    picked = species_ids[:, None] == jnp.arange(SPECIES, dtype=jnp.int32)[None, :]
    counts_mine = jnp.sum(jnp.where(picked, species_counts[None, :], 0), axis=1)
    inverse = 1.0 / counts_mine.astype(jnp.float32)
    inv_total = lax.psum(jnp.sum(inverse), "dp")
    window_weight = WIN_DEV * lax.axis_size("dp") * inverse / inv_total
    row_window = (group_index * own_count + jnp.arange(own_count, dtype=jnp.int32)) // LEN
    row_weight = jnp.sum(
        jnp.where(
            row_window[:, None] == jnp.arange(WIN_DEV, dtype=jnp.int32)[None, :],
            window_weight[None, :],
            0.0,
        ),
        axis=1,
    )
    grad_own = (cotangent.astype(jnp.float32) * row_weight[:, None]).astype(jnp.bfloat16)
    grad_all = lax.all_gather(grad_own, "tensor", axis=0, tiled=True)
    grad_down = inner_rows(hidden, grad_all)
    d_hidden = times_transposed(grad_all, w_down)
    d_gate = (d_hidden * up_pre * (sigmoid_gate * (1.0 + gate_pre * (1.0 - sigmoid_gate)))).astype(
        jnp.bfloat16
    )
    d_up = (d_hidden * silu_gate).astype(jnp.bfloat16)
    grad_gate = inner_rows(normed_mid, d_gate)
    grad_up = inner_rows(normed_mid, d_up)
    d_mid = lax.psum_scatter(
        (times_transposed(d_gate, w_gate) + times_transposed(d_up, w_up)).astype(jnp.bfloat16),
        "tensor",
        scatter_dimension=0,
        tiled=True,
    ).astype(jnp.float32)
    gain2_sum = jnp.sum(d_mid * normed2, axis=0)
    bias2_sum = jnp.sum(d_mid, axis=0)
    d_mixed = grad_own.astype(jnp.float32) + norm_back(d_mid, normed2, inv2, norm2_gain)
    d_branch = lax.all_gather(d_mixed.astype(jnp.bfloat16), "tensor", axis=0, tiled=True)
    grad_out = inner_rows(context, d_branch)
    d_context = times_transposed(d_branch, w_out).astype(jnp.bfloat16)
    d_blocks = d_context.reshape(block_total, QBLOCK, heads_here, HD)

    def attend_back(block_item):
        q_block, log_block, d_block, window = block_item
        k_win = lax.dynamic_index_in_dim(key_blocks, window, 0, keepdims=False)
        v_win = lax.dynamic_index_in_dim(value_blocks, window, 0, keepdims=False)
        scores = (
            jnp.einsum("qhd,khd->hqk", q_block, k_win, preferred_element_type=jnp.float32)
            * score_scale
        )
        prob_full = jnp.exp(scores - log_block[..., None])
        d_prob = jnp.einsum("qhd,khd->hqk", d_block, v_win, preferred_element_type=jnp.float32)
        d_scores = (
            prob_full * (d_prob - jnp.sum(prob_full * d_prob, axis=-1, keepdims=True))
        ).astype(jnp.bfloat16)
        d_query_blk = (
            jnp.einsum("hqk,khd->qhd", d_scores, k_win, preferred_element_type=jnp.float32)
            * score_scale
        )
        d_key_blk = (
            jnp.einsum("hqk,qhd->khd", d_scores, q_block, preferred_element_type=jnp.float32)
            * score_scale
        )
        d_value_blk = jnp.einsum(
            "hqk,qhd->khd",
            prob_full.astype(jnp.bfloat16),
            d_block,
            preferred_element_type=jnp.float32,
        )
        return (d_query_blk, d_key_blk, d_value_blk)

    dq_blocks, dk_parts, dv_parts = lax.map(
        attend_back, (q_blocks, log_totals, d_blocks, block_window)
    )
    dq_rot = dq_blocks.reshape(WIN_DEV, LEN, head_cols)
    dk_rot = jnp.sum(dk_parts.reshape(WIN_DEV, blocks_per, LEN, head_cols), axis=1)
    dv_sum = jnp.sum(dv_parts.reshape(WIN_DEV, blocks_per, LEN, head_cols), axis=1)
    d_query = unrotate(dq_rot).reshape(all_count, head_cols).astype(jnp.bfloat16)
    d_key = unrotate(dk_rot).reshape(all_count, head_cols).astype(jnp.bfloat16)
    d_value = dv_sum.reshape(all_count, head_cols).astype(jnp.bfloat16)
    grad_query = inner_rows(normed_in, d_query)
    grad_key = inner_rows(normed_in, d_key)
    grad_value = inner_rows(normed_in, d_value)
    part_q = times_transposed(d_query, w_query)
    part_k = times_transposed(d_key, w_key)
    part_v = times_transposed(d_value, w_value)
    d_in = lax.psum_scatter(
        (part_q + part_k + part_v).astype(jnp.bfloat16), "tensor", scatter_dimension=0, tiled=True
    ).astype(jnp.float32)
    gain1_sum = jnp.sum(d_in * normed1, axis=0)
    bias1_sum = jnp.sum(d_in, axis=0)
    input_grad = d_mixed + norm_back(d_in, normed1, inv1, norm1_gain)
    weights_summed = (
        lax.psum(grad_query.astype(jnp.bfloat16), "dp").astype(jnp.float32),
        lax.psum(grad_key.astype(jnp.bfloat16), "dp").astype(jnp.float32),
        lax.psum(grad_value.astype(jnp.bfloat16), "dp").astype(jnp.float32),
        lax.psum(grad_out.astype(jnp.bfloat16), "dp").astype(jnp.float32),
        lax.psum(grad_gate.astype(jnp.bfloat16), "dp").astype(jnp.float32),
        lax.psum(grad_up.astype(jnp.bfloat16), "dp").astype(jnp.float32),
        lax.psum(grad_down.astype(jnp.bfloat16), "dp").astype(jnp.float32),
    )
    norms_summed = lax.psum((gain1_sum, bias1_sum, gain2_sum, bias2_sum), ("dp", "tensor"))
    return (
        output,
        input_grad,
        norms_summed[0],
        norms_summed[1],
        weights_summed[0],
        weights_summed[1],
        weights_summed[2],
        weights_summed[3],
        norms_summed[2],
        norms_summed[3],
        weights_summed[4],
        weights_summed[5],
        weights_summed[6],
    )


def solution(mesh):
    return jax.shard_map(
        per_device,
        mesh=mesh,
        in_specs=(
            P(("dp", "tensor"), None),
            P(("dp", "tensor"), None),
            P("dp"),
            P(),
            P(),
            P(),
            P(None, "tensor"),
            P(None, "tensor"),
            P(None, "tensor"),
            P("tensor", None),
            P(),
            P(),
            P(None, "tensor"),
            P(None, "tensor"),
            P("tensor", None),
        ),
        out_specs=(
            P(("dp", "tensor"), None),
            P(("dp", "tensor"), None),
            P(),
            P(),
            P(None, "tensor"),
            P(None, "tensor"),
            P(None, "tensor"),
            P("tensor", None),
            P(),
            P(),
            P(None, "tensor"),
            P(None, "tensor"),
            P("tensor", None),
        ),
        check_vma=False,
    )
```

profile of v0, /device:TPU:0, one launch (start us, length us, event | category | flops | bytes accessed | tf_op | source)
XLA Modules:
  0.0 873.7 jit_solution(12473281393600682390)
XLA Ops:
  9.1 13.8 %all-gather.4.cloned.1.call-done = bf16[1024,1024]{1,0:T(8,128)(2,1)} async-done(((bf16[512,1024]{1,0:T(8,128)(2,1)}), bf16[1024,1024]{1,0:T(8,128)(2,1)}) %all-gather.4.cloned.1.call-update) | async-done | bytes 2097168 | tf_op jit(solution)/shard_map/all_gather | solution.py:87
  41.0 25.9 %while.28 = (s32[]{:T(128)}, bf16[2,512,8,64]{1,3,2,0:T(8,128)(2,1)}, f32[2,8,512]{2,1,0:T(8,128)S(1)}, bf16[2,512,8,64]{1,3,2,0:T(8,128)(2,1)}, bf16[1,1024,8,6...) while((s32[]{:T(128)}, bf16[2,512,8,64]{1,3,2,0:T(8,128)(2,1)}, ...), condition=%wide.region_5.6_spmd, body=%wide.region_2.5_spmd.sunk | while | flops 1111748608 | bytes 61997208 | solution.py:130
  41.2 3.5 multiply_reduce_fusion.5
  44.7 3.4 fusion.140
  48.2 4.9 fusion.141
  54.1 3.5 multiply_reduce_fusion.5
  57.6 3.4 fusion.140
  61.1 4.9 fusion.141
  75.2 42.5 %psum.92 = f32[]{:T(128)} all-reduce(f32[]{:T(128)S(6)} %div.87), channel_id=1, replica_groups=mesh['dp'=16,'tensor'=2] {'dp'}, use_global_device_ids=true, to_apply=%region_11.12 | all-reduce | flops 1 | bytes 8 | tf_op jit(solution)/shard_map/psum | solution.py:158
  119.7 5.1 convert_add_fusion
  128.8 6.7 fusion.78
  135.5 6.7 fusion.77
  142.2 16.5 %multiply_convert_fusion.1 = (bf16[1024,2048]{1,0:T(8,128)(2,1)}, bf16[1024,2048]{1,0:T(8,128)(2,1)}, bf16[1024,2048]{1,0:T(8,128)(2,1)}) fusion(f32[1024,2048]{1,0:T(8,128)} %fusion.77, f32[1024,2048]{1,0:T(8,128)} %fusion.78, bf16[1024,1024]{1,0:T(8,128)(2,1)} %all-gather.6.cloned.1.call-done, bf16[2048,1024]{1,0:T(8,128)(2,1)} %param.33), kind=kOutput, calls=%fused_computation.46 | convolution fusion | flops 4326424576 | bytes 35651584 | tf_op jit(solution)/shard_map/dot_general | solution.py:52
  158.7 6.7 fusion.79
  165.5 5.7 add_convert_fusion.1
  171.7 5.1 reduce-scatter.6.cloned.1.call-done
  176.8 3.2 fusion.56
  180.7 3.5 fusion.74
  185.5 9.3 %convolution_convert_fusion.3 = bf16[1024,1024]{1,0:T(8,128)(2,1)} fusion(bf16[1024,2048]{1,0:T(8,128)(2,1)} %get-tuple-element.225, bf16[2048,1024]{1,0:T(8,128)(2,1)} %param.33), kind=kOutput, calls=%fused_computation.108 | convolution fusion | flops 4296015872 | bytes 10485760 | tf_op jit(solution)/shard_map/dot_general | solution.py:149
  201.1 3.3 copy.36
  204.4 119.7 %while.29 = (s32[]{:T(128)}, f32[2,512,8,64]{1,0,3,2:T(2,128)}, f32[2,1024,8,64]{1,3,2,0:T(8,128)}, f32[2,1024,8,64]{1,3,2,0:T(8,128)}, bf16[2,512,8,64]{1,3,2,0...) while((s32[]{:T(128)}, f32[2,512,8,64]{1,0,3,2:T(2,128)}, ...), condition=%wide.region_17.18_spmd, body=%wide.region_15.17_spmd.sunk | while | flops 2735468544 | bytes 174180528 | solution.py:222
  204.6 3.4 fusion.150
  208.0 5.2 bitcast_dynamic-update-slice_fusion.8
  213.2 9.6 %multiply_reduce_fusion.6 = (f32[8,512]{1,0:T(8,128)S(1)}, f32[8,512,1024]{2,1,0:T(8,128)}) fusion(f32[8,512,1024]{2,1,0:T(8,128)S(1)} %fusion.150, f32[8,512]{1,0:T(8,128)S(1)} %dynamic-slice_bitcast_fusion.2, bf16[1,1024,8,64]{1,3,2,0:T(8,128)(2,1)} %get-tuple-element.399, bf16[2,512,8,64]{1,3,2,0:T(8,128)(2,1)} %get-tuple-element.398, s32[]{:T(128)S(6)} %copy.80), kind=kOutput, calls=%fused_computation.17.clone.1 | convolution fusion | flops 553644032 | bytes 35160068 | tf_op jit(solution)/shard_map/while/body/eval_jaxpr/qhd,khd->hqk/dot_general | solution.py:202
  222.8 10.5 %multiply_convert_fusion.6 = bf16[8,512,1024]{2,1,0:T(8,128)(2,1)} fusion(f32[8,512,1024]{2,1,0:T(8,128)} %get-tuple-element.346, f32[8,512,1024]{2,1,0:T(8,128)S(1)} %fusion.150, f32[8,512]{1,0:T(8,128)S(1)} %get-tuple-element.347, f32[8,512]{1,0:T(8,128)S(1)} %dynamic-slice_bitcast_fusion.2), kind=kLoop, calls=%fused_computation.16.clone.1 | loop fusion | flops 20971520 | bytes 41975808 | tf_op jit(solution)/shard_map/while/body/eval_jaxpr/convert_element_type | solution.py:205
  233.3 6.2 fusion.151
  239.5 3.9 bitcast_dynamic-update-slice_fusion.7
  244.5 19.6 %dynamic_update_slice.37 = f32[2,512,8,64]{1,0,3,2:T(2,128)} dynamic-update-slice(f32[2,512,8,64]{1,0,3,2:T(2,128)} %get-tuple-element.381, f32[1,512,8,64]{1,0,3,2:T(1,128)S(1)} %copy.60, s32[]{:T(128)S(6)} %copy.80, s32[]{:T(128)} %constant.115.clone.1..sunk, s32[]{:T(128)} %constant.115.clone.1..sunk, s32[]{:T(128)} %constant.115.clone.1..sunk) | dynamic-update-slice | bytes 2097156 | tf_op jit(solution)/shard_map/while/body/jit(dynamic_update_index_in_dim)/dynamic_update_slice | solution.py:222
  264.1 3.4 fusion.150
  267.5 5.2 bitcast_dynamic-update-slice_fusion.8
  272.8 9.6 %multiply_reduce_fusion.6 = (f32[8,512]{1,0:T(8,128)S(1)}, f32[8,512,1024]{2,1,0:T(8,128)}) fusion(f32[8,512,1024]{2,1,0:T(8,128)S(1)} %fusion.150, f32[8,512]{1,0:T(8,128)S(1)} %dynamic-slice_bitcast_fusion.2, bf16[1,1024,8,64]{1,3,2,0:T(8,128)(2,1)} %get-tuple-element.399, bf16[2,512,8,64]{1,3,2,0:T(8,128)(2,1)} %get-tuple-element.398, s32[]{:T(128)S(6)} %copy.80), kind=kOutput, calls=%fused_computation.17.clone.1 | convolution fusion | flops 553644032 | bytes 35160068 | tf_op jit(solution)/shard_map/while/body/eval_jaxpr/qhd,khd->hqk/dot_general | solution.py:202
  282.4 10.5 %multiply_convert_fusion.6 = bf16[8,512,1024]{2,1,0:T(8,128)(2,1)} fusion(f32[8,512,1024]{2,1,0:T(8,128)} %get-tuple-element.346, f32[8,512,1024]{2,1,0:T(8,128)S(1)} %fusion.150, f32[8,512]{1,0:T(8,128)S(1)} %get-tuple-element.347, f32[8,512]{1,0:T(8,128)S(1)} %dynamic-slice_bitcast_fusion.2), kind=kLoop, calls=%fused_computation.16.clone.1 | loop fusion | flops 20971520 | bytes 41975808 | tf_op jit(solution)/shard_map/while/body/eval_jaxpr/convert_element_type | solution.py:205
  292.9 6.2 fusion.151
  299.1 3.9 bitcast_dynamic-update-slice_fusion.7
  304.1 19.6 %dynamic_update_slice.37 = f32[2,512,8,64]{1,0,3,2:T(2,128)} dynamic-update-slice(f32[2,512,8,64]{1,0,3,2:T(2,128)} %get-tuple-element.381, f32[1,512,8,64]{1,0,3,2:T(1,128)S(1)} %copy.60, s32[]{:T(128)S(6)} %copy.80, s32[]{:T(128)} %constant.115.clone.1..sunk, s32[]{:T(128)} %constant.115.clone.1..sunk, s32[]{:T(128)} %constant.115.clone.1..sunk) | dynamic-update-slice | bytes 2097156 | tf_op jit(solution)/shard_map/while/body/jit(dynamic_update_index_in_dim)/dynamic_update_slice | solution.py:222
  329.7 4.1 reshape.327
  345.5 8.5 convolution_convert_fusion.1
  354.0 6.2 convolution_convert_fusion.2
  360.2 6.4 convolution_convert_fusion
  376.6 3.4 add_convert_fusion.4
  382.7 44.2 %all-reduce = (f32[1024]{0:T(1024)}, f32[1024]{0:T(1024)}, f32[1024]{0:T(1024)}, f32[1024]{0:T(1024)}) all-reduce(f32[1024]{0:T(1024)S(1)} %get-tuple-element.170, f32[1024]{0:T(1024)S(1)} %get-tuple-element.175, f32[1024]{0:T(1024)S(1)} %copy-done.46, f32[1024]{0:T(1024)S(1)} %copy-done.47), channel_id=1, replica_groups=mesh['dp'=16,'tensor'=2] {'dp','tensor'}, use_global_device_ids=true, to_apply=%region_24.25 | all-reduce | flops 4096 | bytes 32768 | tf_op jit(solution)/shard_map/psum | solution.py:252
  426.9 4.1 fusion.50
  431.0 413.1 %all-reduce.7.cloned.1.call-done = (bf16[1024,512]{1,0:T(8,128)(2,1)}, bf16[1024,512]{1,0:T(8,128)(2,1)}, bf16[1024,512]{1,0:T(8,128)(2,1)}, bf16[512,1024]{1,0:...) async-done(((bf16[1024,512]{1,0:T(8,128)(2,1)}, bf16[1024,512]{1,0:T(8,128)(2,1)}, bf16[1024,512]{1,0:T(8,128)(2,1)}, ...) | async-done | bytes 16777232 | tf_op jit(solution)/shard_map/psum | solution.py:244
  844.1 3.0 convert_element_type.177
  847.1 3.0 convert_element_type.179
  853.3 4.4 convert_element_type.185
  857.7 4.4 convert_element_type.187
  862.2 4.4 convert_element_type.189
  (226 shorter events, 77.7 us)
Async XLA Ops:
  7.2 63.3 %copy-start = (bf16[512,1024]{1,0:T(8,128)(2,1)S(1)}, bf16[512,1024]{1,0:T(8,128)(2,1)}, u32[]{:S(2)}) copy-start(bf16[512,1024]{1,0:T(8,128)(2,1)} %param.28) | copy-start | bytes 3145732
  7.2 20.1 %copy-start.34 = (f32[1024]{0:T(1024)S(1)}, f32[1024]{0:T(1024)}, u32[]{:S(2)}) copy-start(f32[1024]{0:T(1024)} %param.23) | copy-start | bytes 12292
  7.2 20.1 %copy-start.49 = (f32[1024]{0:T(1024)S(1)}, f32[1024]{0:T(1024)}, u32[]{:S(2)}) copy-start(f32[1024]{0:T(1024)} %param.24) | copy-start | bytes 12292
  7.2 15.7 %all-gather.4.cloned.1.call-start = ((), (), s32[]{:S(2)}) async-start(), calls=%async_computation.3 | async-start | bytes 3145728 | tf_op jit(solution)/shard_map/all_gather | solution.py:87
  8.0 111.7 %all-reduce.5.cloned.1.call-start = ((), (), s32[]{:S(2)}) async-start(), calls=%async_computation.4 | async-start | bytes 4194304 | tf_op jit(solution)/shard_map/psum | solution.py:132
  8.0 14.9 %copy-start.51 = (f32[32]{0:T(128)}, f32[32]{0:T(128)S(1)}, u32[]{:S(2)}) copy-start(f32[32]{0:T(128)S(1)} %negate_power_fusion) | copy-start | bytes 388
  9.1 26.7 %copy-start.13 = (f32[1024,64]{0,1:T(8,128)}, f32[1024,64]{0,1:T(8,128)S(1)}, u32[]{:S(2)}) copy-start(f32[1024,64]{0,1:T(8,128)S(1)} %get-tuple-element.244) | copy-start | bytes 786436
  22.9 4.4 copy-start.3
  70.5 47.8 %copy-start.6 = (bf16[512,1024]{1,0:T(8,128)(2,1)S(1)}, bf16[512,1024]{1,0:T(8,128)(2,1)}, u32[]{:S(2)}) copy-start(bf16[512,1024]{1,0:T(8,128)(2,1)} %param.20) | copy-start | bytes 3145732
  73.1 69.1 %all-gather.6.cloned.1.call-start = ((), (), s32[]{:S(2)}) async-start(), calls=%async_computation.6 | async-start | bytes 3145728 | tf_op jit(solution)/shard_map/all_gather | solution.py:170
  118.4 61.7 %copy-start.36 = (f32[512]{0:T(512)}, f32[512]{0:T(512)S(1)}, u32[]{:S(2)}) copy-start(f32[512]{0:T(512)S(1)} %fusion.72) | copy-start | bytes 6148
  119.6 57.2 %reduce-scatter.6.cloned.1.call-start = ((), (), s32[]{:S(2)}) async-start(), calls=%async_computation.7 | async-start | bytes 3145728 | tf_op jit(solution)/shard_map/reduce_scatter | solution.py:179
  119.7 5.2 copy-start.4
  119.7 5.2 copy-start.5
  128.7 6.8 copy-start.15
  128.8 6.7 copy-start.53
  142.2 16.5 %copy-start.54 = (bf16[1024,2048]{1,0:T(8,128)(2,1)S(1)}, bf16[1024,2048]{1,0:T(8,128)(2,1)}, u32[]{:S(2)}) copy-start(bf16[1024,2048]{1,0:T(8,128)(2,1)} %param.31) | copy-start | bytes 12582916
  158.7 6.7 copy-start.56
  158.7 6.7 copy-start.64
  171.2 24.9 %all-gather.8.cloned.1.call-start = ((), (), s32[]{:S(2)}) async-start(), calls=%async_computation.8 | async-start | bytes 3145728 | tf_op jit(solution)/shard_map/all_gather | solution.py:188
  171.7 12.5 %copy-start.40 = (f32[512]{0:T(512)}, f32[512]{0:T(512)S(1)}, u32[]{:S(2)}) copy-start(f32[512]{0:T(512)S(1)} %dynamic-slice.6) | copy-start | bytes 6148
  176.8 7.5 copy-start.52
  180.1 14.7 %copy-start.42 = (f32[512]{0:T(512)}, f32[512]{0:T(512)S(1)}, u32[]{:S(2)}) copy-start(f32[512]{0:T(512)S(1)} %broadcast_multiply_fusion.6) | copy-start | bytes 6148
  184.2 192.4 %reduce-scatter.4.cloned.1.call-start = ((), (), s32[]{:S(2)}) async-start(), calls=%async_computation.5 | async-start | bytes 3145728 | tf_op jit(solution)/shard_map/reduce_scatter | solution.py:148
  194.8 185.2 %reduce-scatter.8.cloned.1.call-start = ((), (), s32[]{:S(2)}) async-start(), calls=%async_computation.9 | async-start | bytes 3145728 | tf_op jit(solution)/shard_map/reduce_scatter | solution.py:237
  233.3 6.2 copy-start.2
  292.9 6.2 copy-start.2
  329.7 6.3 copy-start.23
  345.5 498.7 %all-reduce.7.cloned.1.call-start = ((), (), s32[]{:S(2)}) async-start(), calls=%async_computation.10 | async-start | bytes 33554432 | tf_op jit(solution)/shard_map/psum | solution.py:244
  345.5 8.5 copy-start.63
  354.0 6.2 copy-start.57
  354.0 6.2 copy-start.65
  360.2 6.4 copy-start.18
  376.5 6.2 copy-start.46
  376.5 6.2 copy-start.47
  376.5 50.4 %copy-start.7 = (bf16[512,1024]{1,0:T(8,128)(2,1)S(1)}, bf16[512,1024]{1,0:T(8,128)(2,1)}, u32[]{:S(2)}) copy-start(bf16[512,1024]{1,0:T(8,128)(2,1)} %param.20) | copy-start | bytes 3145732
  376.5 50.4 %copy-start.8 = (bf16[512,1024]{1,0:T(8,128)(2,1)S(1)}, bf16[512,1024]{1,0:T(8,128)(2,1)}, u32[]{:S(2)}) copy-start(bf16[512,1024]{1,0:T(8,128)(2,1)} %reduce-scatter.6.cloned.1.call-done) | copy-start | bytes 3145732
  376.5 50.4 %copy-start.33 = (f32[1024]{0:T(1024)S(1)}, f32[1024]{0:T(1024)}, u32[]{:S(2)}) copy-start(f32[1024]{0:T(1024)} %param.29) | copy-start | bytes 12292
  376.5 50.4 %copy-start.37 = (f32[512]{0:T(512)S(1)}, f32[512]{0:T(512)}, u32[]{:S(2)}) copy-start(f32[512]{0:T(512)} %copy-done.36) | copy-start | bytes 6148
  376.5 50.4 %copy-start.41 = (f32[512]{0:T(512)S(1)}, f32[512]{0:T(512)}, u32[]{:S(2)}) copy-start(f32[512]{0:T(512)} %copy-done.40) | copy-start | bytes 6148
  376.5 50.4 %copy-start.43 = (f32[512]{0:T(512)S(1)}, f32[512]{0:T(512)}, u32[]{:S(2)}) copy-start(f32[512]{0:T(512)} %copy-done.42) | copy-start | bytes 6148
  376.5 50.4 %copy-start.45 = (f32[512]{0:T(512)S(1)}, f32[512]{0:T(512)}, u32[]{:S(2)}) copy-start(f32[512]{0:T(512)} %copy-done.44) | copy-start | bytes 6148
  844.1 6.0 copy-start.22
  844.1 7.6 copy-start.21
  847.1 6.2 copy-start.12
  853.3 4.5 copy-start.11
  857.7 4.5 copy-start.10
  862.2 4.4 copy-start.1
  (29 other events, 58.3 us)
Sparse Core Ops, SparseCore 0:
  9.6 13.2 all-gather.3
  73.3 22.3 all-reduce.4
  119.7 6.4 all-gather.5
  171.3 5.4 reduce-scatter.5
  184.4 11.7 all-gather.7
  198.8 10.7 reduce-scatter.3
  345.6 10.7 reduce-scatter.7
  375.9 468.1 all-reduce.6
where the time goes:
time: 884 us; the launch traced here: 874 us
  waiting for transfers between devices  434 us (49%)
  matrix products  171 us (19%)
  other arithmetic  98.9 us (11%)
  blocking collectives  86.6 us (10%)
  local copies, waits for them, and re-layouts  64.4 us (7%)
  between operations  17.1 us (2%)
    psum x1, waiting for transfers between devices, per_device(): lax.psum(grad_query.astype(jnp.bfloat16), 'dp').astype(jnp.float32)  413 us
    psum x1, blocking collectives, per_device(): lax.psum((gain1_sum, bias1_sum, gain2_sum, bias2_sum), ('dp', 'tensor'))  44.2 us
    psum x1, blocking collectives, per_device(): inv_total = lax.psum(jnp.sum(inverse), 'dp')  42.5 us
    dynamic_update_slice x4, local copies, waits for them, and re-layouts, per_device(): lax.map(attend_back, (q_blocks, log_totals, d_blocks, block_window))  41.4 us
    dot_general x7, matrix products, times_transposed(): lax.dot_general(left_mat, right_mat, (((1,), (1,)), ((), ())), preferred_...  37.1 us
    dot_general x7, matrix products, inner_rows(): lax.dot_general(left_mat, right_mat, (((0,), (0,)), ((), ())), preferred_...  30.2 us
    convert_element_type x2, other arithmetic, attend_back(): d_scores = (prob_full * (d_prob - jnp.sum(prob_full * d_prob, axis=-1, ke...  20.9 us
    dot_general x2, matrix products, attend_back(): jnp.einsum('qhd,khd->hqk', d_block, v_win, preferred_element_type=jnp.flo...  19.3 us
  transfers between devices with their start and end apart: 8, of which 4 were waited for; matrix products, arithmetic and copies ran while one was open for 26% of the time, Pallas kernels for 0%

commit v1 on v0

v1 whole, which is shorter than its diff:
```python
import functools
import math

import jax
import jax.numpy as jnp
from jax import lax
from jax.experimental import pallas as pl
from jax.experimental.pallas import tpu as pltpu
from jax.sharding import PartitionSpec as P

HD = 64
LEN = 1024
SPECIES = 850
LANES = 128

eps_norm = 1e-05
BF = jnp.bfloat16
F32 = jnp.float32
EXP_SCALE = HD ** (-0.5) * math.log2(math.e)
MIB = 1024 * 1024


def shape_of(dims, dtype):
    return jax.ShapeDtypeStruct(dims, dtype)


def dot_nn(left, right):
    return lax.dot_general(left, right, (((1,), (0,)), ((), ())), preferred_element_type=F32)


def dot_nt(left, right):
    return lax.dot_general(left, right, (((1,), (1,)), ((), ())), preferred_element_type=F32)


def dot_tn(left, right):
    return lax.dot_general(left, right, (((0,), (0,)), ((), ())), preferred_element_type=F32)


def row_norm(values):
    center = values - jnp.mean(values, axis=-1, keepdims=True)
    inv_std = lax.rsqrt(jnp.mean(center * center, axis=-1, keepdims=True) + eps_norm)
    return (center * inv_std, inv_std)


def norm_back(upstream, normed, inv_std, gain_vec):
    scaled_up = upstream * gain_vec
    mean_one = jnp.mean(scaled_up, axis=-1, keepdims=True)
    mean_two = jnp.mean(scaled_up * normed, axis=-1, keepdims=True)
    return inv_std * (scaled_up - mean_one - normed * mean_two)


def params(mib):
    return pltpu.CompilerParams(vmem_limit_bytes=mib * MIB)


def swap_halves(values):
    width = values.shape[1]
    lane = lax.broadcasted_iota(jnp.int32, values.shape, 1) % HD
    ahead = pltpu.roll(values, width - HD // 2, 1)
    behind = pltpu.roll(values, HD // 2, 1)
    return jnp.where(lane < HD // 2, ahead, behind)


def rope_tables(start):
    half_dim = HD // 2
    inv_freq = 1.0 / 10000.0 ** (jnp.arange(half_dim, dtype=F32) * 2.0 / HD)
    position = (start + jnp.arange(LEN, dtype=jnp.int32)) % LEN
    angles = position.astype(F32)[:, None] * inv_freq[None, :]
    cos_tab, sin_tab = jnp.cos(angles), jnp.sin(angles)
    return (
        jnp.concatenate([cos_tab] * 4, axis=1),
        jnp.concatenate([-sin_tab, sin_tab] * 2, axis=1),
    )


def project_kernel(own_ref, rest_ref, cos_ref, sin_ref, wq_ref, wk_ref, wv_ref, q_ref, k_ref, v_ref):
    own = own_ref.shape[0]
    for rows, x_ref in ((slice(0, own), own_ref), (slice(own, LEN), rest_ref)):
        x = x_ref[...]
        cos_tab, sin_tab = cos_ref[rows, :], sin_ref[rows, :]
        for w_ref, out_ref in ((wq_ref, q_ref), (wk_ref, k_ref)):
            lin = dot_nn(x, w_ref[...])
            for at in range(0, lin.shape[1], LANES):
                part = lin[:, at : at + LANES]
                turned = part * cos_tab + swap_halves(part) * sin_tab
                out_ref[rows, at : at + LANES] = turned.astype(BF)
        v_ref[rows, :] = dot_nn(x, wv_ref[...]).astype(BF)


def project(own, rest, cos_tab, sin_tab, w_query, w_key, w_value):
    cols = w_query.shape[1]
    block = min(256, cols)
    width = own.shape[1]
    whole = lambda a: pl.BlockSpec(a.shape, lambda i: (0, 0))
    w_spec = pl.BlockSpec((width, block), lambda i: (0, i))
    o_spec = pl.BlockSpec((LEN, block), lambda i: (0, i))
    return pl.pallas_call(
        project_kernel,
        grid=(cols // block,),
        in_specs=[whole(own), whole(rest), whole(cos_tab), whole(sin_tab), w_spec, w_spec, w_spec],
        out_specs=[o_spec] * 3,
        out_shape=[shape_of((LEN, cols), BF)] * 3,
        compiler_params=params(48),
        name="project",
    )(own, rest, cos_tab, sin_tab, w_query, w_key, w_value)


def head_only(values, head):
    lane = lax.broadcasted_iota(jnp.int32, values.shape, 1)
    return jnp.where(lane // HD == head, values, jnp.zeros_like(values))


def attend_kernel(q_ref, k_ref, v_ref, ctx_ref, lse_ref):
    k = k_ref[...]
    v_turned = v_ref[...].T
    parts = []
    for head in range(2):
        scores = dot_nt(k, head_only(q_ref[...], head))
        top = jnp.max(scores, axis=0, keepdims=True)
        exps = jnp.exp2((scores - top) * EXP_SCALE)
        total = jnp.sum(exps, axis=0, keepdims=True)
        mix = dot_nn(v_turned[head * HD : (head + 1) * HD, :], exps.astype(BF))
        parts.append(mix * (1.0 / total))
        lse_ref[0, head : head + 1, :] = top * EXP_SCALE + jnp.log2(total)
    ctx_ref[...] = jnp.concatenate(parts, axis=0).T.astype(BF)


def attend(query, key, value, first, count, tile):
    cols = query.shape[1]
    pairs = cols // LANES
    whole = pl.BlockSpec((LEN, LANES), lambda p, i: (0, p))
    return pl.pallas_call(
        attend_kernel,
        grid=(pairs, count // tile),
        in_specs=[pl.BlockSpec((tile, LANES), lambda p, i: (first // tile + i, p)), whole, whole],
        out_specs=[
            pl.BlockSpec((tile, LANES), lambda p, i: (i, p)),
            pl.BlockSpec((1, 2, tile), lambda p, i: (p, 0, i)),
        ],
        out_shape=[shape_of((count, cols), BF), shape_of((pairs, 2, count), F32)],
        compiler_params=params(48),
        name="attend",
    )(query, key, value)


def attend_back_kernel(
    tile, q_ref, k_ref, v_ref, d_ref, ctx_ref, lse_ref, cos_ref, sin_ref,
    dq_ref, dk_ref, dv_ref, dk_sum, dv_sum,
):
    scale = HD ** (-0.5)
    k, v = k_ref[...], v_ref[...]
    k_turned = k.T

    def unrotate(grads, rows):
        grads = grads * scale
        return (grads * cos_ref[rows, :] - swap_halves(grads) * sin_ref[rows, :]).astype(BF)

    dk_sum[...] = jnp.zeros_like(dk_sum)
    dv_sum[...] = jnp.zeros_like(dv_sum)

    def step(i, carry):
        at = pl.multiple_of(i * tile, tile)
        rows = pl.ds(at, tile)
        q, d = q_ref[rows, :], d_ref[rows, :]
        both = (d.astype(F32) * ctx_ref[rows, :].astype(F32)).T
        parts = []
        for head in range(2):
            q_head, d_head = head_only(q, head), head_only(d, head)
            delta = jnp.sum(both[head * HD : (head + 1) * HD, :], axis=0, keepdims=True)
            scores = dot_nt(k, q_head)
            probs = jnp.exp2(scores * EXP_SCALE - lse_ref[0, head : head + 1, rows])
            d_probs = dot_nt(v, d_head)
            d_scores = (probs * (d_probs - delta)).astype(BF)
            dv_sum[...] += dot_nn(probs.astype(BF), d_head)
            dk_sum[...] += dot_nn(d_scores, q_head)
            parts.append(dot_nn(k_turned[head * HD : (head + 1) * HD, :], d_scores))
        dq_ref[rows, :] = unrotate(jnp.concatenate(parts, axis=0).T, rows)
        return carry

    lax.fori_loop(0, LEN // tile, step, 0)
    everything = slice(0, LEN)
    dk_ref[...] = unrotate(dk_sum[...], everything)
    dv_ref[...] = dv_sum[...].astype(BF)


def attend_back(query, key, value, d_context, context, lse, cos_tab, sin_tab, tile=256):
    cols = query.shape[1]
    pairs = cols // LANES
    strip = pl.BlockSpec((LEN, LANES), lambda p: (0, p))
    table = pl.BlockSpec((LEN, LANES), lambda p: (0, 0))
    return pl.pallas_call(
        functools.partial(attend_back_kernel, tile),
        grid=(pairs,),
        in_specs=[strip] * 5 + [pl.BlockSpec((1, 2, LEN), lambda p: (p, 0, 0)), table, table],
        out_specs=[strip] * 3,
        out_shape=[shape_of((LEN, cols), BF)] * 3,
        scratch_shapes=[pltpu.VMEM((LEN, LANES), F32)] * 2,
        compiler_params=params(48),
        name="attend_back",
    )(query, key, value, d_context, context, lse, cos_tab, sin_tab)


def ff_kernel(
    n_pieces, slots_ref, nm_ref, nt_ref, sg_ref, wg_ref, wu_ref, wd_ref, *refs,
):
    hid_ref, dg_ref, du_ref, gd_ref, gg_ref, gu_ref, ht_ref = refs[-7:]
    width, block = wg_ref.shape
    tile = 256

    def forward(i, carry):
        rows = pl.ds(pl.multiple_of(i * tile, tile), tile)
        x = nm_ref[rows, :]
        gate = dot_nn(x, wg_ref[...])
        up = dot_nn(x, wu_ref[...])
        d_hidden = dot_nt(sg_ref[rows, :], wd_ref[...])
        sig = 1.0 / (1.0 + jnp.exp(-gate))
        silu = gate * sig
        hidden = (silu * up).astype(BF)
        hid_ref[rows, :] = hidden
        ht_ref[:, rows] = hidden.T
        dg_ref[rows, :] = (d_hidden * up * (sig * (1.0 + gate * (1.0 - sig)))).astype(BF)
        du_ref[rows, :] = (d_hidden * silu).astype(BF)
        return carry

    lax.fori_loop(0, LEN // tile, forward, 0)

    def weight_grad(which, left_ref, right_ref, out_ref):
        piece = out_ref.shape[0] // n_pieces
        step = max(tile, piece)
        per = step // piece

        def body(i, carry):
            rows = pl.ds(pl.multiple_of(i * step, step), step)
            grads = dot_nn(left_ref[rows, :], right_ref[...]).astype(BF)
            for j in range(per):
                at = pl.multiple_of(slots_ref[which, i * per + j] * piece, piece)
                out_ref[pl.ds(at, piece), :] = grads[j * piece : (j + 1) * piece, :]
            return carry

        lax.fori_loop(0, out_ref.shape[0] // step, body, 0)

    weight_grad(0, ht_ref, sg_ref, gd_ref)
    weight_grad(1, nt_ref, dg_ref, gg_ref)
    weight_grad(2, nt_ref, du_ref, gu_ref)


def feed_forward(index, block, n_pieces, slots, nm, nt, sg, w_gate, w_up, w_down, kept):
    width, units = w_gate.shape
    whole = pl.BlockSpec((LEN, width), lambda i, s: (0, 0))
    cols = pl.BlockSpec((width, block), lambda i, s: (0, index))
    kept_spec = pl.BlockSpec((LEN, block), lambda i, s: (0, index))
    grad = lambda dims: pl.BlockSpec(dims, lambda i, s: (0, 0))
    previous = list(kept) if kept is not None else []
    return pl.pallas_call(
        functools.partial(ff_kernel, n_pieces),
        grid_spec=pltpu.PrefetchScalarGridSpec(
            num_scalar_prefetch=1,
            grid=(1,),
            in_specs=[whole, pl.BlockSpec((width, LEN), lambda i, s: (0, 0)), whole, cols, cols,
                      pl.BlockSpec((block, width), lambda i, s: (index, 0))]
            + [pl.BlockSpec(memory_space=pl.ANY)] * len(previous),
            out_specs=[kept_spec] * 3 + [grad((block, width)), grad((width, block)), grad((width, block))],
            scratch_shapes=[pltpu.VMEM((block, LEN), BF)],
        ),
        out_shape=[shape_of((LEN, units), BF)] * 3
        + [shape_of((block, width), BF)] + [shape_of((width, block), BF)] * 2,
        input_output_aliases={7 + i: i for i in range(len(previous))},
        compiler_params=params(56),
        name="feed_forward",
    )(slots, nm, nt, sg, w_gate, w_up, w_down, *previous)


def orders_of(n_dp):
    bits = [1 << i for i in range(n_dp.bit_length() - 1)]
    if len(bits) < 4:
        return [bits] * 3
    a, b, c = bits[:3]
    return [[a, b, c] + bits[3:], [b, a, c] + bits[3:], [c, a, b] + bits[3:]]


def masks_of(order):
    size = 1 << len(order)
    masks = []
    for slot in range(size):
        mask = 0
        for level, bit in enumerate(order):
            if slot >> (len(order) - 1 - level) & 1:
                mask |= bit
        masks.append(mask)
    return masks


def slots_of(order, me):
    masks = masks_of(order)
    inverse = [0] * len(masks)
    for slot, mask in enumerate(masks):
        inverse[mask] = slot
    table = jnp.array(inverse, jnp.int32)
    return table[jnp.arange(len(masks), dtype=jnp.int32) ^ me]


def swap_dp(values, bit, n_dp):
    return lax.ppermute(values, "dp", [(i, i ^ bit) for i in range(n_dp)])


def sum_over_dp(values, order, n_dp):
    for bit in order:
        half = values.shape[0] // 2
        values = values[:half] + swap_dp(values[half:], bit, n_dp)
    for bit in order[::-1]:
        values = jnp.concatenate([values, swap_dp(values, bit, n_dp)], axis=0)
    return values


def place_kernel(pieces_ref, in_ref, *refs):
    refs[-1][...] = in_ref[...].astype(F32)


def place(summed, pieces, full_shape, block_index, base):
    n_pieces = pieces.shape[0]
    rows, cols = summed.shape
    piece = rows // n_pieces
    row_block, col_block = block_index
    given = [] if base is None else [base]
    return pl.pallas_call(
        place_kernel,
        grid_spec=pltpu.PrefetchScalarGridSpec(
            num_scalar_prefetch=1,
            grid=(n_pieces,),
            in_specs=[pl.BlockSpec((piece, cols), lambda i, s: (i, 0))]
            + [pl.BlockSpec(memory_space=pl.ANY)] * len(given),
            out_specs=pl.BlockSpec((piece, cols), lambda i, s: (row_block * n_pieces + s[i], col_block)),
        ),
        out_shape=shape_of(full_shape, F32),
        input_output_aliases={2: 0} if given else {},
        compiler_params=params(32),
        name="place",
    )(pieces, summed, *given)


def per_device(
    tokens,
    cotangent,
    species_ids,
    species_counts,
    norm1_gain,
    norm1_bias,
    w_query,
    w_key,
    w_value,
    w_out,
    norm2_gain,
    norm2_bias,
    w_gate,
    w_up,
    w_down,
):
    own, width = tokens.shape
    group = lax.axis_size("tensor")
    member = lax.axis_index("tensor")
    n_dp = lax.axis_size("dp")
    me = lax.axis_index("dp")
    rest = LEN - own
    units = w_gate.shape[1]
    block = min(512, units)
    hypercube = n_dp & (n_dp - 1) == 0

    def from_member(values, step):
        return lax.ppermute(values, "tensor", [((i + step) % group, i) for i in range(group)])

    def rest_rows(values):
        parts = [from_member(values, step) for step in range(1, group)]
        return parts[0] if group == 2 else jnp.concatenate(parts, axis=0)

    def to_owner(first, others):
        total = first
        for step in range(1, group):
            piece = others[(step - 1) * own : step * own].astype(BF)
            perm = [(i, (i + step) % group) for i in range(group)]
            total = total + lax.ppermute(piece, "tensor", perm).astype(F32)
        return total

    def rows_to_owner(partial):
        return to_owner(partial[:own], partial[own:])

    picked = species_ids[:, None] == jnp.arange(SPECIES, dtype=jnp.int32)[None, :]
    count = jnp.sum(jnp.where(picked, species_counts[None, :], 0), axis=1)
    inverse = jnp.broadcast_to(1.0 / count.astype(F32)[0], (1, LANES))
    inverse_sum = inverse
    if hypercube:
        for level in range(n_dp.bit_length() - 1):
            inverse_sum = inverse_sum + swap_dp(inverse_sum, 1 << level, n_dp)
    else:
        inverse_sum = lax.psum(inverse_sum, "dp")
    weight = (n_dp * inverse / inverse_sum)[:, :1]

    tok_own = tokens.astype(F32)
    normed1, inv1 = row_norm(tok_own)
    in_own = (normed1 * norm1_gain + norm1_bias).astype(BF)
    in_rest = rest_rows(in_own)
    cot_rest = rest_rows(cotangent)
    cos_tab, sin_tab = rope_tables(member * own)

    query, key, value = project(in_own, in_rest, cos_tab, sin_tab, w_query, w_key, w_value)
    ctx_rest, lse_rest = attend(query, key, value, own, rest, own)
    branch_rest = dot_nn(ctx_rest, w_out).astype(BF)
    ctx_own, lse_own = attend(query, key, value, 0, own, own)
    mixed = tok_own + to_owner(dot_nn(ctx_own, w_out), branch_rest)
    normed2, inv2 = row_norm(mixed)
    mid_own = (normed2 * norm2_gain + norm2_bias).astype(BF)
    mid_rest = rest_rows(mid_own)
    mid = jnp.concatenate([mid_own, mid_rest], axis=0)
    mid_turned = mid.T
    sg_own = (cotangent.astype(F32) * weight).astype(BF)
    sg = jnp.concatenate([sg_own, (cot_rest.astype(F32) * weight).astype(BF)], axis=0)

    orders = orders_of(n_dp) if hypercube else None
    masks = [jnp.array(masks_of(o), jnp.int32) ^ me for o in orders]
    slots = jnp.stack([slots_of(o, me) for o in orders])

    grads = []
    kept = None
    for index in range(units // block):
        *kept, g_down, g_gate, g_up = feed_forward(
            index, block, n_dp, slots, mid, mid_turned, sg, w_gate, w_up, w_down, kept
        )
        grads.append((g_down, g_gate, g_up))
    hidden, d_gate, d_up = kept

    summed = [[sum_over_dp(g, o, n_dp) for g, o in zip(trio, orders)] for trio in grads]

    d_mid = rows_to_owner(dot_nt(d_gate, w_gate) + dot_nt(d_up, w_up))
    gain2_sum = jnp.sum(d_mid * normed2, axis=0)
    bias2_sum = jnp.sum(d_mid, axis=0)
    d_mixed = sg_own.astype(F32) + norm_back(d_mid, normed2, inv2, norm2_gain)
    d_branch_own = d_mixed.astype(BF)
    d_branch = jnp.concatenate([d_branch_own, rest_rows(d_branch_own)], axis=0)
    context = jnp.concatenate([ctx_own, ctx_rest], axis=0)
    lse = jnp.concatenate([lse_own, lse_rest], axis=2)
    d_context = dot_nt(d_branch, w_out).astype(BF)
    d_query, d_key, d_value = attend_back(
        query, key, value, d_context, context, lse, cos_tab, sin_tab
    )
    normed_in = jnp.concatenate([in_own, in_rest], axis=0)
    grad_out = dot_tn(context, d_branch).astype(BF)
    late = [dot_tn(normed_in, d).astype(BF) for d in (d_query, d_key, d_value)]

    output = (mixed + rows_to_owner(dot_nn(hidden, w_down))).astype(BF)
    d_in = rows_to_owner(dot_nt(d_query, w_query) + dot_nt(d_key, w_key) + dot_nt(d_value, w_value))
    gain1_sum = jnp.sum(d_in * normed1, axis=0)
    bias1_sum = jnp.sum(d_in, axis=0)
    input_grad = d_mixed + norm_back(d_in, normed1, inv1, norm1_gain)

    vectors = jnp.stack([gain1_sum, bias1_sum, gain2_sum, bias2_sum])
    if hypercube:
        for level in range(n_dp.bit_length() - 1):
            vectors = vectors + swap_dp(vectors, 1 << level, n_dp)
        total = vectors
        for step in range(1, group):
            total = total + from_member(vectors, step)
        vectors = total
    else:
        vectors = lax.psum(vectors, ("dp", "tensor"))

    def small_sum(values, order_at):
        piece = values.shape[0] // n_dp
        if piece < 16:
            return lax.psum(values, "dp").astype(F32)
        order = orders[order_at]
        pieces = values.reshape(n_dp, piece, values.shape[1])
        rel = jnp.take(pieces, masks[order_at], axis=0).reshape(values.shape)
        return place(sum_over_dp(rel, order, n_dp), masks[order_at], values.shape, (0, 0), None)

    g_out = small_sum(grad_out, 2)
    g_query, g_key, g_value = (small_sum(g, at) for at, g in enumerate(late))
    g_down = g_gate = g_up = None
    for index, (s_down, s_gate, s_up) in enumerate(summed):
        g_down = place(s_down, masks[0], w_down.shape, (index, 0), g_down)
        g_gate = place(s_gate, masks[1], w_gate.shape, (0, index), g_gate)
        g_up = place(s_up, masks[2], w_up.shape, (0, index), g_up)
    return (
        output,
        input_grad,
        vectors[0],
        vectors[1],
        g_query,
        g_key,
        g_value,
        g_out,
        vectors[2],
        vectors[3],
        g_gate,
        g_up,
        g_down,
    )


def solution(mesh):
    split = P(("dp", "tensor"), None)
    cols = P(None, "tensor")
    rows = P("tensor", None)
    return jax.shard_map(
        per_device,
        mesh=mesh,
        in_specs=(split, split, P("dp"), P(), P(), P(), cols, cols, cols, rows, P(), P(), cols, cols, rows),
        out_specs=(split, split, P(), P(), cols, cols, cols, rows, P(), P(), cols, cols, rows),
        check_vma=False,
    )
```

time: 884 us -> 781 us (0.88)
  Pallas kernels: 0 us -> 215 us
  starting transfers between devices: 0.73 us -> 149 us
  waiting for transfers between devices: 434 us -> 298 us
  matrix products: 171 us -> 38.6 us
  blocking collectives: 86.6 us -> 0 us
  other arithmetic: 98.9 us -> 37.9 us
  local copies, waits for them, and re-layouts: 64.4 us -> 33.1 us
  between operations: 17.1 us -> 4.7 us
    psum x2 -> x0, waiting for transfers between devices: 413 us -> none  [the longest x1 413 us: per_device(): lax.psum(grad_query.astype(jnp.bfloat16), 'dp').astype(jnp.float32)]
    ppermute x0 -> x145, waiting for transfers between devices: none -> 298 us  [the longest x136 297 us: swap_dp(): return lax.ppermute(values, 'dp', [(i, i ^ bit) for i in range(n_dp)])]
    pallas_call x0 -> x24, Pallas kernels: none -> 215 us  [the longest x16 94.7 us: place(): pl.pallas_call(place_kernel, grid_spec=pltpu.PrefetchScalarGridSpec(num_s...]
    ppermute x0 -> x145, starting transfers between devices: none -> 149 us  [the longest x136 148 us: swap_dp(): return lax.ppermute(values, 'dp', [(i, i ^ bit) for i in range(n_dp)])]
    dot_general x35 -> x13, matrix products: 171 us -> 38.6 us  [the longest x6 21.2 us: dot_nt(): lax.dot_general(left, right, (((1,), (1,)), ((), ())), preferred_element_...]
    psum x2 -> x0, blocking collectives: 86.6 us -> none  [the longest x1 44.2 us: per_device(): lax.psum((gain1_sum, bias1_sum, gain2_sum, bias2_sum), ('dp', 'tensor'))]
    convert_element_type x15 -> x6, other arithmetic: 57.9 us -> 7.59 us  [the longest x1 3.4 us: per_device(): d_branch_own = d_mixed.astype(BF)]
    dynamic_update_slice x4 -> x0, local copies, waits for them, and re-layouts: 41.4 us -> none  [per_device(): lax.map(attend_back, (q_blocks, log_totals, d_blocks, block_window))]
  transfers between devices with their start and end apart: 8 -> 145, of which waited for: 4 -> 86; matrix products, arithmetic and copies ran while one was open for 26% -> 9% of each run, Pallas kernels for 0% -> 15%
where the time goes in v1:
time: 781 us; the launch traced here: 776 us
  waiting for transfers between devices  298 us (38%)
  Pallas kernels  215 us (28%)
  starting transfers between devices  149 us (19%)
  matrix products  38.6 us (5%)
  other arithmetic  37.9 us (5%)
  local copies, waits for them, and re-layouts  33.1 us (4%)
    ppermute x136, waiting for transfers between devices, swap_dp(): return lax.ppermute(values, 'dp', [(i, i ^ bit) for i in range(n_dp)])  297 us
    ppermute x136, starting transfers between devices, swap_dp(): return lax.ppermute(values, 'dp', [(i, i ^ bit) for i in range(n_dp)])  148 us
    pallas_call x16, Pallas kernels, place(): pl.pallas_call(place_kernel, grid_spec=pltpu.PrefetchScalarGridSpec(num_s...  94.7 us
    pallas_call x4, Pallas kernels, feed_forward(): pl.pallas_call(functools.partial(ff_kernel, n_pieces), grid_spec=pltpu.Pr...  66 us
    pallas_call x1, Pallas kernels, attend_back(): pl.pallas_call(functools.partial(attend_back_kernel, tile), grid=(pairs,)...  30.4 us
    dot_general x6, matrix products, dot_nt(): lax.dot_general(left, right, (((1,), (1,)), ((), ())), preferred_element_...  21.2 us
    pallas_call x2, Pallas kernels, attend(): pl.pallas_call(attend_kernel, grid=(pairs, count // tile), in_specs=[pl.B...  17.6 us
  transfers between devices with their start and end apart: 145, of which 86 were waited for; matrix products, arithmetic and copies ran while one was open for 9% of the time, Pallas kernels for 15%

profile of v1, /device:TPU:0, one launch (start us, length us, event | category | flops | bytes accessed | tf_op | source)
XLA Modules:
  0.0 776.5 jit_solution(16712205418882238552)
XLA Ops:
  16.5 6.5 project.1
  23.0 8.8 %attend.3 = (bf16[512,512]{1,0:T(8,128)(2,1)S(1)}, f32[4,2,512]{2,1,0:T(2,128)S(1)}) custom-call(bf16[1024,512]{1,0:T(8,128)(2,1)S(1)} %get-tuple-element.48.q_ref, bf16[1024,512]{1,0:T(8,128)(2,1)S(1)} %get-tuple-element.49.k_ref, bf16[1024,512]{1,0:T(8,128)(2,1)S(1)} %get-tuple-element.50.v_ref), custom_call_target="tpu_custom_call" | custom-call | tf_op jit(solution)/shard_map/attend/pallas_call | solution.py:132
  47.7 8.8 %attend.2 = (bf16[512,512]{1,0:T(8,128)(2,1)S(1)}, f32[4,2,512]{2,1,0:T(2,128)S(1)}) custom-call(bf16[1024,512]{1,0:T(8,128)(2,1)S(1)} %get-tuple-element.48.q_ref, bf16[1024,512]{1,0:T(8,128)(2,1)S(1)} %get-tuple-element.49.k_ref, bf16[1024,512]{1,0:T(8,128)(2,1)S(1)} %copy-done.3), custom_call_target="tpu_custom_call" | custom-call | tf_op jit(solution)/shard_map/attend/pallas_call | solution.py:132
  71.7 16.0 %feed_forward.4 = (bf16[1024,2048]{1,0:T(8,128)(2,1)}, bf16[1024,2048]{1,0:T(8,128)(2,1)}, bf16[1024,2048]{1,0:T(8,128)(2,1)}, bf16[512,1024]{1,0:T(8,128)(2,1)}...) custom-call(s32[3,16]{1,0:T(4,128)} %pad_add_fusion.slots_ref, bf16[1024,1024]{1,0:T(8,128)(2,1)} %get-tuple-element.132.nm_ref, ...), custom_call_target="tpu_custom_call" | custom-call | tf_op jit(solution)/shard_map/feed_forward/pallas_call | solution.py:254
  87.7 16.8 %feed_forward.5 = (bf16[1024,2048]{1,0:T(8,128)(2,1)}, bf16[1024,2048]{1,0:T(8,128)(2,1)}, bf16[1024,2048]{1,0:T(8,128)(2,1)}, bf16[512,1024]{1,0:T(8,128)(2,1)}...) custom-call(s32[3,16]{1,0:T(4,128)} %pad_add_fusion.slots_ref, ...), custom_call_target="tpu_custom_call", output_to_operand_aliasing={{0}: (7, {}), {1}: (8, {}), {2}: (9, {})} | custom-call | tf_op jit(solution)/shard_map/feed_forward/pallas_call | solution.py:254
  104.5 16.4 %feed_forward.6 = (bf16[1024,2048]{1,0:T(8,128)(2,1)}, bf16[1024,2048]{1,0:T(8,128)(2,1)}, bf16[1024,2048]{1,0:T(8,128)(2,1)}, bf16[512,1024]{1,0:T(8,128)(2,1)}...) custom-call(s32[3,16]{1,0:T(4,128)} %pad_add_fusion.slots_ref, ...), custom_call_target="tpu_custom_call", output_to_operand_aliasing={{0}: (7, {}), {1}: (8, {}), {2}: (9, {})} | custom-call | tf_op jit(solution)/shard_map/feed_forward/pallas_call | solution.py:254
  120.9 16.9 %feed_forward.7 = (bf16[1024,2048]{1,0:T(8,128)(2,1)}, bf16[1024,2048]{1,0:T(8,128)(2,1)}, bf16[1024,2048]{1,0:T(8,128)(2,1)}, bf16[512,1024]{1,0:T(8,128)(2,1)}...) custom-call(s32[3,16]{1,0:T(4,128)} %pad_add_fusion.slots_ref, ...), custom_call_target="tpu_custom_call", output_to_operand_aliasing={{0}: (7, {}), {1}: (8, {}), {2}: (9, {})} | custom-call | tf_op jit(solution)/shard_map/feed_forward/pallas_call | solution.py:254
  137.7 8.5 %fusion.40 = f32[1024,1024]{1,0:T(8,128)} fusion(bf16[1024,2048]{1,0:T(8,128)(2,1)} %get-tuple-element.64, bf16[1024,2048]{1,0:T(8,128)(2,1)S(1)} %copy-done.18), kind=kOutput, calls=%fused_computation.313 | convolution fusion | flops 4294967296 | bytes 12582912 | tf_op jit(solution)/shard_map/dot_general | solution.py:32
  146.2 6.7 convolution_add_fusion
  170.1 9.6 %collective-permute-done.57 = bf16[512,512]{1,0:T(8,128)(2,1)S(1)} collective-permute-done((bf16[512,512]{1,0:T(8,128)(2,1)S(1)}, bf16[512,512]{1,0:T(8,128)(2,1)S(1)}, u32[]{:S(2)}, u32[]{:S(2)}) %collective-permute-start.57) | collective-permute-done | bytes 524320 | tf_op jit(solution)/shard_map/ppermute | solution.py:303
  180.7 10.3 %collective-permute-done.65 = bf16[512,512]{1,0:T(8,128)(2,1)S(1)} collective-permute-done((bf16[512,512]{1,0:T(8,128)(2,1)S(1)}, bf16[512,512]{1,0:T(8,128)(2,1)S(1)}, u32[]{:S(2)}, u32[]{:S(2)}) %collective-permute-start.65) | collective-permute-done | bytes 524320 | tf_op jit(solution)/shard_map/ppermute | solution.py:303
  191.9 9.4 %collective-permute-done.73 = bf16[512,512]{1,0:T(8,128)(2,1)S(1)} collective-permute-done((bf16[512,512]{1,0:T(8,128)(2,1)S(1)}, bf16[512,512]{1,0:T(8,128)(2,1)S(1)}, u32[]{:S(2)}, u32[]{:S(2)}) %collective-permute-start.73) | collective-permute-done | bytes 524320 | tf_op jit(solution)/shard_map/ppermute | solution.py:303
  204.2 11.9 %collective-permute-done.97 = bf16[512,512]{1,0:T(8,128)(2,1)S(1)} collective-permute-done((bf16[512,512]{1,0:T(8,128)(2,1)S(1)}, bf16[512,512]{1,0:T(8,128)(2,1)S(1)}, u32[]{:S(2)}, u32[]{:S(2)}) %collective-permute-start.97) | collective-permute-done | bytes 524320 | tf_op jit(solution)/shard_map/ppermute | solution.py:303
  216.8 8.8 %collective-permute-done.105 = bf16[512,512]{1,0:T(8,128)(2,1)S(1)} collective-permute-done((bf16[512,512]{1,0:T(8,128)(2,1)S(1)}, bf16[512,512]{1,0:T(8,128)(2,1)S(1)}, u32[]{:S(2)}, u32[]{:S(2)}) %collective-permute-start.105) | collective-permute-done | bytes 524320 | tf_op jit(solution)/shard_map/ppermute | solution.py:303
  228.7 11.7 %collective-permute-done.129 = bf16[256,1024]{1,0:T(8,128)(2,1)S(1)} collective-permute-done((bf16[256,1024]{1,0:T(8,128)(2,1)S(1)}, bf16[256,1024]{1,0:T(8,128)(2,1)S(1)}, u32[]{:S(2)}, u32[]{:S(2)}) %collective-permute-start.129) | collective-permute-done | bytes 524320 | tf_op jit(solution)/shard_map/ppermute | solution.py:303
  241.1 10.6 %collective-permute-done.137 = bf16[256,1024]{1,0:T(8,128)(2,1)S(1)} collective-permute-done((bf16[256,1024]{1,0:T(8,128)(2,1)S(1)}, bf16[256,1024]{1,0:T(8,128)(2,1)S(1)}, u32[]{:S(2)}, u32[]{:S(2)}) %collective-permute-start.137) | collective-permute-done | bytes 524320 | tf_op jit(solution)/shard_map/ppermute | solution.py:303
  257.9 5.0 collective-permute-done.58
  263.5 5.0 collective-permute-done.66
  269.1 5.0 collective-permute-done.74
  274.7 5.0 collective-permute-done.82
  280.4 5.0 collective-permute-done.90
  393.3 5.1 collective-permute-start.54
  426.4 5.1 collective-permute-done.63
  432.0 5.0 collective-permute-done.71
  437.6 5.1 collective-permute-done.79
  469.5 9.7 %collective-permute-done.56 = bf16[512,512]{1,0:T(8,128)(2,1)S(1)} collective-permute-done((bf16[512,512]{1,0:T(8,128)(2,1)S(1)}, bf16[512,512]{1,0:T(8,128)(2,1)S(1)}, u32[]{:S(2)}, u32[]{:S(2)}) %collective-permute-start.56) | collective-permute-done | bytes 524320 | tf_op jit(solution)/shard_map/ppermute | solution.py:303
  480.7 9.8 %collective-permute-done.64 = bf16[512,512]{1,0:T(8,128)(2,1)S(1)} collective-permute-done((bf16[512,512]{1,0:T(8,128)(2,1)S(1)}, bf16[512,512]{1,0:T(8,128)(2,1)S(1)}, u32[]{:S(2)}, u32[]{:S(2)}) %collective-permute-start.64) | collective-permute-done | bytes 524320 | tf_op jit(solution)/shard_map/ppermute | solution.py:303
  491.9 5.3 collective-permute-done.72
  507.3 5.9 place.20.refs_0_
  513.2 5.9 place.21.refs_0_
  519.1 5.9 place.22.refs_0_
  525.0 5.9 place.23
  530.9 5.9 place.24.refs_0_
  536.8 5.9 place.25.refs_0_
  542.8 5.9 place.26.refs_0_
  548.7 5.9 place.27
  554.7 5.9 place.28.refs_0_
  560.6 5.9 place.29.refs_0_
  566.6 5.9 place.30.refs_0_
  572.6 5.9 place.31
  581.8 30.4 %attend_back.1 = (bf16[1024,512]{1,0:T(8,128)(2,1)S(1)}, bf16[1024,512]{1,0:T(8,128)(2,1)S(1)}, bf16[1024,512]{1,0:T(8,128)(2,1)S(1)}) custom-call(bf16[1024,512]{1,0:T(8,128)(2,1)S(1)} %get-tuple-element.48.q_ref, bf16[1024,512]{1,0:T(8,128)(2,1)} %copy-done.1, bf16[1024,512]{1,0:T(8,128)(2,1)} %copy-done.2, ...), custom_call_target="tpu_custom_call" | custom-call | tf_op jit(solution)/shard_map/attend_back/pallas_call | solution.py:191
  659.7 7.5 collective-permute-done.41
  731.8 4.9 collective-permute-done.39
  744.5 7.9 %collective-permute-done.24 = bf16[512,512]{1,0:T(8,128)(2,1)S(1)} collective-permute-done((bf16[512,512]{1,0:T(8,128)(2,1)S(1)}, bf16[512,512]{1,0:T(8,128)(2,1)S(1)}, u32[]{:S(2)}, u32[]{:S(2)}) %collective-permute-start.24) | collective-permute-done | bytes 524320 | tf_op jit(solution)/shard_map/ppermute | solution.py:303
  752.5 5.9 place.16
  758.5 5.9 place.17
  764.4 5.9 place.18
  770.4 5.9 place.19
  (731 shorter events, 378.5 us)
Async XLA Ops:
  5.0 56.7 %collective-permute-start.7 = (bf16[512,1024]{1,0:T(8,128)(2,1)}, bf16[512,1024]{1,0:T(8,128)(2,1)}, u32[]{:S(2)}, u32[]{:S(2)}) collective-permute-start(bf16[512,1024]{1,0:T(8,128)(2,1)} %param.24), channel_id=1, source_target_pairs={{1,0},{0,1},{3,2},{2,3},{5,4},{4,5},{7,6},{6,7},{9,8},{8,9},{11,10... | collective-permute-start | bytes 3145736 | tf_op jit(solution)/shard_map/ppermute | solution.py:369
  7.0 27.2 %collective-permute-start.3 = (f32[1,128]{1,0:T(1,128)S(1)}, f32[1,128]{1,0:T(1,128)S(1)}, u32[]{:S(2)}, u32[]{:S(2)}) collective-permute-start(f32[1,128]{1,0:T(1,128)S(1)} %broadcast_in_dim.25), channel_id=1, source_target_pairs={{0,2},{2,0},{4,6},{6,4},{8,10},{10,8},{12,14},{14,12},{16,18},{18,... | collective-permute-start | bytes 1544 | tf_op jit(solution)/shard_map/ppermute | solution.py:303
  33.6 22.9 %collective-permute-start.1 = (bf16[512,1024]{1,0:T(8,128)(2,1)}, bf16[512,1024]{1,0:T(8,128)(2,1)}, u32[]{:S(2)}, u32[]{:S(2)}) collective-permute-start(bf16[512,1024]{1,0:T(8,128)(2,1)} %convolution_convert_fusion.5), channel_id=1, source_target_pairs={{0,1},{1,0},{2,3},{3,2},{4,5},{5,4},{6,7},{7,6},{8,9},{9,8},{10,11... | collective-permute-start | bytes 3145736 | tf_op jit(solution)/shard_map/ppermute | solution.py:380
  153.1 247.2 %collective-permute-start.9 = (bf16[512,1024]{1,0:T(8,128)(2,1)S(1)}, bf16[512,1024]{1,0:T(8,128)(2,1)S(1)}, u32[]{:S(2)}, u32[]{:S(2)}) collective-permute-start(bf16[512,1024]{1,0:T(8,128)(2,1)S(1)} %slice.810), channel_id=1, source_target_pairs={{0,1},{1,0},{2,3},{3,2},{4,5},{5,4},{6,7},{7,6},{8,9},{9,8},{10,11... | collective-permute-start | bytes 3145736 | tf_op jit(solution)/shard_map/ppermute | solution.py:380
  155.3 24.4 %collective-permute-start.57 = (bf16[512,512]{1,0:T(8,128)(2,1)S(1)}, bf16[512,512]{1,0:T(8,128)(2,1)S(1)}, u32[]{:S(2)}, u32[]{:S(2)}) collective-permute-start(bf16[512,512]{1,0:T(8,128)(2,1)S(1)} %slice.504), channel_id=1, source_target_pairs={{0,4},{2,6},{4,0},{6,2},{8,12},{10,14},{12,8},{14,10},{16,20},{18,... | collective-permute-start | bytes 1572872 | tf_op jit(solution)/shard_map/ppermute | solution.py:303
  160.5 241.3 %collective-permute-start.8 = (bf16[512,1024]{1,0:T(8,128)(2,1)S(1)}, bf16[512,1024]{1,0:T(8,128)(2,1)S(1)}, u32[]{:S(2)}, u32[]{:S(2)}) collective-permute-start(bf16[512,1024]{1,0:T(8,128)(2,1)S(1)} %slice.811), channel_id=1, source_target_pairs={{0,1},{1,0},{2,3},{3,2},{4,5},{5,4},{6,7},{7,6},{8,9},{9,8},{10,11... | collective-permute-start | bytes 3145736 | tf_op jit(solution)/shard_map/ppermute | solution.py:380
  160.7 30.3 %collective-permute-start.65 = (bf16[512,512]{1,0:T(8,128)(2,1)S(1)}, bf16[512,512]{1,0:T(8,128)(2,1)S(1)}, u32[]{:S(2)}, u32[]{:S(2)}) collective-permute-start(bf16[512,512]{1,0:T(8,128)(2,1)S(1)} %slice.512), channel_id=1, source_target_pairs={{0,4},{2,6},{4,0},{6,2},{8,12},{10,14},{12,8},{14,10},{16,20},{18,... | collective-permute-start | bytes 1572872 | tf_op jit(solution)/shard_map/ppermute | solution.py:303
  168.5 32.8 %collective-permute-start.73 = (bf16[512,512]{1,0:T(8,128)(2,1)S(1)}, bf16[512,512]{1,0:T(8,128)(2,1)S(1)}, u32[]{:S(2)}, u32[]{:S(2)}) collective-permute-start(bf16[512,512]{1,0:T(8,128)(2,1)S(1)} %slice.520), channel_id=1, source_target_pairs={{0,4},{2,6},{4,0},{6,2},{8,12},{10,14},{12,8},{14,10},{16,20},{18,... | collective-permute-start | bytes 1572872 | tf_op jit(solution)/shard_map/ppermute | solution.py:303
  179.7 22.5 %collective-permute-start.81 = (bf16[512,512]{1,0:T(8,128)(2,1)S(1)}, bf16[512,512]{1,0:T(8,128)(2,1)S(1)}, u32[]{:S(2)}, u32[]{:S(2)}) collective-permute-start(bf16[512,512]{1,0:T(8,128)(2,1)S(1)} %slice.528), channel_id=1, source_target_pairs={{0,8},{2,10},{4,12},{6,14},{8,0},{10,2},{12,4},{14,6},{16,24},{18,... | collective-permute-start | bytes 1572872 | tf_op jit(solution)/shard_map/ppermute | solution.py:303
  202.2 23.4 %collective-permute-start.105 = (bf16[512,512]{1,0:T(8,128)(2,1)S(1)}, bf16[512,512]{1,0:T(8,128)(2,1)S(1)}, u32[]{:S(2)}, u32[]{:S(2)}) collective-permute-start(bf16[512,512]{1,0:T(8,128)(2,1)S(1)} %slice.552), channel_id=1, source_target_pairs={{0,8},{2,10},{4,12},{6,14},{8,0},{10,2},{12,4},{14,6},{16,24},{18,... | collective-permute-start | bytes 1572872 | tf_op jit(solution)/shard_map/ppermute | solution.py:303
  203.6 22.7 %collective-permute-start.113 = (bf16[256,1024]{1,0:T(8,128)(2,1)S(1)}, bf16[256,1024]{1,0:T(8,128)(2,1)S(1)}, u32[]{:S(2)}, u32[]{:S(2)}) collective-permute-start(bf16[256,1024]{1,0:T(8,128)(2,1)S(1)} %slice.560), channel_id=1, source_target_pairs={{0,2},{2,0},{4,6},{6,4},{8,10},{10,8},{12,14},{14,12},{16,18},{18,... | collective-permute-start | bytes 1572872 | tf_op jit(solution)/shard_map/ppermute | solution.py:303
  226.2 25.5 %collective-permute-start.137 = (bf16[256,1024]{1,0:T(8,128)(2,1)S(1)}, bf16[256,1024]{1,0:T(8,128)(2,1)S(1)}, u32[]{:S(2)}, u32[]{:S(2)}) collective-permute-start(bf16[256,1024]{1,0:T(8,128)(2,1)S(1)} %slice.584), channel_id=1, source_target_pairs={{0,2},{2,0},{4,6},{6,4},{8,10},{10,8},{12,14},{14,12},{16,18},{18,... | collective-permute-start | bytes 1572872 | tf_op jit(solution)/shard_map/ppermute | solution.py:303
  228.1 29.2 %collective-permute-start.50 = (bf16[256,512]{1,0:T(8,128)(2,1)S(1)}, bf16[256,512]{1,0:T(8,128)(2,1)S(1)}, u32[]{:S(2)}, u32[]{:S(2)}) collective-permute-start(bf16[256,512]{1,0:T(8,128)(2,1)S(1)} %slice.648), channel_id=1, source_target_pairs={{0,2},{2,0},{4,6},{6,4},{8,10},{10,8},{12,14},{14,12},{16,18},{18,... | collective-permute-start | bytes 786440 | tf_op jit(solution)/shard_map/ppermute | solution.py:303
  240.5 22.5 %collective-permute-start.58 = (bf16[256,512]{1,0:T(8,128)(2,1)S(1)}, bf16[256,512]{1,0:T(8,128)(2,1)S(1)}, u32[]{:S(2)}, u32[]{:S(2)}) collective-permute-start(bf16[256,512]{1,0:T(8,128)(2,1)S(1)} %slice.654), channel_id=1, source_target_pairs={{0,2},{2,0},{4,6},{6,4},{8,10},{10,8},{12,14},{14,12},{16,18},{18,... | collective-permute-start | bytes 786440 | tf_op jit(solution)/shard_map/ppermute | solution.py:303
  251.7 16.9 %collective-permute-start.66 = (bf16[256,512]{1,0:T(8,128)(2,1)S(1)}, bf16[256,512]{1,0:T(8,128)(2,1)S(1)}, u32[]{:S(2)}, u32[]{:S(2)}) collective-permute-start(bf16[256,512]{1,0:T(8,128)(2,1)S(1)} %slice.660), channel_id=1, source_target_pairs={{0,2},{2,0},{4,6},{6,4},{8,10},{10,8},{12,14},{14,12},{16,18},{18,... | collective-permute-start | bytes 786440 | tf_op jit(solution)/shard_map/ppermute | solution.py:303
  257.3 16.9 %collective-permute-start.74 = (bf16[256,512]{1,0:T(8,128)(2,1)S(1)}, bf16[256,512]{1,0:T(8,128)(2,1)S(1)}, u32[]{:S(2)}, u32[]{:S(2)}) collective-permute-start(bf16[256,512]{1,0:T(8,128)(2,1)S(1)} %slice.666), channel_id=1, source_target_pairs={{0,2},{2,0},{4,6},{6,4},{8,10},{10,8},{12,14},{14,12},{16,18},{18,... | collective-permute-start | bytes 786440 | tf_op jit(solution)/shard_map/ppermute | solution.py:303
  262.9 16.9 %collective-permute-start.82 = (bf16[256,512]{1,0:T(8,128)(2,1)S(1)}, bf16[256,512]{1,0:T(8,128)(2,1)S(1)}, u32[]{:S(2)}, u32[]{:S(2)}) collective-permute-start(bf16[256,512]{1,0:T(8,128)(2,1)S(1)} %slice.672), channel_id=1, source_target_pairs={{0,2},{2,0},{4,6},{6,4},{8,10},{10,8},{12,14},{14,12},{16,18},{18,... | collective-permute-start | bytes 786440 | tf_op jit(solution)/shard_map/ppermute | solution.py:303
  274.2 16.9 %collective-permute-start.98 = (bf16[256,512]{1,0:T(8,128)(2,1)S(1)}, bf16[256,512]{1,0:T(8,128)(2,1)S(1)}, u32[]{:S(2)}, u32[]{:S(2)}) collective-permute-start(bf16[256,512]{1,0:T(8,128)(2,1)S(1)} %slice.684), channel_id=1, source_target_pairs={{0,2},{2,0},{4,6},{6,4},{8,10},{10,8},{12,14},{14,12},{16,18},{18,... | collective-permute-start | bytes 786440 | tf_op jit(solution)/shard_map/ppermute | solution.py:303
  418.8 18.3 %collective-permute-start.71 = (bf16[256,512]{1,0:T(8,128)(2,1)S(1)}, bf16[256,512]{1,0:T(8,128)(2,1)S(1)}, u32[]{:S(2)}, u32[]{:S(2)}) collective-permute-start(bf16[256,512]{1,0:T(8,128)(2,1)S(1)} %pad_maximum_fusion.33), channel_id=1, source_target_pairs={{0,2},{2,0},{4,6},{6,4},{8,10},{10,8},{12,14},{14,12},{16,18},{18,... | collective-permute-start | bytes 786440 | tf_op jit(solution)/shard_map/ppermute | solution.py:303
  419.4 23.2 %collective-permute-start.79 = (bf16[256,512]{1,0:T(8,128)(2,1)S(1)}, bf16[256,512]{1,0:T(8,128)(2,1)S(1)}, u32[]{:S(2)}, u32[]{:S(2)}) collective-permute-start(bf16[256,512]{1,0:T(8,128)(2,1)S(1)} %pad_maximum_fusion.34), channel_id=1, source_target_pairs={{0,2},{2,0},{4,6},{6,4},{8,10},{10,8},{12,14},{14,12},{16,18},{18,... | collective-permute-start | bytes 786440 | tf_op jit(solution)/shard_map/ppermute | solution.py:303
  421.0 26.4 %collective-permute-start.87 = (bf16[256,512]{1,0:T(8,128)(2,1)S(1)}, bf16[256,512]{1,0:T(8,128)(2,1)S(1)}, u32[]{:S(2)}, u32[]{:S(2)}) collective-permute-start(bf16[256,512]{1,0:T(8,128)(2,1)S(1)} %pad_maximum_fusion.35), channel_id=1, source_target_pairs={{0,2},{2,0},{4,6},{6,4},{8,10},{10,8},{12,14},{14,12},{16,18},{18,... | collective-permute-start | bytes 786440 | tf_op jit(solution)/shard_map/ppermute | solution.py:303
  425.8 24.4 %collective-permute-start.95 = (bf16[256,512]{1,0:T(8,128)(2,1)S(1)}, bf16[256,512]{1,0:T(8,128)(2,1)S(1)}, u32[]{:S(2)}, u32[]{:S(2)}) collective-permute-start(bf16[256,512]{1,0:T(8,128)(2,1)S(1)} %pad_maximum_fusion.36), channel_id=1, source_target_pairs={{0,2},{2,0},{4,6},{6,4},{8,10},{10,8},{12,14},{14,12},{16,18},{18,... | collective-permute-start | bytes 786440 | tf_op jit(solution)/shard_map/ppermute | solution.py:303
  431.4 21.6 %collective-permute-start.103 = (bf16[256,512]{1,0:T(8,128)(2,1)S(1)}, bf16[256,512]{1,0:T(8,128)(2,1)S(1)}, u32[]{:S(2)}, u32[]{:S(2)}) collective-permute-start(bf16[256,512]{1,0:T(8,128)(2,1)S(1)} %pad_maximum_fusion.37), channel_id=1, source_target_pairs={{0,2},{2,0},{4,6},{6,4},{8,10},{10,8},{12,14},{14,12},{16,18},{18,... | collective-permute-start | bytes 786440 | tf_op jit(solution)/shard_map/ppermute | solution.py:303
  437.1 18.8 %collective-permute-start.111 = (bf16[256,512]{1,0:T(8,128)(2,1)S(1)}, bf16[256,512]{1,0:T(8,128)(2,1)S(1)}, u32[]{:S(2)}, u32[]{:S(2)}) collective-permute-start(bf16[256,512]{1,0:T(8,128)(2,1)S(1)} %pad_maximum_fusion.38), channel_id=1, source_target_pairs={{0,2},{2,0},{4,6},{6,4},{8,10},{10,8},{12,14},{14,12},{16,18},{18,... | collective-permute-start | bytes 786440 | tf_op jit(solution)/shard_map/ppermute | solution.py:303
  455.9 23.3 %collective-permute-start.56 = (bf16[512,512]{1,0:T(8,128)(2,1)S(1)}, bf16[512,512]{1,0:T(8,128)(2,1)S(1)}, u32[]{:S(2)}, u32[]{:S(2)}) collective-permute-start(bf16[512,512]{1,0:T(8,128)(2,1)S(1)} %pad_maximum_fusion.15), channel_id=1, source_target_pairs={{0,4},{2,6},{4,0},{6,2},{8,12},{10,14},{12,8},{14,10},{16,20},{18,... | collective-permute-start | bytes 1572872 | tf_op jit(solution)/shard_map/ppermute | solution.py:303
  457.6 32.8 %collective-permute-start.64 = (bf16[512,512]{1,0:T(8,128)(2,1)S(1)}, bf16[512,512]{1,0:T(8,128)(2,1)S(1)}, u32[]{:S(2)}, u32[]{:S(2)}) collective-permute-start(bf16[512,512]{1,0:T(8,128)(2,1)S(1)} %pad_maximum_fusion.16), channel_id=1, source_target_pairs={{0,4},{2,6},{4,0},{6,2},{8,12},{10,14},{12,8},{14,10},{16,20},{18,... | collective-permute-start | bytes 1572872 | tf_op jit(solution)/shard_map/ppermute | solution.py:303
  458.2 39.0 %collective-permute-start.72 = (bf16[512,512]{1,0:T(8,128)(2,1)S(1)}, bf16[512,512]{1,0:T(8,128)(2,1)S(1)}, u32[]{:S(2)}, u32[]{:S(2)}) collective-permute-start(bf16[512,512]{1,0:T(8,128)(2,1)S(1)} %pad_maximum_fusion.17), channel_id=1, source_target_pairs={{0,4},{2,6},{4,0},{6,2},{8,12},{10,14},{12,8},{14,10},{16,20},{18,... | collective-permute-start | bytes 1572872 | tf_op jit(solution)/shard_map/ppermute | solution.py:303
  462.3 40.5 %collective-permute-start.80 = (bf16[512,512]{1,0:T(8,128)(2,1)S(1)}, bf16[512,512]{1,0:T(8,128)(2,1)S(1)}, u32[]{:S(2)}, u32[]{:S(2)}) collective-permute-start(bf16[512,512]{1,0:T(8,128)(2,1)S(1)} %pad_maximum_fusion.18), channel_id=1, source_target_pairs={{0,4},{2,6},{4,0},{6,2},{8,12},{10,14},{12,8},{14,10},{16,20},{18,... | collective-permute-start | bytes 1572872 | tf_op jit(solution)/shard_map/ppermute | solution.py:303
  467.9 34.9 %collective-permute-start.88 = (bf16[512,512]{1,0:T(8,128)(2,1)S(1)}, bf16[512,512]{1,0:T(8,128)(2,1)S(1)}, u32[]{:S(2)}, u32[]{:S(2)}) collective-permute-start(bf16[512,512]{1,0:T(8,128)(2,1)S(1)} %pad_maximum_fusion.19), channel_id=1, source_target_pairs={{0,8},{2,10},{4,12},{6,14},{8,0},{10,2},{12,4},{14,6},{16,24},{18,... | collective-permute-start | bytes 1572872 | tf_op jit(solution)/shard_map/ppermute | solution.py:303
  479.2 24.3 %collective-permute-start.96 = (bf16[512,512]{1,0:T(8,128)(2,1)S(1)}, bf16[512,512]{1,0:T(8,128)(2,1)S(1)}, u32[]{:S(2)}, u32[]{:S(2)}) collective-permute-start(bf16[512,512]{1,0:T(8,128)(2,1)S(1)} %pad_maximum_fusion.20), channel_id=1, source_target_pairs={{0,8},{2,10},{4,12},{6,14},{8,0},{10,2},{12,4},{14,6},{16,24},{18,... | collective-permute-start | bytes 1572872 | tf_op jit(solution)/shard_map/ppermute | solution.py:303
  502.8 75.7 %collective-permute-start.10 = (bf16[512,1024]{1,0:T(8,128)(2,1)S(1)}, bf16[512,1024]{1,0:T(8,128)(2,1)S(1)}, u32[]{:S(2)}, u32[]{:S(2)}) collective-permute-start(bf16[512,1024]{1,0:T(8,128)(2,1)S(1)} %get-tuple-element.128), channel_id=1, source_target_pairs={{1,0},{0,1},{3,2},{2,3},{5,4},{4,5},{7,6},{6,7},{9,8},{8,9},{11,10... | collective-permute-start | bytes 3145736 | tf_op jit(solution)/shard_map/ppermute | solution.py:369
  502.8 51.8 %collective-permute-start.144 = (bf16[256,1024]{1,0:T(8,128)(2,1)S(1)}, bf16[256,1024]{1,0:T(8,128)(2,1)S(1)}, u32[]{:S(2)}, u32[]{:S(2)}) collective-permute-start(bf16[256,1024]{1,0:T(8,128)(2,1)S(1)} %pad_maximum_fusion.26), channel_id=1, source_target_pairs={{0,2},{2,0},{4,6},{6,4},{8,10},{10,8},{12,14},{14,12},{16,18},{18,... | collective-permute-start | bytes 1572872 | tf_op jit(solution)/shard_map/ppermute | solution.py:303
  503.5 57.1 %collective-permute-start.136 = (bf16[256,1024]{1,0:T(8,128)(2,1)S(1)}, bf16[256,1024]{1,0:T(8,128)(2,1)S(1)}, u32[]{:S(2)}, u32[]{:S(2)}) collective-permute-start(bf16[256,1024]{1,0:T(8,128)(2,1)S(1)} %pad_maximum_fusion.25), channel_id=1, source_target_pairs={{0,2},{2,0},{4,6},{6,4},{8,10},{10,8},{12,14},{14,12},{16,18},{18,... | collective-permute-start | bytes 1572872 | tf_op jit(solution)/shard_map/ppermute | solution.py:303
  505.0 61.6 %collective-permute-start.128 = (bf16[256,1024]{1,0:T(8,128)(2,1)S(1)}, bf16[256,1024]{1,0:T(8,128)(2,1)S(1)}, u32[]{:S(2)}, u32[]{:S(2)}) collective-permute-start(bf16[256,1024]{1,0:T(8,128)(2,1)S(1)} %pad_maximum_fusion.24), channel_id=1, source_target_pairs={{0,2},{2,0},{4,6},{6,4},{8,10},{10,8},{12,14},{14,12},{16,18},{18,... | collective-permute-start | bytes 1572872 | tf_op jit(solution)/shard_map/ppermute | solution.py:303
  506.6 65.9 %collective-permute-start.120 = (bf16[256,1024]{1,0:T(8,128)(2,1)S(1)}, bf16[256,1024]{1,0:T(8,128)(2,1)S(1)}, u32[]{:S(2)}, u32[]{:S(2)}) collective-permute-start(bf16[256,1024]{1,0:T(8,128)(2,1)S(1)} %pad_maximum_fusion.23), channel_id=1, source_target_pairs={{0,2},{2,0},{4,6},{6,4},{8,10},{10,8},{12,14},{14,12},{16,18},{18,... | collective-permute-start | bytes 1572872 | tf_op jit(solution)/shard_map/ppermute | solution.py:303
  617.6 76.4 %collective-permute-start.11 = (bf16[512,1024]{1,0:T(8,128)(2,1)}, bf16[512,1024]{1,0:T(8,128)(2,1)}, u32[]{:S(2)}, u32[]{:S(2)}) collective-permute-start(bf16[512,1024]{1,0:T(8,128)(2,1)} %slice.809), channel_id=1, source_target_pairs={{0,1},{1,0},{2,3},{3,2},{4,5},{5,4},{6,7},{7,6},{8,9},{9,8},{10,11... | collective-permute-start | bytes 3145736 | tf_op jit(solution)/shard_map/ppermute | solution.py:380
  627.4 23.7 %collective-permute-start.17 = (bf16[512,512]{1,0:T(8,128)(2,1)}, bf16[512,512]{1,0:T(8,128)(2,1)}, u32[]{:S(2)}, u32[]{:S(2)}) collective-permute-start(bf16[512,512]{1,0:T(8,128)(2,1)} %bitcast.15), channel_id=1, source_target_pairs={{0,2},{2,0},{4,6},{6,4},{8,10},{10,8},{12,14},{14,12},{16,18},{18,... | collective-permute-start | bytes 1572872 | tf_op jit(solution)/shard_map/ppermute | solution.py:303
  650.2 17.1 %collective-permute-start.41 = (bf16[256,1024]{1,0:T(8,128)(2,1)S(1)}, bf16[256,1024]{1,0:T(8,128)(2,1)S(1)}, u32[]{:S(2)}, u32[]{:S(2)}) collective-permute-start(bf16[256,1024]{1,0:T(8,128)(2,1)S(1)} %bitcast.60), channel_id=1, source_target_pairs={{0,8},{2,10},{4,12},{6,14},{8,0},{10,2},{12,4},{14,6},{16,24},{18,... | collective-permute-start | bytes 1572872 | tf_op jit(solution)/shard_map/ppermute | solution.py:303
  653.8 17.2 %collective-permute-start.26 = (bf16[256,512]{1,0:T(8,128)(2,1)S(1)}, bf16[256,512]{1,0:T(8,128)(2,1)S(1)}, u32[]{:S(2)}, u32[]{:S(2)}) collective-permute-start(bf16[256,512]{1,0:T(8,128)(2,1)S(1)} %slice.624), channel_id=1, source_target_pairs={{0,2},{2,0},{4,6},{6,4},{8,10},{10,8},{12,14},{14,12},{16,18},{18,... | collective-permute-start | bytes 786440 | tf_op jit(solution)/shard_map/ppermute | solution.py:303
  696.6 23.7 %collective-permute-start.22 = (bf16[128,512]{1,0:T(8,128)(2,1)S(1)}, bf16[128,512]{1,0:T(8,128)(2,1)S(1)}, u32[]{:S(2)}, u32[]{:S(2)}) collective-permute-start(bf16[128,512]{1,0:T(8,128)(2,1)S(1)} %pad_maximum_fusion.43), channel_id=1, source_target_pairs={{0,8},{2,10},{4,12},{6,14},{8,0},{10,2},{12,4},{14,6},{16,24},{18,... | collective-permute-start | bytes 393224 | tf_op jit(solution)/shard_map/ppermute | solution.py:303
  700.4 21.5 %collective-permute-start.30 = (bf16[128,512]{1,0:T(8,128)(2,1)S(1)}, bf16[128,512]{1,0:T(8,128)(2,1)S(1)}, u32[]{:S(2)}, u32[]{:S(2)}) collective-permute-start(bf16[128,512]{1,0:T(8,128)(2,1)S(1)} %pad_maximum_fusion.44), channel_id=1, source_target_pairs={{0,8},{2,10},{4,12},{6,14},{8,0},{10,2},{12,4},{14,6},{16,24},{18,... | collective-permute-start | bytes 393224 | tf_op jit(solution)/shard_map/ppermute | solution.py:303
  700.5 21.5 %collective-permute-start.38 = (bf16[128,512]{1,0:T(8,128)(2,1)S(1)}, bf16[128,512]{1,0:T(8,128)(2,1)S(1)}, u32[]{:S(2)}, u32[]{:S(2)}) collective-permute-start(bf16[128,512]{1,0:T(8,128)(2,1)S(1)} %pad_maximum_fusion.45), channel_id=1, source_target_pairs={{0,4},{2,6},{4,0},{6,2},{8,12},{10,14},{12,8},{14,10},{16,20},{18,... | collective-permute-start | bytes 393224 | tf_op jit(solution)/shard_map/ppermute | solution.py:303
  701.9 22.1 %collective-permute-start.46 = (bf16[64,1024]{1,0:T(8,128)(2,1)S(1)}, bf16[64,1024]{1,0:T(8,128)(2,1)S(1)}, u32[]{:S(2)}, u32[]{:S(2)}) collective-permute-start(bf16[64,1024]{1,0:T(8,128)(2,1)S(1)} %pad_maximum_fusion.46), channel_id=1, source_target_pairs={{0,4},{2,6},{4,0},{6,2},{8,12},{10,14},{12,8},{14,10},{16,20},{18,... | collective-permute-start | bytes 393224 | tf_op jit(solution)/shard_map/ppermute | solution.py:303
  724.0 18.3 %collective-permute-start.47 = (bf16[128,1024]{1,0:T(8,128)(2,1)S(1)}, bf16[128,1024]{1,0:T(8,128)(2,1)S(1)}, u32[]{:S(2)}, u32[]{:S(2)}) collective-permute-start(bf16[128,1024]{1,0:T(8,128)(2,1)S(1)} %pad_maximum_fusion.30), channel_id=1, source_target_pairs={{0,2},{2,0},{4,6},{6,4},{8,10},{10,8},{12,14},{14,12},{16,18},{18,... | collective-permute-start | bytes 786440 | tf_op jit(solution)/shard_map/ppermute | solution.py:303
  728.8 23.6 %collective-permute-start.24 = (bf16[512,512]{1,0:T(8,128)(2,1)S(1)}, bf16[512,512]{1,0:T(8,128)(2,1)S(1)}, u32[]{:S(2)}, u32[]{:S(2)}) collective-permute-start(bf16[512,512]{1,0:T(8,128)(2,1)S(1)} %pad_maximum_fusion.11), channel_id=1, source_target_pairs={{0,2},{2,0},{4,6},{6,4},{8,10},{10,8},{12,14},{14,12},{16,18},{18,... | collective-permute-start | bytes 1572872 | tf_op jit(solution)/shard_map/ppermute | solution.py:303
  731.1 27.3 %collective-permute-start.32 = (bf16[512,512]{1,0:T(8,128)(2,1)S(1)}, bf16[512,512]{1,0:T(8,128)(2,1)S(1)}, u32[]{:S(2)}, u32[]{:S(2)}) collective-permute-start(bf16[512,512]{1,0:T(8,128)(2,1)S(1)} %pad_maximum_fusion.12), channel_id=1, source_target_pairs={{0,4},{2,6},{4,0},{6,2},{8,12},{10,14},{12,8},{14,10},{16,20},{18,... | collective-permute-start | bytes 1572872 | tf_op jit(solution)/shard_map/ppermute | solution.py:303
  736.7 27.6 %collective-permute-start.40 = (bf16[512,512]{1,0:T(8,128)(2,1)S(1)}, bf16[512,512]{1,0:T(8,128)(2,1)S(1)}, u32[]{:S(2)}, u32[]{:S(2)}) collective-permute-start(bf16[512,512]{1,0:T(8,128)(2,1)S(1)} %pad_maximum_fusion.13), channel_id=1, source_target_pairs={{0,8},{2,10},{4,12},{6,14},{8,0},{10,2},{12,4},{14,6},{16,24},{18,... | collective-permute-start | bytes 1572872 | tf_op jit(solution)/shard_map/ppermute | solution.py:303
  742.4 28.0 %collective-permute-start.48 = (bf16[256,1024]{1,0:T(8,128)(2,1)S(1)}, bf16[256,1024]{1,0:T(8,128)(2,1)S(1)}, u32[]{:S(2)}, u32[]{:S(2)}) collective-permute-start(bf16[256,1024]{1,0:T(8,128)(2,1)S(1)} %pad_maximum_fusion.14), channel_id=1, source_target_pairs={{0,8},{2,10},{4,12},{6,14},{8,0},{10,2},{12,4},{14,6},{16,24},{18,... | collective-permute-start | bytes 1572872 | tf_op jit(solution)/shard_map/ppermute | solution.py:303
  (170 other events, 1556.0 us)

commit v2 on v1

--- a/solution.py
+++ b/solution.py
@@ -183,16 +183,17 @@
     dv_ref[...] = dv_sum[...].astype(BF)
 
 
-def attend_back(query, key, value, d_context, context, lse, cos_tab, sin_tab, tile=256):
-    cols = query.shape[1]
+def attend_back(query, key, value, d_context, context, lse, cos_tab, sin_tab, at, cols, tile=256):
     pairs = cols // LANES
-    strip = pl.BlockSpec((LEN, LANES), lambda p: (0, p))
+    first = at * pairs
+    strip = pl.BlockSpec((LEN, LANES), lambda p: (0, first + p))
+    result = pl.BlockSpec((LEN, LANES), lambda p: (0, p))
     table = pl.BlockSpec((LEN, LANES), lambda p: (0, 0))
     return pl.pallas_call(
         functools.partial(attend_back_kernel, tile),
         grid=(pairs,),
-        in_specs=[strip] * 5 + [pl.BlockSpec((1, 2, LEN), lambda p: (p, 0, 0)), table, table],
-        out_specs=[strip] * 3,
+        in_specs=[strip] * 5 + [pl.BlockSpec((1, 2, LEN), lambda p: (first + p, 0, 0)), table, table],
+        out_specs=[result] * 3,
         out_shape=[shape_of((LEN, cols), BF)] * 3,
         scratch_shapes=[pltpu.VMEM((LEN, LANES), F32)] * 2,
         compiler_params=params(48),
@@ -203,7 +204,7 @@
 def ff_kernel(
     n_pieces, slots_ref, nm_ref, nt_ref, sg_ref, wg_ref, wu_ref, wd_ref, *refs,
 ):
-    hid_ref, dg_ref, du_ref, gd_ref, gg_ref, gu_ref, ht_ref = refs[-7:]
+    hid_ref, dg_ref, du_ref, gd_ref, ga_ref, gb_ref, ht_ref = refs[-7:]
     width, block = wg_ref.shape
     tile = 256
 
@@ -224,24 +225,30 @@
 
     lax.fori_loop(0, LEN // tile, forward, 0)
 
-    def weight_grad(which, left_ref, right_ref, out_ref):
-        piece = out_ref.shape[0] // n_pieces
+    def weight_grad(which, left_ref, first, count, right_refs, out_ref):
+        piece = count // n_pieces
         step = max(tile, piece)
         per = step // piece
 
         def body(i, carry):
-            rows = pl.ds(pl.multiple_of(i * step, step), step)
-            grads = dot_nn(left_ref[rows, :], right_ref[...]).astype(BF)
-            for j in range(per):
-                at = pl.multiple_of(slots_ref[which, i * per + j] * piece, piece)
-                out_ref[pl.ds(at, piece), :] = grads[j * piece : (j + 1) * piece, :]
+            rows = pl.ds(pl.multiple_of(first + i * step, step), step)
+            left = left_ref[rows, :]
+            at_lane = 0
+            for right_ref in right_refs:
+                grads = dot_nn(left, right_ref[...]).astype(BF)
+                lanes = slice(at_lane, at_lane + grads.shape[1])
+                for j in range(per):
+                    at = pl.multiple_of(slots_ref[which, i * per + j] * piece, piece)
+                    out_ref[pl.ds(at, piece), lanes] = grads[j * piece : (j + 1) * piece, :]
+                at_lane = lanes.stop
             return carry
 
-        lax.fori_loop(0, out_ref.shape[0] // step, body, 0)
-
-    weight_grad(0, ht_ref, sg_ref, gd_ref)
-    weight_grad(1, nt_ref, dg_ref, gg_ref)
-    weight_grad(2, nt_ref, du_ref, gu_ref)
+        lax.fori_loop(0, count // step, body, 0)
+
+    half = width // 2
+    weight_grad(0, ht_ref, 0, block, [sg_ref], gd_ref)
+    weight_grad(1, nt_ref, 0, half, [dg_ref, du_ref], ga_ref)
+    weight_grad(2, nt_ref, half, half, [dg_ref, du_ref], gb_ref)
 
 
 def feed_forward(index, block, n_pieces, slots, nm, nt, sg, w_gate, w_up, w_down, kept):
@@ -250,6 +257,7 @@
     cols = pl.BlockSpec((width, block), lambda i, s: (0, index))
     kept_spec = pl.BlockSpec((LEN, block), lambda i, s: (0, index))
     grad = lambda dims: pl.BlockSpec(dims, lambda i, s: (0, 0))
+    chunks = [(block, width), (width // 2, 2 * block), (width // 2, 2 * block)]
     previous = list(kept) if kept is not None else []
     return pl.pallas_call(
         functools.partial(ff_kernel, n_pieces),
@@ -259,11 +267,11 @@
             in_specs=[whole, pl.BlockSpec((width, LEN), lambda i, s: (0, 0)), whole, cols, cols,
                       pl.BlockSpec((block, width), lambda i, s: (index, 0))]
             + [pl.BlockSpec(memory_space=pl.ANY)] * len(previous),
-            out_specs=[kept_spec] * 3 + [grad((block, width)), grad((width, block)), grad((width, block))],
+            out_specs=[kept_spec] * 3 + [grad(dims) for dims in chunks],
             scratch_shapes=[pltpu.VMEM((block, LEN), BF)],
         ),
         out_shape=[shape_of((LEN, units), BF)] * 3
-        + [shape_of((block, width), BF)] + [shape_of((width, block), BF)] * 2,
+        + [shape_of(dims, BF) for dims in chunks],
         input_output_aliases={7 + i: i for i in range(len(previous))},
         compiler_params=params(56),
         name="feed_forward",
@@ -273,9 +281,9 @@
 def orders_of(n_dp):
     bits = [1 << i for i in range(n_dp.bit_length() - 1)]
     if len(bits) < 4:
-        return [bits] * 3
+        return [bits] * 4
     a, b, c = bits[:3]
-    return [[a, b, c] + bits[3:], [b, a, c] + bits[3:], [c, a, b] + bits[3:]]
+    return [o + bits[3:] for o in ([a, b, c], [b, a, c], [c, a, b], [c, b, a])]
 
 
 def masks_of(order):
@@ -290,52 +298,208 @@
     return masks
 
 
-def slots_of(order, me):
-    masks = masks_of(order)
-    inverse = [0] * len(masks)
-    for slot, mask in enumerate(masks):
-        inverse[mask] = slot
-    table = jnp.array(inverse, jnp.int32)
-    return table[jnp.arange(len(masks), dtype=jnp.int32) ^ me]
+def slots_of(orders, me):
+    table = []
+    for order in orders:
+        inverse = [0] * (1 << len(order))
+        for slot, mask in enumerate(masks_of(order)):
+            inverse[mask] = slot
+        table.append(inverse)
+    size = len(table[0])
+    here = jnp.arange(size, dtype=jnp.int32) ^ me
+    match = here[:, None] == jnp.arange(size, dtype=jnp.int32)[None, :]
+    return jnp.stack([jnp.sum(jnp.where(match, jnp.array(t, jnp.int32)[None, :], 0), axis=1) for t in table])
 
 
 def swap_dp(values, bit, n_dp):
     return lax.ppermute(values, "dp", [(i, i ^ bit) for i in range(n_dp)])
 
 
-def sum_over_dp(values, order, n_dp):
-    for bit in order:
-        half = values.shape[0] // 2
-        values = values[:half] + swap_dp(values[half:], bit, n_dp)
-    for bit in order[::-1]:
-        values = jnp.concatenate([values, swap_dp(values, bit, n_dp)], axis=0)
-    return values
-
-
-def place_kernel(pieces_ref, in_ref, *refs):
-    refs[-1][...] = in_ref[...].astype(F32)
-
-
-def place(summed, pieces, full_shape, block_index, base):
-    n_pieces = pieces.shape[0]
-    rows, cols = summed.shape
-    piece = rows // n_pieces
-    row_block, col_block = block_index
-    given = [] if base is None else [base]
+class Chunk:
+    def __init__(self, values, order, done):
+        self.order, self.done = list(order), done
+        self.current, self.rows = values, values.shape[0]
+        self.at, self.last, self.parts = 0, -9, []
+
+    @property
+    def open(self):
+        return self.at < 2 * len(self.order)
+
+    @property
+    def bit(self):
+        return (self.order + self.order[::-1])[self.at]
+
+    def next_rows(self):
+        levels = len(self.order)
+        return self.rows >> (self.at + 1 if self.at < levels else 2 * levels - self.at)
+
+    def outgoing(self):
+        if self.at < len(self.order):
+            return [self.current[self.current.shape[0] // 2 :]]
+        return self.parts
+
+    def incoming(self, got):
+        self.at += 1
+        if self.at <= len(self.order):
+            self.current = self.current[: self.current.shape[0] // 2] + got
+            self.parts = [self.current]
+        else:
+            self.parts = self.parts + [got]
+
+
+def in_rounds(work, chunks, n_dp, limit):
+    placing = []
+    wanted = next(work)
+    before = None
+    now = 0
+
+    def finish(picks, got):
+        for bit, members in picks.items():
+            at = 0
+            for chunk in members:
+                rows = chunk.next_rows()
+                chunk.incoming(got[bit][at : at + rows])
+                at += rows
+                if not chunk.open:
+                    placing.append(chunk)
+
+    while wanted is not None or before is not None or any(c.open for c in chunks):
+        picks, loads = {}, {}
+        for chunk in chunks:
+            if not chunk.open or chunk.last > now - 2:
+                continue
+            bit, rows = chunk.bit, chunk.next_rows()
+            if loads.get(bit, 0) and loads[bit] + rows > limit:
+                continue
+            loads[bit] = loads.get(bit, 0) + rows
+            picks.setdefault(bit, []).append(chunk)
+            chunk.last = now
+        sends = {}
+        for bit in sorted(picks):
+            parts = [part for chunk in picks[bit] for part in chunk.outgoing()]
+            sends[bit] = parts[0] if len(parts) == 1 else jnp.concatenate(parts, axis=0)
+        ready = [jnp.concatenate(c.parts, axis=0) for c in placing]
+        held = (before[1] if before else {}, sends, ready, wanted)
+        got, tied_sends, ready, wanted = lax.optimization_barrier(held)
+        taken = {bit: swap_dp(values, bit, n_dp) for bit, values in sends.items()}
+        finished, placing = placing, []
+        if before:
+            finish(before[0], got)
+        for chunk, values in zip(finished, ready):
+            chunk.done(values)
+        if wanted is not None:
+            try:
+                wanted = work.send(wanted)
+            except StopIteration:
+                wanted = None
+        before = (picks, taken) if picks else None
+        now += 1
+        if not picks and placing:
+            for chunk in placing:
+                chunk.done(jnp.concatenate(chunk.parts, axis=0))
+            placing = []
+
+
+def place_kernel(slots_ref, which, n_pieces, folds, in_ref, *refs):
+    outs = refs[-max(fold[2] for fold in folds) - 1 :]
+    piece = in_ref.shape[0] // n_pieces
+    for p in range(n_pieces):
+        at = pl.multiple_of(slots_ref[which, p] * piece, piece)
+        rows = in_ref[pl.ds(at, piece), :].astype(F32)
+        for lane, end, out, row, col in folds:
+            width = end - lane
+            outs[out][row + p * piece : row + (p + 1) * piece, col : col + width] = rows[:, lane:end]
+
+
+def place(values, slots, which, n_pieces, folds, blocks, bases):
+    given = [base for base in bases if base is not None]
+    index_map = lambda at: (lambda i, s: at)
     return pl.pallas_call(
-        place_kernel,
+        lambda s, i, *refs: place_kernel(s, which, n_pieces, folds, i, *refs),
         grid_spec=pltpu.PrefetchScalarGridSpec(
             num_scalar_prefetch=1,
-            grid=(n_pieces,),
-            in_specs=[pl.BlockSpec((piece, cols), lambda i, s: (i, 0))]
+            grid=(1,),
+            in_specs=[pl.BlockSpec(values.shape, lambda i, s: (0, 0))]
             + [pl.BlockSpec(memory_space=pl.ANY)] * len(given),
-            out_specs=pl.BlockSpec((piece, cols), lambda i, s: (row_block * n_pieces + s[i], col_block)),
+            out_specs=[pl.BlockSpec(dims, index_map(at)) for _, dims, at in blocks],
         ),
-        out_shape=shape_of(full_shape, F32),
-        input_output_aliases={2: 0} if given else {},
+        out_shape=[shape_of(full, F32) for full, _, _ in blocks],
+        input_output_aliases={2 + i: i for i in range(len(given))},
         compiler_params=params(32),
         name="place",
-    )(pieces, summed, *given)
+    )(slots, values, *given)
+
+
+def late_kernel(n_pieces, slots_ref, nt_ref, dq_ref, dk_ref, dv_ref, *out_refs):
+    width = nt_ref.shape[0]
+    cols = dq_ref.shape[1]
+    rows = out_refs[0].shape[0]
+    piece = rows // n_pieces
+
+    def body(i, carry):
+        left = nt_ref[pl.ds(pl.multiple_of(i * rows, rows), rows), :]
+        for which, (d_ref, out_ref) in enumerate(zip((dq_ref, dk_ref, dv_ref), out_refs)):
+            grads = dot_nn(left, d_ref[...]).astype(BF)
+            for p in range(n_pieces):
+                at = pl.multiple_of(slots_ref[which, p] * piece, piece)
+                out_ref[pl.ds(at, piece), pl.ds(pl.multiple_of(i * cols, cols), cols)] = grads[
+                    p * piece : (p + 1) * piece, :
+                ]
+        return carry
+
+    lax.fori_loop(0, width // rows, body, 0)
+
+
+def late_grads(slots, n_pieces, turned, d_query, d_key, d_value):
+    width = turned.shape[0]
+    cols = d_query.shape[1]
+    rows = width * cols // 1024
+    whole = lambda a: pl.BlockSpec(a.shape, lambda i, s: (0, 0))
+    return pl.pallas_call(
+        functools.partial(late_kernel, n_pieces),
+        grid_spec=pltpu.PrefetchScalarGridSpec(
+            num_scalar_prefetch=1,
+            grid=(1,),
+            in_specs=[whole(turned)] + [whole(d_query)] * 3,
+            out_specs=[pl.BlockSpec((rows, 1024), lambda i, s: (0, 0))] * 3,
+        ),
+        out_shape=[shape_of((rows, 1024), BF)] * 3,
+        compiler_params=params(48),
+        name="late_grads",
+    )(slots, turned, d_query, d_key, d_value)
+
+
+def out_grad_kernel(n_pieces, slots_ref, ct_ref, d_ref, out_ref):
+    rows = ct_ref.shape[0]
+    piece = rows // n_pieces
+    step = max(256, piece)
+    per = step // piece
+
+    def body(i, carry):
+        left = ct_ref[pl.ds(pl.multiple_of(i * step, step), step), :]
+        grads = dot_nn(left, d_ref[...]).astype(BF)
+        for j in range(per):
+            at = pl.multiple_of(slots_ref[3, i * per + j] * piece, piece)
+            out_ref[pl.ds(at, piece), :] = grads[j * piece : (j + 1) * piece, :]
+        return carry
+
+    lax.fori_loop(0, rows // step, body, 0)
+
+
+def out_grad(slots, n_pieces, turned, d_branch):
+    whole = lambda a: pl.BlockSpec(a.shape, lambda i, s: (0, 0))
+    return pl.pallas_call(
+        functools.partial(out_grad_kernel, n_pieces),
+        grid_spec=pltpu.PrefetchScalarGridSpec(
+            num_scalar_prefetch=1,
+            grid=(1,),
+            in_specs=[whole(turned), whole(d_branch)],
+            out_specs=pl.BlockSpec(turned.shape, lambda i, s: (0, 0)),
+        ),
+        out_shape=shape_of(turned.shape, BF),
+        compiler_params=params(48),
+        name="out_grad",
+    )(slots, turned, d_branch)
 
 
 def per_device(
@@ -363,7 +527,8 @@
     rest = LEN - own
     units = w_gate.shape[1]
     block = min(512, units)
-    hypercube = n_dp & (n_dp - 1) == 0
+    head_cols = w_query.shape[1]
+    own_out_rows = w_out.shape[0]
 
     def from_member(values, step):
         return lax.ppermute(values, "tensor", [((i + step) % group, i) for i in range(group)])
@@ -387,11 +552,8 @@
     count = jnp.sum(jnp.where(picked, species_counts[None, :], 0), axis=1)
     inverse = jnp.broadcast_to(1.0 / count.astype(F32)[0], (1, LANES))
     inverse_sum = inverse
-    if hypercube:
-        for level in range(n_dp.bit_length() - 1):
-            inverse_sum = inverse_sum + swap_dp(inverse_sum, 1 << level, n_dp)
-    else:
-        inverse_sum = lax.psum(inverse_sum, "dp")
+    for level in range(n_dp.bit_length() - 1):
+        inverse_sum = inverse_sum + swap_dp(inverse_sum, 1 << level, n_dp)
     weight = (n_dp * inverse / inverse_sum)[:, :1]
 
     tok_own = tokens.astype(F32)
@@ -414,84 +576,107 @@
     sg_own = (cotangent.astype(F32) * weight).astype(BF)
     sg = jnp.concatenate([sg_own, (cot_rest.astype(F32) * weight).astype(BF)], axis=0)
 
-    orders = orders_of(n_dp) if hypercube else None
-    masks = [jnp.array(masks_of(o), jnp.int32) ^ me for o in orders]
-    slots = jnp.stack([slots_of(o, me) for o in orders])
-
-    grads = []
-    kept = None
-    for index in range(units // block):
-        *kept, g_down, g_gate, g_up = feed_forward(
-            index, block, n_dp, slots, mid, mid_turned, sg, w_gate, w_up, w_down, kept
-        )
-        grads.append((g_down, g_gate, g_up))
-    hidden, d_gate, d_up = kept
-
-    summed = [[sum_over_dp(g, o, n_dp) for g, o in zip(trio, orders)] for trio in grads]
-
-    d_mid = rows_to_owner(dot_nt(d_gate, w_gate) + dot_nt(d_up, w_up))
-    gain2_sum = jnp.sum(d_mid * normed2, axis=0)
-    bias2_sum = jnp.sum(d_mid, axis=0)
-    d_mixed = sg_own.astype(F32) + norm_back(d_mid, normed2, inv2, norm2_gain)
-    d_branch_own = d_mixed.astype(BF)
-    d_branch = jnp.concatenate([d_branch_own, rest_rows(d_branch_own)], axis=0)
-    context = jnp.concatenate([ctx_own, ctx_rest], axis=0)
-    lse = jnp.concatenate([lse_own, lse_rest], axis=2)
-    d_context = dot_nt(d_branch, w_out).astype(BF)
-    d_query, d_key, d_value = attend_back(
-        query, key, value, d_context, context, lse, cos_tab, sin_tab
-    )
-    normed_in = jnp.concatenate([in_own, in_rest], axis=0)
-    grad_out = dot_tn(context, d_branch).astype(BF)
-    late = [dot_tn(normed_in, d).astype(BF) for d in (d_query, d_key, d_value)]
-
-    output = (mixed + rows_to_owner(dot_nn(hidden, w_down))).astype(BF)
-    d_in = rows_to_owner(dot_nt(d_query, w_query) + dot_nt(d_key, w_key) + dot_nt(d_value, w_value))
-    gain1_sum = jnp.sum(d_in * normed1, axis=0)
-    bias1_sum = jnp.sum(d_in, axis=0)
-    input_grad = d_mixed + norm_back(d_in, normed1, inv1, norm1_gain)
-
-    vectors = jnp.stack([gain1_sum, bias1_sum, gain2_sum, bias2_sum])
-    if hypercube:
-        for level in range(n_dp.bit_length() - 1):
-            vectors = vectors + swap_dp(vectors, 1 << level, n_dp)
+    orders = orders_of(n_dp)
+    slots = slots_of(orders, me)
+    chunks, found = [], {}
+    late_fits = width * min(256, head_cols) // 1024 >= 16 * n_dp and own_out_rows >= 16 * n_dp
+
+    def send_off(values, which, folds, blocks, names):
+        def done(summed):
+            bases = [found.get(name) for name in names]
+            results = place(summed, slots, which, n_dp, folds, blocks, bases)
+            found.update(zip(names, results))
+
+        chunks.append(Chunk(values, orders[which], done))
+
+    def work():
+        kept = None
+        gate_slots = slots
+        for index in range(units // block):
+            *kept, g_down, g_first, g_second = feed_forward(
+                index, block, n_dp, gate_slots, mid, mid_turned, sg, w_gate, w_up, w_down, kept
+            )
+            send_off(
+                g_down, 0, [(0, width, 0, 0, 0)], [(w_down.shape, (block, width), (index, 0))], ["down"]
+            )
+            for at, values in enumerate((g_first, g_second)):
+                dims = (width // 2, block)
+                folds = [(0, block, 0, 0, 0), (block, 2 * block, 1, 0, 0)]
+                blocks = [(w.shape, dims, (at, index)) for w in (w_gate, w_up)]
+                send_off(values, 1 + at, folds, blocks, ["gate", "up"])
+            gate_slots, kept = yield (gate_slots, kept)
+        hidden, d_gate, d_up = kept
+        d_mid_part = dot_nt(d_gate, w_gate) + dot_nt(d_up, w_up)
+        d_mid_part, hidden = yield (d_mid_part, hidden)
+        d_mid = rows_to_owner(d_mid_part)
+        out_part = dot_nn(hidden, w_down)
+        d_mid, out_part = yield (d_mid, out_part)
+        found["output"] = (mixed + rows_to_owner(out_part)).astype(BF)
+        gain2_sum = jnp.sum(d_mid * normed2, axis=0)
+        bias2_sum = jnp.sum(d_mid, axis=0)
+        d_mixed = sg_own.astype(F32) + norm_back(d_mid, normed2, inv2, norm2_gain)
+        d_branch_own = d_mixed.astype(BF)
+        d_branch = jnp.concatenate([d_branch_own, rest_rows(d_branch_own)], axis=0)
+        (d_branch,) = yield (d_branch,)
+        context = jnp.concatenate([ctx_own, ctx_rest], axis=0)
+        lse = jnp.concatenate([lse_own, lse_rest], axis=2)
+        d_context = dot_nt(d_branch, w_out).astype(BF)
+        normed_in = jnp.concatenate([in_own, in_rest], axis=0)
+        in_turned = normed_in.T
+        if late_fits:
+            send_off(
+                out_grad(slots, n_dp, context.T, d_branch), 3, [(0, width, 0, 0, 0)],
+                [(w_out.shape, w_out.shape, (0, 0))], ["out"],
+            )
+        else:
+            found["out"] = lax.psum(dot_tn(context, d_branch).astype(BF), "dp").astype(F32)
+        cols = min(256, head_cols)
+        d_in_part = 0.0
+        for at in range(head_cols // cols):
+            d_context, d_in_part = yield (d_context, d_in_part)
+            strip = slice(at * cols, (at + 1) * cols)
+            backs = attend_back(query, key, value, d_context, context, lse, cos_tab, sin_tab, at, cols)
+            if late_fits:
+                rows = width * cols // 1024
+                folds = [(i * cols, (i + 1) * cols, 0, i * rows, 0) for i in range(width // rows)]
+                late = late_grads(slots, n_dp, in_turned, *backs)
+                for which, (name, values) in enumerate(zip(("query", "key", "value"), late)):
+                    blocks = [(w_query.shape, (width, cols), (0, at))]
+                    send_off(values, which, folds, blocks, [name])
+            else:
+                for name, d in zip(("query", "key", "value"), backs):
+                    summed = lax.psum(dot_tn(normed_in, d).astype(BF), "dp").astype(F32)
+                    found.setdefault(name, []).append(summed)
+            for d, w in zip(backs, (w_query, w_key, w_value)):
+                d_in_part = d_in_part + dot_nt(d, w[:, strip])
+        (d_in_part,) = yield (d_in_part,)
+        d_in = rows_to_owner(d_in_part)
+        gain1_sum = jnp.sum(d_in * normed1, axis=0)
+        bias1_sum = jnp.sum(d_in, axis=0)
+        found["input"] = d_mixed + norm_back(d_in, normed1, inv1, norm1_gain)
+        vectors = jnp.stack([gain1_sum, bias1_sum, gain2_sum, bias2_sum])
         total = vectors
         for step in range(1, group):
             total = total + from_member(vectors, step)
-        vectors = total
-    else:
-        vectors = lax.psum(vectors, ("dp", "tensor"))
-
-    def small_sum(values, order_at):
-        piece = values.shape[0] // n_dp
-        if piece < 16:
-            return lax.psum(values, "dp").astype(F32)
-        order = orders[order_at]
-        pieces = values.reshape(n_dp, piece, values.shape[1])
-        rel = jnp.take(pieces, masks[order_at], axis=0).reshape(values.shape)
-        return place(sum_over_dp(rel, order, n_dp), masks[order_at], values.shape, (0, 0), None)
-
-    g_out = small_sum(grad_out, 2)
-    g_query, g_key, g_value = (small_sum(g, at) for at, g in enumerate(late))
-    g_down = g_gate = g_up = None
-    for index, (s_down, s_gate, s_up) in enumerate(summed):
-        g_down = place(s_down, masks[0], w_down.shape, (index, 0), g_down)
-        g_gate = place(s_gate, masks[1], w_gate.shape, (0, index), g_gate)
-        g_up = place(s_up, masks[2], w_up.shape, (0, index), g_up)
+        for level in range(n_dp.bit_length() - 1):
+            (total,) = yield (total,)
+            total = total + swap_dp(total, 1 << level, n_dp)
+        found["vectors"] = total
+
+    in_rounds(work(), chunks, n_dp, 512)
+    vectors = found["vectors"]
     return (
-        output,
-        input_grad,
+        found["output"],
+        found["input"],
         vectors[0],
         vectors[1],
-        g_query,
-        g_key,
-        g_value,
-        g_out,
+        *(found[n] if late_fits else jnp.concatenate(found[n], axis=1) for n in ("query", "key", "value")),
+        found["out"],
         vectors[2],
         vectors[3],
-        g_gate,
-        g_up,
-        g_down,
+        found["gate"],
+        found["up"],
+        found["down"],
     )
 
 

time: 781 us -> 567 us (0.73)
  waiting for transfers between devices: 298 us -> 59.9 us
  other arithmetic: 37.9 us -> 87.6 us
  local copies, waits for them, and re-layouts: 33.1 us -> 79.9 us
  Pallas kernels: 215 us -> 169 us
  starting transfers between devices: 149 us -> 118 us
    ppermute x136 -> x86, waiting for transfers between devices: 297 us -> 59.8 us  [swap_dp(): return lax.ppermute(values, 'dp', [(i, i ^ bit) for i in range(n_dp)])]
    pallas_call x16 -> x22, Pallas kernels: 94.7 us -> 43.9 us  [the longest x19 35.9 us: place(): pl.pallas_call(lambda s, i, *refs: place_kernel(s, which, n_pieces, folds...]
    add x54 -> x49, other arithmetic: 7.23 us -> 46.3 us  [the longest x41 30.4 us: incoming(): self.current = self.current[:self.current.shape[0] // 2] + got]
    ppermute x136 -> x86, starting transfers between devices: 148 us -> 117 us  [swap_dp(): return lax.ppermute(values, 'dp', [(i, i ^ bit) for i in range(n_dp)])]
    unnamed x195 -> x421, local copies, waits for them, and re-layouts: 10.6 us -> 30.8 us
    slice x64 -> x68, local copies, waits for them, and re-layouts: 4.19 us -> 22.4 us  [the longest x66 20.5 us: outgoing(): return [self.current[self.current.shape[0] // 2:]]]
    concatenate x49 -> x47, other arithmetic: 1.01 us -> 13 us  [the longest x46 11.2 us: in_rounds(): sends[bit] = parts[0] if len(parts) == 1 else jnp.concatenate(parts, axis=0)]
    gather x7 -> x0, local copies, waits for them, and re-layouts: 11.8 us -> none  [the longest x4 9.78 us: small_sum(): rel = jnp.take(pieces, masks[order_at], axis=0).reshape(values.shape)]
  transfers between devices with their start and end apart: 145 -> 95, of which waited for: 86 -> 21; matrix products, arithmetic and copies ran while one was open for 9% -> 33% of each run, Pallas kernels for 15% -> 23%
where the time goes in v2:
time: 567 us; the launch traced here: 561 us
  Pallas kernels  169 us (30%)
  starting transfers between devices  118 us (21%)
  other arithmetic  87.6 us (15%)
  local copies, waits for them, and re-layouts  79.9 us (14%)
  waiting for transfers between devices  59.9 us (11%)
  matrix products  40.7 us (7%)
  between operations  5.67 us (1%)
    ppermute x86, starting transfers between devices, swap_dp(): return lax.ppermute(values, 'dp', [(i, i ^ bit) for i in range(n_dp)])  117 us
    pallas_call x4, Pallas kernels, feed_forward(): pl.pallas_call(functools.partial(ff_kernel, n_pieces), grid_spec=pltpu.Pr...  70.3 us
    ppermute x86, waiting for transfers between devices, swap_dp(): return lax.ppermute(values, 'dp', [(i, i ^ bit) for i in range(n_dp)])  59.8 us
    pallas_call x19, Pallas kernels, place(): pl.pallas_call(lambda s, i, *refs: place_kernel(s, which, n_pieces, folds...  35.9 us
    pallas_call x2, Pallas kernels, attend_back(): pl.pallas_call(functools.partial(attend_back_kernel, tile), grid=(pairs,)...  31.1 us
    unnamed x421, local copies, waits for them, and re-layouts  30.8 us
    add x41, other arithmetic, incoming(): self.current = self.current[:self.current.shape[0] // 2] + got  30.4 us
    dot_general x9, matrix products, dot_nt(): lax.dot_general(left, right, (((1,), (1,)), ((), ())), preferred_element_...  30.3 us
  transfers between devices with their start and end apart: 95, of which 21 were waited for; matrix products, arithmetic and copies ran while one was open for 33% of the time, Pallas kernels for 23%

profile of v2, /device:TPU:0, one launch (start us, length us, event | category | flops | bytes accessed | tf_op | source)
XLA Modules:
  0.0 561.4 jit_solution(17968689171462122308)
XLA Ops:
  14.5 6.1 %project.1 = (bf16[1024,512]{1,0:T(8,128)(2,1)S(1)}, bf16[1024,512]{1,0:T(8,128)(2,1)S(1)}, bf16[1024,512]{1,0:T(8,128)(2,1)S(1)}) custom-call(bf16[512,1024]{1,0:T(8,128)(2,1)S(1)} %copy-done.15, bf16[512,1024]{1,0:T(8,128)(2,1)} %copy.122.rest_ref, f32[1024,128]{1,0:T(8,128)S(1)} %copy-done.9, f32[1024,128]{1,0:T(8,128)S(1)} %copy-done.11, ...), custom_call_target="tpu_custom_call" | custom-call | tf_op jit(solution)/shard_map/project/pallas_call | solution.py:97
  20.7 8.8 %attend.3 = (bf16[512,512]{1,0:T(8,128)(2,1)S(1)}, f32[4,2,512]{2,1,0:T(2,128)S(1)}) custom-call(bf16[1024,512]{1,0:T(8,128)(2,1)S(1)} %get-tuple-element.195.q_ref, bf16[1024,512]{1,0:T(8,128)(2,1)S(1)} %get-tuple-element.196.k_ref, bf16[1024,512]{1,0:T(8,128)(2,1)S(1)} %get-tuple-element.197.v_ref), custom_call_target="tpu_custom_call" | custom-call | tf_op jit(solution)/shard_map/attend/pallas_call | solution.py:132
  33.4 3.0 collective-permute-start.3
  45.9 2.6 collective-permute-start.6
  49.7 9.1 %attend.2 = (bf16[512,512]{1,0:T(8,128)(2,1)S(1)}, f32[4,2,512]{2,1,0:T(2,128)S(1)}) custom-call(bf16[1024,512]{1,0:T(8,128)(2,1)S(1)} %get-tuple-element.195.q_ref, bf16[1024,512]{1,0:T(8,128)(2,1)S(1)} %get-tuple-element.196.k_ref, bf16[1024,512]{1,0:T(8,128)(2,1)S(1)} %copy-done.7), custom_call_target="tpu_custom_call" | custom-call | tf_op jit(solution)/shard_map/attend/pallas_call | solution.py:132
  67.0 2.6 copy.128.sg_ref
  69.5 3.4 fusion.38
  75.5 15.2 %feed_forward.4 = (bf16[1024,2048]{1,0:T(8,128)(2,1)}, bf16[1024,2048]{1,0:T(8,128)(2,1)}, bf16[1024,2048]{1,0:T(8,128)(2,1)}, bf16[512,1024]{1,0:T(8,128)(2,1)}...) custom-call(s32[4,16]{1,0:T(4,128)} %pad_add_fusion.slots_ref.s, bf16[1024,1024]{1,0:T(8,128)(2,1)} %copy.127.nm_ref, ...), custom_call_target="tpu_custom_call" | custom-call | tf_op jit(solution)/shard_map/feed_forward/pallas_call | solution.py:262
  103.0 15.5 %feed_forward.5 = (bf16[1024,2048]{1,0:T(8,128)(2,1)}, bf16[1024,2048]{1,0:T(8,128)(2,1)}, bf16[1024,2048]{1,0:T(8,128)(2,1)}, bf16[512,1024]{1,0:T(8,128)(2,1)}...) custom-call(s32[4,16]{1,0:T(4,128)} %pad_add_fusion.slots_ref.s, ...), custom_call_target="tpu_custom_call", output_to_operand_aliasing={{0}: (7, {}), {1}: (8, {}), {2}: (9, {})} | custom-call | tf_op jit(solution)/shard_map/feed_forward/pallas_call | solution.py:262
  125.0 24.2 %feed_forward.6 = (bf16[1024,2048]{1,0:T(8,128)(2,1)}, bf16[1024,2048]{1,0:T(8,128)(2,1)}, bf16[1024,2048]{1,0:T(8,128)(2,1)}, bf16[512,1024]{1,0:T(8,128)(2,1)}...) custom-call(s32[4,16]{1,0:T(4,128)} %pad_add_fusion.slots_ref.s, ...), custom_call_target="tpu_custom_call", output_to_operand_aliasing={{0}: (7, {}), {1}: (8, {}), {2}: (9, {})} | custom-call | tf_op jit(solution)/shard_map/feed_forward/pallas_call | solution.py:262
  161.2 15.4 %feed_forward.7 = (bf16[1024,2048]{1,0:T(8,128)(2,1)}, bf16[1024,2048]{1,0:T(8,128)(2,1)}, bf16[1024,2048]{1,0:T(8,128)(2,1)}, bf16[512,1024]{1,0:T(8,128)(2,1)}...) custom-call(s32[4,16]{1,0:T(4,128)} %pad_add_fusion.slots_ref.s, ...), custom_call_target="tpu_custom_call", output_to_operand_aliasing={{0}: (7, {}), {1}: (8, {}), {2}: (9, {})} | custom-call | tf_op jit(solution)/shard_map/feed_forward/pallas_call | solution.py:262
  191.9 4.5 fusion.44
  196.5 4.6 convolution_add_fusion
  203.9 4.2 collective-permute-done.20
  212.7 6.4 %fusion.45 = f32[1024,1024]{1,0:T(8,128)} fusion(bf16[1024,2048]{1,0:T(8,128)(2,1)S(1)} %copy-done.40, bf16[2048,1024]{1,0:T(8,128)(2,1)S(1)} %copy-done.36), kind=kOutput, calls=%fused_computation.427 | convolution fusion | flops 4294967296 | bytes 12582912 | tf_op jit(solution)/shard_map/dot_general | solution.py:28
  230.1 5.4 copy.137
  235.5 2.7 slice.1577
  252.6 4.0 copy.140.d_ref
  266.3 15.4 %attend_back.2 = (bf16[1024,256]{1,0:T(8,128)(2,1)S(1)}, bf16[1024,256]{1,0:T(8,128)(2,1)S(1)}, bf16[1024,256]{1,0:T(8,128)(2,1)S(1)}) custom-call(bf16[1024,512]{1,0:T(8,128)(2,1)S(1)} %copy-done.3, bf16[1024,512]{1,0:T(8,128)(2,1)S(1)} %copy-done.5, bf16[1024,512]{1,0:T(8,128)(2,1)S(1)} %copy-done.8, bf16[1024,512]{1,0:T(8,128)(2,1)} %convolution_convert_fusion.d_ref, ...), custom_call_target="tpu_custom_call" | custom-call | tf_op jit(solution)/shard_map/attend_back/pallas_call | solution.py:192
  281.7 2.8 fusion.26
  284.5 2.8 fusion.28
  287.3 3.1 late_grads.2
  300.4 5.1 add_add_fusion.1
  310.1 15.7 %attend_back.3 = (bf16[1024,256]{1,0:T(8,128)(2,1)S(1)}, bf16[1024,256]{1,0:T(8,128)(2,1)S(1)}, bf16[1024,256]{1,0:T(8,128)(2,1)S(1)}) custom-call(bf16[1024,512]{1,0:T(8,128)(2,1)S(1)} %copy-done.3, bf16[1024,512]{1,0:T(8,128)(2,1)S(1)} %copy-done.5, bf16[1024,512]{1,0:T(8,128)(2,1)S(1)} %copy-done.8, bf16[1024,512]{1,0:T(8,128)(2,1)} %convolution_convert_fusion.d_ref, ...), custom_call_target="tpu_custom_call" | custom-call | tf_op jit(solution)/shard_map/attend_back/pallas_call | solution.py:192
  329.1 2.8 fusion.16
  331.8 2.8 fusion.18
  334.6 2.8 fusion.20
  339.3 10.4 %add_add_fusion = f32[1024,1024]{0,1:T(8,128)} fusion(f32[1024,1024]{0,1:T(8,128)} %fusion.16, f32[1024,1024]{0,1:T(8,128)} %fusion.18, f32[1024,1024]{0,1:T(8,128)} %add_add_fusion.1, f32[1024,1024]{0,1:T(8,128)} %fusion.20), kind=kLoop, calls=%fused_computation | loop fusion | flops 3145728 | bytes 20971520 | tf_op jit(solution)/shard_map/add | solution.py:651
  350.3 2.9 late_grads.3
  374.8 4.4 fusion.11
  381.4 2.9 copy.148
  389.1 2.7 collective-permute-done.47
  411.2 2.6 collective-permute-done.57
  415.9 3.3 collective-permute-start.52
  421.7 5.5 collective-permute-done.58
  430.8 2.8 collective-permute-start.59
  433.7 5.0 collective-permute-done.59
  441.6 3.4 collective-permute-start.71
  446.4 6.3 %collective-permute-done.71 = bf16[48,1024]{1,0:T(8,128)(2,1)S(1)} collective-permute-done((bf16[48,1024]{1,0:T(8,128)(2,1)S(1)}, bf16[48,1024]{1,0:T(8,128)(2,1)S(1)}, u32[]{:S(2)}, u32[]{:S(2)}) %collective-permute-start.71) | collective-permute-done | bytes 98336 | tf_op jit(solution)/shard_map/ppermute | solution.py:315
  455.9 3.0 collective-permute-start.66
  461.0 3.0 collective-permute-start.67
  466.5 3.7 collective-permute-done.67
  471.7 4.2 collective-permute-start.78
  477.3 3.1 collective-permute-start.79
  480.4 6.9 %collective-permute-done.64 = bf16[512,1024]{1,0:T(8,128)(2,1)S(1)} collective-permute-done((bf16[512,1024]{1,0:T(8,128)(2,1)S(1)}, bf16[512,1024]{1,0:T(8,128)(2,1)S(1)}, u32[]{:S(2)}, u32[]{:S(2)}) %collective-permute-start.64) | collective-permute-done | bytes 1048608 | tf_op jit(solution)/shard_map/ppermute | solution.py:315
  498.5 3.4 collective-permute-start.75
  509.1 4.3 collective-permute-start.83
  539.0 3.4 collective-permute-done.86
  (852 shorter events, 277.8 us)
Async XLA Ops:
  31.4 27.4 %collective-permute-start.1 = (bf16[512,1024]{0,1:T(8,128)(2,1)}, bf16[512,1024]{0,1:T(8,128)(2,1)}, u32[]{:S(2)}, u32[]{:S(2)}) collective-permute-start(bf16[512,1024]{0,1:T(8,128)(2,1)} %convolution_convert_fusion.1), channel_id=1, source_target_pairs={{0,1},{1,0},{2,3},{3,2},{4,5},{5,4},{6,7},{7,6},{8,9},{9,8},{10,11... | collective-permute-start | bytes 3145736 | tf_op jit(solution)/shard_map/ppermute | solution.py:545
  38.7 26.6 %collective-permute-start.7 = (bf16[512,1024]{0,1:T(8,128)(2,1)}, bf16[512,1024]{0,1:T(8,128)(2,1)}, u32[]{:S(2)}, u32[]{:S(2)}) collective-permute-start(bf16[512,1024]{0,1:T(8,128)(2,1)} %copy.125), channel_id=1, source_target_pairs={{1,0},{0,1},{3,2},{2,3},{5,4},{4,5},{7,6},{6,7},{9,8},{8,9},{11,10... | collective-permute-start | bytes 3145736 | tf_op jit(solution)/shard_map/ppermute | solution.py:534
  92.7 31.8 %collective-permute-start.8 = (bf16[256,1024]{1,0:T(8,128)(2,1)}, bf16[256,1024]{1,0:T(8,128)(2,1)}, u32[]{:S(2)}, u32[]{:S(2)}) collective-permute-start(bf16[256,1024]{1,0:T(8,128)(2,1)} %slice.868), channel_id=1, source_target_pairs={{0,2},{2,0},{4,6},{6,4},{8,10},{10,8},{12,14},{14,12},{16,18},{18,... | collective-permute-start | bytes 1572872 | tf_op jit(solution)/shard_map/ppermute | solution.py:315
  95.8 29.2 %collective-permute-start.9 = (bf16[256,1024]{1,0:T(8,128)(2,1)}, bf16[256,1024]{1,0:T(8,128)(2,1)}, u32[]{:S(2)}, u32[]{:S(2)}) collective-permute-start(bf16[256,1024]{1,0:T(8,128)(2,1)} %slice.869), channel_id=1, source_target_pairs={{0,4},{2,6},{4,0},{6,2},{8,12},{10,14},{12,8},{14,10},{16,20},{18,... | collective-permute-start | bytes 1572872 | tf_op jit(solution)/shard_map/ppermute | solution.py:315
  98.2 26.9 %collective-permute-start.10 = (bf16[256,1024]{1,0:T(8,128)(2,1)}, bf16[256,1024]{1,0:T(8,128)(2,1)}, u32[]{:S(2)}, u32[]{:S(2)}) collective-permute-start(bf16[256,1024]{1,0:T(8,128)(2,1)} %slice.870), channel_id=1, source_target_pairs={{0,8},{2,10},{4,12},{6,14},{8,0},{10,2},{12,4},{14,6},{16,24},{18,... | collective-permute-start | bytes 1572872 | tf_op jit(solution)/shard_map/ppermute | solution.py:315
  123.2 36.4 %collective-permute-start.14 = (bf16[256,1024]{1,0:T(8,128)(2,1)}, bf16[256,1024]{1,0:T(8,128)(2,1)}, u32[]{:S(2)}, u32[]{:S(2)}) collective-permute-start(bf16[256,1024]{1,0:T(8,128)(2,1)} %slice.871), channel_id=1, source_target_pairs={{0,2},{2,0},{4,6},{6,4},{8,10},{10,8},{12,14},{14,12},{16,18},{18,... | collective-permute-start | bytes 1572872 | tf_op jit(solution)/shard_map/ppermute | solution.py:315
  124.1 37.1 %collective-permute-start.15 = (bf16[256,1024]{1,0:T(8,128)(2,1)}, bf16[256,1024]{1,0:T(8,128)(2,1)}, u32[]{:S(2)}, u32[]{:S(2)}) collective-permute-start(bf16[256,1024]{1,0:T(8,128)(2,1)} %slice.872), channel_id=1, source_target_pairs={{0,4},{2,6},{4,0},{6,2},{8,12},{10,14},{12,8},{14,10},{16,20},{18,... | collective-permute-start | bytes 1572872 | tf_op jit(solution)/shard_map/ppermute | solution.py:315
  124.6 36.6 %collective-permute-start.16 = (bf16[256,1024]{1,0:T(8,128)(2,1)}, bf16[256,1024]{1,0:T(8,128)(2,1)}, u32[]{:S(2)}, u32[]{:S(2)}) collective-permute-start(bf16[256,1024]{1,0:T(8,128)(2,1)} %slice.873), channel_id=1, source_target_pairs={{0,8},{2,10},{4,12},{6,14},{8,0},{10,2},{12,4},{14,6},{16,24},{18,... | collective-permute-start | bytes 1572872 | tf_op jit(solution)/shard_map/ppermute | solution.py:315
  153.8 30.1 %collective-permute-start.11 = (bf16[512,1024]{1,0:T(8,128)(2,1)}, bf16[512,1024]{1,0:T(8,128)(2,1)}, u32[]{:S(2)}, u32[]{:S(2)}) collective-permute-start(bf16[512,1024]{1,0:T(8,128)(2,1)} %pad_maximum_fusion.3), channel_id=1, source_target_pairs={{0,2},{2,0},{4,6},{6,4},{8,10},{10,8},{12,14},{14,12},{16,18},{18,... | collective-permute-start | bytes 3145736 | tf_op jit(solution)/shard_map/ppermute | solution.py:315
  157.2 26.7 %collective-permute-start.12 = (bf16[384,1024]{1,0:T(8,128)(2,1)}, bf16[384,1024]{1,0:T(8,128)(2,1)}, u32[]{:S(2)}, u32[]{:S(2)}) collective-permute-start(bf16[384,1024]{1,0:T(8,128)(2,1)} %pad_maximum_fusion.5), channel_id=1, source_target_pairs={{0,4},{2,6},{4,0},{6,2},{8,12},{10,14},{12,8},{14,10},{16,20},{18,... | collective-permute-start | bytes 2359304 | tf_op jit(solution)/shard_map/ppermute | solution.py:315
  159.6 23.9 %collective-permute-start.13 = (bf16[256,1024]{1,0:T(8,128)(2,1)}, bf16[256,1024]{1,0:T(8,128)(2,1)}, u32[]{:S(2)}, u32[]{:S(2)}) collective-permute-start(bf16[256,1024]{1,0:T(8,128)(2,1)} %slice.883), channel_id=1, source_target_pairs={{0,8},{2,10},{4,12},{6,14},{8,0},{10,2},{12,4},{14,6},{16,24},{18,... | collective-permute-start | bytes 1572872 | tf_op jit(solution)/shard_map/ppermute | solution.py:315
  181.9 26.2 %collective-permute-start.20 = (bf16[512,1024]{1,0:T(8,128)(2,1)S(1)}, bf16[512,1024]{1,0:T(8,128)(2,1)S(1)}, u32[]{:S(2)}, u32[]{:S(2)}) collective-permute-start(bf16[512,1024]{1,0:T(8,128)(2,1)S(1)} %pad_maximum_fusion.4), channel_id=1, source_target_pairs={{0,2},{2,0},{4,6},{6,4},{8,10},{10,8},{12,14},{14,12},{16,18},{18,... | collective-permute-start | bytes 3145736 | tf_op jit(solution)/shard_map/ppermute | solution.py:315
  182.9 20.9 %collective-permute-start.21 = (bf16[384,1024]{1,0:T(8,128)(2,1)S(1)}, bf16[384,1024]{1,0:T(8,128)(2,1)S(1)}, u32[]{:S(2)}, u32[]{:S(2)}) collective-permute-start(bf16[384,1024]{1,0:T(8,128)(2,1)S(1)} %pad_maximum_fusion.6), channel_id=1, source_target_pairs={{0,4},{2,6},{4,0},{6,2},{8,12},{10,14},{12,8},{14,10},{16,20},{18,... | collective-permute-start | bytes 2359304 | tf_op jit(solution)/shard_map/ppermute | solution.py:315
  189.0 33.0 %collective-permute-start.17 = (bf16[256,1024]{1,0:T(8,128)(2,1)S(1)}, bf16[256,1024]{1,0:T(8,128)(2,1)S(1)}, u32[]{:S(2)}, u32[]{:S(2)}) collective-permute-start(bf16[256,1024]{1,0:T(8,128)(2,1)S(1)} %pad_maximum_fusion.10), channel_id=1, source_target_pairs={{0,2},{2,0},{4,6},{6,4},{8,10},{10,8},{12,14},{14,12},{16,18},{18,... | collective-permute-start | bytes 1572872 | tf_op jit(solution)/shard_map/ppermute | solution.py:315
  190.3 31.7 %collective-permute-start.18 = (bf16[192,1024]{1,0:T(8,128)(2,1)S(1)}, bf16[192,1024]{1,0:T(8,128)(2,1)S(1)}, u32[]{:S(2)}, u32[]{:S(2)}) collective-permute-start(bf16[192,1024]{1,0:T(8,128)(2,1)S(1)} %pad_maximum_fusion.21), channel_id=1, source_target_pairs={{0,4},{2,6},{4,0},{6,2},{8,12},{10,14},{12,8},{14,10},{16,20},{18,... | collective-permute-start | bytes 1179656 | tf_op jit(solution)/shard_map/ppermute | solution.py:315
  202.2 19.3 %collective-permute-start.19 = (bf16[128,1024]{1,0:T(8,128)(2,1)S(1)}, bf16[128,1024]{1,0:T(8,128)(2,1)S(1)}, u32[]{:S(2)}, u32[]{:S(2)}) collective-permute-start(bf16[128,1024]{1,0:T(8,128)(2,1)S(1)} %pad_maximum_fusion.24), channel_id=1, source_target_pairs={{0,8},{2,10},{4,12},{6,14},{8,0},{10,2},{12,4},{14,6},{16,24},{18,... | collective-permute-start | bytes 786440 | tf_op jit(solution)/shard_map/ppermute | solution.py:315
  210.5 33.1 %collective-permute-start.28 = (bf16[256,1024]{1,0:T(8,128)(2,1)}, bf16[256,1024]{1,0:T(8,128)(2,1)}, u32[]{:S(2)}, u32[]{:S(2)}) collective-permute-start(bf16[256,1024]{1,0:T(8,128)(2,1)} %pad_maximum_fusion.11), channel_id=1, source_target_pairs={{0,2},{2,0},{4,6},{6,4},{8,10},{10,8},{12,14},{14,12},{16,18},{18,... | collective-permute-start | bytes 1572872 | tf_op jit(solution)/shard_map/ppermute | solution.py:315
  220.6 22.9 %collective-permute-start.29 = (bf16[192,1024]{1,0:T(8,128)(2,1)}, bf16[192,1024]{1,0:T(8,128)(2,1)}, u32[]{:S(2)}, u32[]{:S(2)}) collective-permute-start(bf16[192,1024]{1,0:T(8,128)(2,1)} %pad_maximum_fusion.22), channel_id=1, source_target_pairs={{0,4},{2,6},{4,0},{6,2},{8,12},{10,14},{12,8},{14,10},{16,20},{18,... | collective-permute-start | bytes 1179656 | tf_op jit(solution)/shard_map/ppermute | solution.py:315
  221.6 21.6 %collective-permute-start.30 = (bf16[128,1024]{1,0:T(8,128)(2,1)}, bf16[128,1024]{1,0:T(8,128)(2,1)}, u32[]{:S(2)}, u32[]{:S(2)}) collective-permute-start(bf16[128,1024]{1,0:T(8,128)(2,1)} %pad_maximum_fusion.25), channel_id=1, source_target_pairs={{0,8},{2,10},{4,12},{6,14},{8,0},{10,2},{12,4},{14,6},{16,24},{18,... | collective-permute-start | bytes 786440 | tf_op jit(solution)/shard_map/ppermute | solution.py:315
  226.4 37.2 %collective-permute-start.25 = (bf16[64,1024]{1,0:T(8,128)(2,1)}, bf16[64,1024]{1,0:T(8,128)(2,1)}, u32[]{:S(2)}, u32[]{:S(2)}) collective-permute-start(bf16[64,1024]{1,0:T(8,128)(2,1)} %slice.1183), channel_id=1, source_target_pairs={{0,4},{2,6},{4,0},{6,2},{8,12},{10,14},{12,8},{14,10},{16,20},{18,... | collective-permute-start | bytes 393224 | tf_op jit(solution)/shard_map/ppermute | solution.py:315
  239.7 26.6 %collective-permute-start.26 = (bf16[128,1024]{1,0:T(8,128)(2,1)}, bf16[128,1024]{1,0:T(8,128)(2,1)}, u32[]{:S(2)}, u32[]{:S(2)}) collective-permute-start(bf16[128,1024]{1,0:T(8,128)(2,1)} %pad_maximum_fusion.26), channel_id=1, source_target_pairs={{0,8},{2,10},{4,12},{6,14},{8,0},{10,2},{12,4},{14,6},{16,24},{18,... | collective-permute-start | bytes 786440 | tf_op jit(solution)/shard_map/ppermute | solution.py:315
  243.1 21.0 %collective-permute-start.27 = (bf16[96,1024]{1,0:T(8,128)(2,1)}, bf16[96,1024]{1,0:T(8,128)(2,1)}, u32[]{:S(2)}, u32[]{:S(2)}) collective-permute-start(bf16[96,1024]{1,0:T(8,128)(2,1)} %pad_maximum_fusion.38), channel_id=1, source_target_pairs={{0,16},{2,18},{4,20},{6,22},{8,24},{10,26},{12,28},{14,30},{16,0},... | collective-permute-start | bytes 589832 | tf_op jit(solution)/shard_map/ppermute | solution.py:315
  243.5 131.0 %collective-permute-start.24 = (bf16[512,1024]{0,1:T(8,128)(2,1)}, bf16[512,1024]{0,1:T(8,128)(2,1)}, u32[]{:S(2)}, u32[]{:S(2)}) collective-permute-start(bf16[512,1024]{0,1:T(8,128)(2,1)} %slice.1577), channel_id=1, source_target_pairs={{0,1},{1,0},{2,3},{3,2},{4,5},{5,4},{6,7},{7,6},{8,9},{9,8},{10,11... | collective-permute-start | bytes 3145736 | tf_op jit(solution)/shard_map/ppermute | solution.py:545
  262.0 44.2 %collective-permute-start.36 = (bf16[64,1024]{1,0:T(8,128)(2,1)}, bf16[64,1024]{1,0:T(8,128)(2,1)}, u32[]{:S(2)}, u32[]{:S(2)}) collective-permute-start(bf16[64,1024]{1,0:T(8,128)(2,1)} %slice.1195), channel_id=1, source_target_pairs={{0,4},{2,6},{4,0},{6,2},{8,12},{10,14},{12,8},{14,10},{16,20},{18,... | collective-permute-start | bytes 393224 | tf_op jit(solution)/shard_map/ppermute | solution.py:315
  263.5 45.6 %collective-permute-start.37 = (bf16[384,1024]{1,0:T(8,128)(2,1)}, bf16[384,1024]{1,0:T(8,128)(2,1)S(1)}, u32[]{:S(2)}, u32[]{:S(2)}) collective-permute-start(bf16[384,1024]{1,0:T(8,128)(2,1)} %pad_maximum_fusion.7), channel_id=1, source_target_pairs={{0,8},{2,10},{4,12},{6,14},{8,0},{10,2},{12,4},{14,6},{16,24},{18,... | collective-permute-start | bytes 2359304 | tf_op jit(solution)/shard_map/ppermute | solution.py:315
  264.1 43.5 %collective-permute-start.38 = (bf16[96,1024]{1,0:T(8,128)(2,1)S(1)}, bf16[96,1024]{1,0:T(8,128)(2,1)S(1)}, u32[]{:S(2)}, u32[]{:S(2)}) collective-permute-start(bf16[96,1024]{1,0:T(8,128)(2,1)S(1)} %pad_maximum_fusion.39), channel_id=1, source_target_pairs={{0,16},{2,18},{4,20},{6,22},{8,24},{10,26},{12,28},{14,30},{16,0},... | collective-permute-start | bytes 589832 | tf_op jit(solution)/shard_map/ppermute | solution.py:315
  291.1 65.1 %collective-permute-start.32 = (bf16[128,1024]{1,0:T(8,128)(2,1)}, bf16[128,1024]{1,0:T(8,128)(2,1)}, u32[]{:S(2)}, u32[]{:S(2)}) collective-permute-start(bf16[128,1024]{1,0:T(8,128)(2,1)} %slice.967), channel_id=1, source_target_pairs={{0,2},{2,0},{4,6},{6,4},{8,10},{10,8},{12,14},{14,12},{16,18},{18,... | collective-permute-start | bytes 786440 | tf_op jit(solution)/shard_map/ppermute | solution.py:315
  306.1 51.2 %collective-permute-start.33 = (bf16[128,1024]{1,0:T(8,128)(2,1)}, bf16[128,1024]{1,0:T(8,128)(2,1)}, u32[]{:S(2)}, u32[]{:S(2)}) collective-permute-start(bf16[128,1024]{1,0:T(8,128)(2,1)} %slice.968), channel_id=1, source_target_pairs={{0,4},{2,6},{4,0},{6,2},{8,12},{10,14},{12,8},{14,10},{16,20},{18,... | collective-permute-start | bytes 786440 | tf_op jit(solution)/shard_map/ppermute | solution.py:315
  307.5 50.3 %collective-permute-start.34 = (bf16[128,1024]{1,0:T(8,128)(2,1)}, bf16[128,1024]{1,0:T(8,128)(2,1)}, u32[]{:S(2)}, u32[]{:S(2)}) collective-permute-start(bf16[128,1024]{1,0:T(8,128)(2,1)} %slice.969), channel_id=1, source_target_pairs={{0,8},{2,10},{4,12},{6,14},{8,0},{10,2},{12,4},{14,6},{16,24},{18,... | collective-permute-start | bytes 786440 | tf_op jit(solution)/shard_map/ppermute | solution.py:315
  309.1 49.3 %collective-permute-start.35 = (bf16[192,1024]{1,0:T(8,128)(2,1)}, bf16[192,1024]{1,0:T(8,128)(2,1)}, u32[]{:S(2)}, u32[]{:S(2)}) collective-permute-start(bf16[192,1024]{1,0:T(8,128)(2,1)} %constant_dynamic-update-slice_fusion.4), channel_id=1, source_target_pairs={{0,16},{2,18},{4,20},{6,22},{8,24},{10,26},{12,28},{14,30},{16,0},... | collective-permute-start | bytes 1179656 | tf_op jit(solution)/shard_map/ppermute | solution.py:315
  356.2 29.8 %collective-permute-start.44 = (bf16[128,1024]{1,0:T(8,128)(2,1)}, bf16[128,1024]{1,0:T(8,128)(2,1)}, u32[]{:S(2)}, u32[]{:S(2)}) collective-permute-start(bf16[128,1024]{1,0:T(8,128)(2,1)} %slice.987), channel_id=1, source_target_pairs={{0,2},{2,0},{4,6},{6,4},{8,10},{10,8},{12,14},{14,12},{16,18},{18,... | collective-permute-start | bytes 786440 | tf_op jit(solution)/shard_map/ppermute | solution.py:315
  357.3 34.4 %collective-permute-start.45 = (bf16[256,1024]{1,0:T(8,128)(2,1)}, bf16[256,1024]{1,0:T(8,128)(2,1)}, u32[]{:S(2)}, u32[]{:S(2)}) collective-permute-start(bf16[256,1024]{1,0:T(8,128)(2,1)} %pad_maximum_fusion.12), channel_id=1, source_target_pairs={{0,4},{2,6},{4,0},{6,2},{8,12},{10,14},{12,8},{14,10},{16,20},{18,... | collective-permute-start | bytes 1572872 | tf_op jit(solution)/shard_map/ppermute | solution.py:315
  357.8 29.6 %collective-permute-start.46 = (bf16[128,1024]{1,0:T(8,128)(2,1)}, bf16[128,1024]{1,0:T(8,128)(2,1)}, u32[]{:S(2)}, u32[]{:S(2)}) collective-permute-start(bf16[128,1024]{1,0:T(8,128)(2,1)} %slice.992), channel_id=1, source_target_pairs={{0,8},{2,10},{4,12},{6,14},{8,0},{10,2},{12,4},{14,6},{16,24},{18,... | collective-permute-start | bytes 786440 | tf_op jit(solution)/shard_map/ppermute | solution.py:315
  370.5 21.3 %collective-permute-start.47 = (bf16[192,1024]{1,0:T(8,128)(2,1)}, bf16[192,1024]{1,0:T(8,128)(2,1)}, u32[]{:S(2)}, u32[]{:S(2)}) collective-permute-start(bf16[192,1024]{1,0:T(8,128)(2,1)} %constant_dynamic-update-slice_fusion.10), channel_id=1, source_target_pairs={{0,16},{2,18},{4,20},{6,22},{8,24},{10,26},{12,28},{14,30},{16,0},... | collective-permute-start | bytes 1179656 | tf_op jit(solution)/shard_map/ppermute | solution.py:315
  384.4 20.4 %collective-permute-start.40 = (bf16[128,1024]{1,0:T(8,128)(2,1)}, bf16[128,1024]{1,0:T(8,128)(2,1)S(1)}, u32[]{:S(2)}, u32[]{:S(2)}) collective-permute-start(bf16[128,1024]{1,0:T(8,128)(2,1)} %pad_maximum_fusion.27), channel_id=1, source_target_pairs={{0,2},{2,0},{4,6},{6,4},{8,10},{10,8},{12,14},{14,12},{16,18},{18,... | collective-permute-start | bytes 786440 | tf_op jit(solution)/shard_map/ppermute | solution.py:315
  386.0 20.2 %collective-permute-start.41 = (bf16[128,1024]{1,0:T(8,128)(2,1)}, bf16[128,1024]{1,0:T(8,128)(2,1)S(1)}, u32[]{:S(2)}, u32[]{:S(2)}) collective-permute-start(bf16[128,1024]{1,0:T(8,128)(2,1)} %pad_maximum_fusion.28), channel_id=1, source_target_pairs={{0,4},{2,6},{4,0},{6,2},{8,12},{10,14},{12,8},{14,10},{16,20},{18,... | collective-permute-start | bytes 786440 | tf_op jit(solution)/shard_map/ppermute | solution.py:315
  387.5 20.7 %collective-permute-start.42 = (bf16[128,1024]{1,0:T(8,128)(2,1)}, bf16[128,1024]{1,0:T(8,128)(2,1)S(1)}, u32[]{:S(2)}, u32[]{:S(2)}) collective-permute-start(bf16[128,1024]{1,0:T(8,128)(2,1)} %pad_maximum_fusion.29), channel_id=1, source_target_pairs={{0,8},{2,10},{4,12},{6,14},{8,0},{10,2},{12,4},{14,6},{16,24},{18,... | collective-permute-start | bytes 786440 | tf_op jit(solution)/shard_map/ppermute | solution.py:315
  400.3 18.9 %collective-permute-start.53 = (bf16[192,1024]{1,0:T(8,128)(2,1)S(1)}, bf16[192,1024]{1,0:T(8,128)(2,1)S(1)}, u32[]{:S(2)}, u32[]{:S(2)}) collective-permute-start(bf16[192,1024]{1,0:T(8,128)(2,1)S(1)} %pad_maximum_fusion.23), channel_id=1, source_target_pairs={{0,2},{2,0},{4,6},{6,4},{8,10},{10,8},{12,14},{14,12},{16,18},{18,... | collective-permute-start | bytes 1179656 | tf_op jit(solution)/shard_map/ppermute | solution.py:315
  420.4 24.6 %collective-permute-start.60 = (bf16[256,1024]{1,0:T(8,128)(2,1)S(1)}, bf16[256,1024]{1,0:T(8,128)(2,1)S(1)}, u32[]{:S(2)}, u32[]{:S(2)}) collective-permute-start(bf16[256,1024]{1,0:T(8,128)(2,1)S(1)} %get-tuple-element.576), channel_id=1, source_target_pairs={{0,2},{2,0},{4,6},{6,4},{8,10},{10,8},{12,14},{14,12},{16,18},{18,... | collective-permute-start | bytes 1572872 | tf_op jit(solution)/shard_map/ppermute | solution.py:315
  438.6 26.1 %collective-permute-start.68 = (bf16[512,1024]{1,0:T(8,128)(2,1)S(1)}, bf16[512,1024]{1,0:T(8,128)(2,1)S(1)}, u32[]{:S(2)}, u32[]{:S(2)}) collective-permute-start(bf16[512,1024]{1,0:T(8,128)(2,1)S(1)} %get-tuple-element.511), channel_id=1, source_target_pairs={{0,2},{2,0},{4,6},{6,4},{8,10},{10,8},{12,14},{14,12},{16,18},{18,... | collective-permute-start | bytes 3145736 | tf_op jit(solution)/shard_map/ppermute | solution.py:315
  440.5 20.5 %collective-permute-start.69 = (bf16[384,1024]{1,0:T(8,128)(2,1)S(1)}, bf16[384,1024]{1,0:T(8,128)(2,1)S(1)}, u32[]{:S(2)}, u32[]{:S(2)}) collective-permute-start(bf16[384,1024]{1,0:T(8,128)(2,1)S(1)} %get-tuple-element.521), channel_id=1, source_target_pairs={{0,4},{2,6},{4,0},{6,2},{8,12},{10,14},{12,8},{14,10},{16,20},{18,... | collective-permute-start | bytes 2359304 | tf_op jit(solution)/shard_map/ppermute | solution.py:315
  445.5 41.7 %collective-permute-start.64 = (bf16[512,1024]{1,0:T(8,128)(2,1)S(1)}, bf16[512,1024]{1,0:T(8,128)(2,1)S(1)}, u32[]{:S(2)}, u32[]{:S(2)}) collective-permute-start(bf16[512,1024]{1,0:T(8,128)(2,1)S(1)} %get-tuple-element.508), channel_id=1, source_target_pairs={{0,2},{2,0},{4,6},{6,4},{8,10},{10,8},{12,14},{14,12},{16,18},{18,... | collective-permute-start | bytes 3145736 | tf_op jit(solution)/shard_map/ppermute | solution.py:315
  452.7 24.6 %collective-permute-start.65 = (bf16[384,1024]{1,0:T(8,128)(2,1)S(1)}, bf16[384,1024]{1,0:T(8,128)(2,1)S(1)}, u32[]{:S(2)}, u32[]{:S(2)}) collective-permute-start(bf16[384,1024]{1,0:T(8,128)(2,1)S(1)} %get-tuple-element.517), channel_id=1, source_target_pairs={{0,4},{2,6},{4,0},{6,2},{8,12},{10,14},{12,8},{14,10},{16,20},{18,... | collective-permute-start | bytes 2359304 | tf_op jit(solution)/shard_map/ppermute | solution.py:315
  464.8 33.6 %collective-permute-start.76 = (bf16[256,1024]{1,0:T(8,128)(2,1)S(1)}, bf16[256,1024]{1,0:T(8,128)(2,1)S(1)}, u32[]{:S(2)}, u32[]{:S(2)}) collective-permute-start(bf16[256,1024]{1,0:T(8,128)(2,1)S(1)} %pad_maximum_fusion.15), channel_id=1, source_target_pairs={{0,2},{2,0},{4,6},{6,4},{8,10},{10,8},{12,14},{14,12},{16,18},{18,... | collective-permute-start | bytes 1572872 | tf_op jit(solution)/shard_map/ppermute | solution.py:315
  470.2 28.2 %collective-permute-start.77 = (bf16[256,1024]{1,0:T(8,128)(2,1)S(1)}, bf16[256,1024]{1,0:T(8,128)(2,1)S(1)}, u32[]{:S(2)}, u32[]{:S(2)}) collective-permute-start(bf16[256,1024]{1,0:T(8,128)(2,1)S(1)} %pad_maximum_fusion.16), channel_id=1, source_target_pairs={{0,4},{2,6},{4,0},{6,2},{8,12},{10,14},{12,8},{14,10},{16,20},{18,... | collective-permute-start | bytes 1572872 | tf_op jit(solution)/shard_map/ppermute | solution.py:315
  471.7 30.1 %collective-permute-start.78 = (bf16[256,1024]{1,0:T(8,128)(2,1)S(1)}, bf16[256,1024]{1,0:T(8,128)(2,1)S(1)}, u32[]{:S(2)}, u32[]{:S(2)}) collective-permute-start(bf16[256,1024]{1,0:T(8,128)(2,1)S(1)} %pad_maximum_fusion.17), channel_id=1, source_target_pairs={{0,8},{2,10},{4,12},{6,14},{8,0},{10,2},{12,4},{14,6},{16,24},{18,... | collective-permute-start | bytes 1572872 | tf_op jit(solution)/shard_map/ppermute | solution.py:315
  487.4 26.1 %collective-permute-start.72 = (bf16[320,1024]{1,0:T(8,128)(2,1)S(1)}, bf16[320,1024]{1,0:T(8,128)(2,1)S(1)}, u32[]{:S(2)}, u32[]{:S(2)}) collective-permute-start(bf16[320,1024]{1,0:T(8,128)(2,1)S(1)} %get-tuple-element.630), channel_id=1, source_target_pairs={{0,2},{2,0},{4,6},{6,4},{8,10},{10,8},{12,14},{14,12},{16,18},{18,... | collective-permute-start | bytes 1966088 | tf_op jit(solution)/shard_map/ppermute | solution.py:315
  516.5 18.7 %collective-permute-start.87 = (bf16[128,1024]{1,0:T(8,128)(2,1)S(1)}, bf16[128,1024]{1,0:T(8,128)(2,1)S(1)}, u32[]{:S(2)}, u32[]{:S(2)}) collective-permute-start(bf16[128,1024]{1,0:T(8,128)(2,1)S(1)} %get-tuple-element.668), channel_id=1, source_target_pairs={{0,2},{2,0},{4,6},{6,4},{8,10},{10,8},{12,14},{14,12},{16,18},{18,... | collective-permute-start | bytes 786440 | tf_op jit(solution)/shard_map/ppermute | solution.py:315
  (220 other events, 1941.6 us)

commit v3 on v2

v3 whole, which is shorter than its diff:
```python
import functools
import math

import jax
import jax.numpy as jnp
from jax import lax
from jax.experimental import pallas as pl
from jax.experimental.pallas import tpu as pltpu
from jax.sharding import PartitionSpec as P

HD = 64
LEN = 1024
SPECIES = 850
LANES = 128

eps_norm = 1e-05
BF = jnp.bfloat16
F32 = jnp.float32
EXP_SCALE = HD ** (-0.5) * math.log2(math.e)
MIB = 1024 * 1024


def shape_of(dims, dtype):
    return jax.ShapeDtypeStruct(dims, dtype)


def dot_nn(left, right):
    return lax.dot_general(left, right, (((1,), (0,)), ((), ())), preferred_element_type=F32)


def dot_nt(left, right):
    return lax.dot_general(left, right, (((1,), (1,)), ((), ())), preferred_element_type=F32)


def dot_tn(left, right):
    return lax.dot_general(left, right, (((0,), (0,)), ((), ())), preferred_element_type=F32)


def row_norm(values):
    center = values - jnp.mean(values, axis=-1, keepdims=True)
    inv_std = lax.rsqrt(jnp.mean(center * center, axis=-1, keepdims=True) + eps_norm)
    return (center * inv_std, inv_std)


def norm_back(upstream, normed, inv_std, gain_vec):
    scaled_up = upstream * gain_vec
    mean_one = jnp.mean(scaled_up, axis=-1, keepdims=True)
    mean_two = jnp.mean(scaled_up * normed, axis=-1, keepdims=True)
    return inv_std * (scaled_up - mean_one - normed * mean_two)


def params(mib):
    return pltpu.CompilerParams(vmem_limit_bytes=mib * MIB)


def swap_halves(values):
    width = values.shape[1]
    lane = lax.broadcasted_iota(jnp.int32, values.shape, 1) % HD
    ahead = pltpu.roll(values, width - HD // 2, 1)
    behind = pltpu.roll(values, HD // 2, 1)
    return jnp.where(lane < HD // 2, ahead, behind)


def rope_tables(start):
    half_dim = HD // 2
    inv_freq = 1.0 / 10000.0 ** (jnp.arange(half_dim, dtype=F32) * 2.0 / HD)
    position = (start + jnp.arange(LEN, dtype=jnp.int32)) % LEN
    angles = position.astype(F32)[:, None] * inv_freq[None, :]
    cos_tab, sin_tab = jnp.cos(angles), jnp.sin(angles)
    return (
        jnp.concatenate([cos_tab] * 4, axis=1),
        jnp.concatenate([-sin_tab, sin_tab] * 2, axis=1),
    )


def project_kernel(own_ref, rest_ref, cos_ref, sin_ref, wq_ref, wk_ref, wv_ref, q_ref, k_ref, v_ref):
    own = own_ref.shape[0]
    for rows, x_ref in ((slice(0, own), own_ref), (slice(own, LEN), rest_ref)):
        x = x_ref[...]
        cos_tab, sin_tab = cos_ref[rows, :], sin_ref[rows, :]
        for w_ref, out_ref in ((wq_ref, q_ref), (wk_ref, k_ref)):
            lin = dot_nn(x, w_ref[...])
            for at in range(0, lin.shape[1], LANES):
                part = lin[:, at : at + LANES]
                turned = part * cos_tab + swap_halves(part) * sin_tab
                out_ref[rows, at : at + LANES] = turned.astype(BF)
        v_ref[rows, :] = dot_nn(x, wv_ref[...]).astype(BF)


def project(own, rest, cos_tab, sin_tab, w_query, w_key, w_value):
    cols = w_query.shape[1]
    block = min(256, cols)
    width = own.shape[1]
    whole = lambda a: pl.BlockSpec(a.shape, lambda i: (0, 0))
    w_spec = pl.BlockSpec((width, block), lambda i: (0, i))
    o_spec = pl.BlockSpec((LEN, block), lambda i: (0, i))
    return pl.pallas_call(
        project_kernel,
        grid=(cols // block,),
        in_specs=[whole(own), whole(rest), whole(cos_tab), whole(sin_tab), w_spec, w_spec, w_spec],
        out_specs=[o_spec] * 3,
        out_shape=[shape_of((LEN, cols), BF)] * 3,
        compiler_params=params(28),
        name="project",
    )(own, rest, cos_tab, sin_tab, w_query, w_key, w_value)


def head_only(values, head):
    lane = lax.broadcasted_iota(jnp.int32, values.shape, 1)
    return jnp.where(lane // HD == head, values, jnp.zeros_like(values))


def attend_kernel(q_ref, k_ref, v_ref, ctx_ref, lse_ref):
    k = k_ref[...]
    v_turned = v_ref[...].T
    parts = []
    for head in range(2):
        scores = dot_nt(k, head_only(q_ref[...], head))
        top = jnp.max(scores, axis=0, keepdims=True)
        exps = jnp.exp2((scores - top) * EXP_SCALE)
        total = jnp.sum(exps, axis=0, keepdims=True)
        mix = dot_nn(v_turned[head * HD : (head + 1) * HD, :], exps.astype(BF))
        parts.append(mix * (1.0 / total))
        lse_ref[0, head : head + 1, :] = top * EXP_SCALE + jnp.log2(total)
    ctx_ref[...] = jnp.concatenate(parts, axis=0).T.astype(BF)


def attend(query, key, value, first, count, tile):
    cols = query.shape[1]
    pairs = cols // LANES
    whole = pl.BlockSpec((LEN, LANES), lambda p, i: (0, p))
    return pl.pallas_call(
        attend_kernel,
        grid=(pairs, count // tile),
        in_specs=[pl.BlockSpec((tile, LANES), lambda p, i: (first // tile + i, p)), whole, whole],
        out_specs=[
            pl.BlockSpec((tile, LANES), lambda p, i: (i, p)),
            pl.BlockSpec((1, 2, tile), lambda p, i: (p, 0, i)),
        ],
        out_shape=[shape_of((count, cols), BF), shape_of((pairs, 2, count), F32)],
        compiler_params=params(24),
        name="attend",
    )(query, key, value)


def attend_back_kernel(
    tile, q_ref, k_ref, v_ref, d_ref, delta_ref, lse_ref, cos_ref, sin_ref, *refs,
):
    dq_ref, dk_ref, dv_ref, dk_sum, dv_sum = refs[-5:]
    scale = HD ** (-0.5)
    k, v = k_ref[...], v_ref[...]
    k_turned = k.T

    def unrotate(grads, rows):
        grads = grads * scale
        return (grads * cos_ref[rows, :] - swap_halves(grads) * sin_ref[rows, :]).astype(BF)

    dk_sum[...] = jnp.zeros_like(dk_sum)
    dv_sum[...] = jnp.zeros_like(dv_sum)

    def step(i, carry):
        at = pl.multiple_of(i * tile, tile)
        rows = pl.ds(at, tile)
        q, d = q_ref[rows, :], d_ref[rows, :]
        parts = []
        for head in range(2):
            q_head, d_head = head_only(q, head), head_only(d, head)
            scores = dot_nt(k, q_head)
            probs = jnp.exp2(scores * EXP_SCALE - lse_ref[0, head : head + 1, rows])
            d_probs = dot_nt(v, d_head)
            d_scores = (probs * (d_probs - delta_ref[0, head : head + 1, rows])).astype(BF)
            dv_sum[...] += dot_nn(probs.astype(BF), d_head)
            dk_sum[...] += dot_nn(d_scores, q_head)
            parts.append(dot_nn(k_turned[head * HD : (head + 1) * HD, :], d_scores))
        dq_ref[rows, :] = unrotate(jnp.concatenate(parts, axis=0).T, rows)
        return carry

    lax.fori_loop(0, LEN // tile, step, 0)
    everything = slice(0, LEN)
    dk_ref[...] = unrotate(dk_sum[...], everything)
    dv_ref[...] = dv_sum[...].astype(BF)


def attend_back(query, key, value, d_context, delta, lse, cos_tab, sin_tab, first, pairs, given, tile=256):
    cols = query.shape[1]
    strip = pl.BlockSpec((LEN, LANES), lambda p: (0, first + p))
    table = pl.BlockSpec((LEN, LANES), lambda p: (0, 0))
    sums = pl.BlockSpec((1, 2, LEN), lambda p: (first + p, 0, 0))
    given = list(given)
    return pl.pallas_call(
        functools.partial(attend_back_kernel, tile),
        grid=(pairs,),
        in_specs=[strip] * 4 + [sums, sums, table, table] + [pl.BlockSpec(memory_space=pl.ANY)] * len(given),
        out_specs=[strip] * 3,
        out_shape=[shape_of((LEN, cols), BF)] * 3,
        scratch_shapes=[pltpu.VMEM((LEN, LANES), F32)] * 2,
        input_output_aliases={8 + i: i for i in range(len(given))},
        compiler_params=params(24),
        name="attend_back",
    )(query, key, value, d_context, delta, lse, cos_tab, sin_tab, *given)


def whole_of(array):
    return pl.BlockSpec(array.shape, lambda *_: (0,) * array.ndim)


def norm_in_kernel(tok_ref, gain_ref, bias_ref, out_ref):
    normed, _ = row_norm(tok_ref[...].astype(F32))
    out_ref[...] = (normed * gain_ref[...] + bias_ref[...]).astype(BF)


def norm_in(tokens, gain, bias):
    return pl.pallas_call(
        norm_in_kernel,
        out_shape=shape_of(tokens.shape, BF),
        compiler_params=params(16),
        name="norm_in",
    )(tokens, gain[None, :], bias[None, :])


def norm_mid_kernel(n_got, tok_ref, ctx_ref, w_ref, gain_ref, bias_ref, *refs):
    mixed_ref, mid_ref = refs[n_got:]
    mixed = tok_ref[...].astype(F32) + dot_nn(ctx_ref[...], w_ref[...])
    for got_ref in refs[:n_got]:
        mixed = mixed + got_ref[...].astype(F32)
    mixed_ref[...] = mixed
    normed, _ = row_norm(mixed)
    mid_ref[...] = (normed * gain_ref[...] + bias_ref[...]).astype(BF)


def norm_mid(tokens, ctx, w_out, gain, bias, got):
    return pl.pallas_call(
        functools.partial(norm_mid_kernel, len(got)),
        out_shape=[shape_of(tokens.shape, F32), shape_of(tokens.shape, BF)],
        compiler_params=params(24),
        name="norm_mid",
    )(tokens, ctx, w_out, gain[None, :], bias[None, :], *got)


def norm_back_kernel(n_got, kind, x_ref, base_ref, gain_ref, scale_ref, part_ref, *refs):
    upstream = part_ref[...]
    for got_ref in refs[:n_got]:
        upstream = upstream + got_ref[...].astype(F32)
    normed, inv_std = row_norm(x_ref[...].astype(F32))
    result = base_ref[...].astype(F32) + norm_back(upstream, normed, inv_std, gain_ref[...])
    sums_ref = refs[-1]
    sums_ref[0:1, :] = jnp.sum(upstream * normed, axis=0, keepdims=True)
    sums_ref[1:2, :] = jnp.sum(upstream, axis=0, keepdims=True)
    if kind == "mid":
        refs[n_got][...] = result
        refs[n_got + 1][...] = result.astype(BF)
    else:
        refs[n_got][...] = result * scale_ref[...]


def norm_backward(kind, values, base, gain, scale, part, got):
    rows, width = values.shape
    outs = [shape_of((rows, width), F32)]
    if kind == "mid":
        outs.append(shape_of((rows, width), BF))
    outs.append(shape_of((2, width), F32))
    own = pl.BlockSpec((rows, width), lambda i: (0, 0))
    vector = pl.BlockSpec((1, width), lambda i: (0, 0))
    return pl.pallas_call(
        functools.partial(norm_back_kernel, len(got), kind),
        grid=(1,),
        in_specs=[own, own, vector, pl.BlockSpec((1, 1), lambda i: (0, 0)), own] + [own] * len(got),
        out_specs=[pl.BlockSpec(o.shape, lambda i: (0, 0)) for o in outs],
        out_shape=outs,
        compiler_params=params(32),
        name="norm_back",
    )(values, base, gain[None, :], scale, part, *got)


def turn_kernel(n_pieces, slots_ref, own_ref, rest_ref, turned_ref, both_ref):
    at = 0
    for x_ref in (own_ref, rest_ref):
        count = x_ref.shape[0]
        both_ref[at : at + count, :] = x_ref[...]
        turned = x_ref[...].T
        half = turned.shape[0] // 2
        piece = half // n_pieces
        for which in (1, 2):
            first = (which - 1) * half
            for p in range(n_pieces):
                to = pl.multiple_of(first + slots_ref[which, p] * piece, piece)
                turned_ref[pl.ds(to, piece), at : at + count] = turned[
                    first + p * piece : first + (p + 1) * piece, :
                ]
        at += count


def turn(own, rest, slots, n_pieces):
    width = own.shape[1]
    return pl.pallas_call(
        functools.partial(turn_kernel, n_pieces),
        grid_spec=pltpu.PrefetchScalarGridSpec(
            num_scalar_prefetch=1,
            grid=(1,),
            in_specs=[whole_of(own), whole_of(rest)],
            out_specs=[pl.BlockSpec((width, LEN), lambda i, s: (0, 0)), pl.BlockSpec((LEN, width), lambda i, s: (0, 0))],
        ),
        out_shape=[shape_of((width, LEN), BF), shape_of((LEN, width), BF)],
        compiler_params=params(24),
        name="turn",
    )(slots, own, rest)


def ff_kernel(n_pieces, slots_ref, nm_ref, nt_ref, so_ref, sr_ref, wg_ref, wu_ref, wd_ref, *refs):
    hid_ref, dg_ref, du_ref, *grad_refs, ht_ref = refs[-10:]
    block = wg_ref.shape[1]
    own = so_ref.shape[0]
    tile = min(512, own)
    piece = block // n_pieces

    def forward(first, s_ref):
        def body(i, carry):
            here = pl.ds(pl.multiple_of(i * tile, tile), tile)
            rows = pl.ds(pl.multiple_of(first + i * tile, tile), tile)
            x = nm_ref[rows, :]
            gate = dot_nn(x, wg_ref[...])
            up = dot_nn(x, wu_ref[...])
            d_hidden = dot_nt(s_ref[here, :], wd_ref[...])
            sig = 1.0 / (1.0 + jnp.exp(-gate))
            silu = gate * sig
            hidden = (silu * up).astype(BF)
            hid_ref[rows, :] = hidden
            turned = hidden.T
            for p in range(n_pieces):
                to = pl.multiple_of(slots_ref[0, p] * piece, piece)
                ht_ref[pl.ds(to, piece), rows] = turned[p * piece : (p + 1) * piece, :]
            dg_ref[rows, :] = (d_hidden * up * (sig * (1.0 + gate * (1.0 - sig)))).astype(BF)
            du_ref[rows, :] = (d_hidden * silu).astype(BF)
            return carry

        lax.fori_loop(0, s_ref.shape[0] // tile, body, 0)

    forward(0, so_ref)
    forward(own, sr_ref)
    step = min(256, block // 2)
    for half in range(2):
        out_ref = grad_refs[half]
        for at in range(0, block // 2, step):
            rows = slice(half * block // 2 + at, half * block // 2 + at + step)
            down = dot_nn(ht_ref[rows, :own], so_ref[...]) + dot_nn(ht_ref[rows, own:], sr_ref[...])
            out_ref[at : at + step, :] = down.astype(BF)
    quarter = nt_ref.shape[0] // 4
    for at in range(4):
        left = nt_ref[at * quarter : (at + 1) * quarter, :]
        out_ref = grad_refs[2 + at]
        out_ref[:, :block] = dot_nn(left, dg_ref[...]).astype(BF)
        out_ref[:, block:] = dot_nn(left, du_ref[...]).astype(BF)


def feed_forward(index, block, n_pieces, slots, nm, nt, sg_own, sg_rest, w_gate, w_up, w_down, kept):
    width, units = w_gate.shape
    cols = pl.BlockSpec((width, block), lambda i, s: (0, index))
    kept_spec = pl.BlockSpec((LEN, block), lambda i, s: (0, index))
    grads = [(block // 2, width)] * 2 + [(width // 4, 2 * block)] * 4
    previous = list(kept) if kept is not None else []
    in_vmem = pl.BlockSpec(memory_space=pltpu.VMEM)
    return pl.pallas_call(
        functools.partial(ff_kernel, n_pieces),
        grid_spec=pltpu.PrefetchScalarGridSpec(
            num_scalar_prefetch=1,
            grid=(1,),
            in_specs=[in_vmem] * 4
            + [cols, cols, pl.BlockSpec((block, width), lambda i, s: (index, 0))]
            + [pl.BlockSpec(memory_space=pl.ANY)] * len(previous),
            out_specs=[kept_spec] * 3 + [pl.BlockSpec(dims, lambda i, s: (0, 0)) for dims in grads],
            scratch_shapes=[pltpu.VMEM((block, LEN), BF)],
        ),
        out_shape=[shape_of((LEN, units), BF)] * 3 + [shape_of(dims, BF) for dims in grads],
        input_output_aliases={8 + i: i for i in range(len(previous))},
        compiler_params=params(34),
        name="feed_forward",
    )(slots, nm, nt, sg_own, sg_rest, w_gate, w_up, w_down, *previous)


def orders_of(n_dp):
    bits = [1 << i for i in range(n_dp.bit_length() - 1)]
    if len(bits) < 4:
        return [bits] * 4
    a, b, c = bits[:3]
    return [o + bits[3:] for o in ([a, b, c], [b, a, c], [c, a, b], [c, b, a])]


def masks_of(order):
    size = 1 << len(order)
    masks = []
    for slot in range(size):
        mask = 0
        for level, bit in enumerate(order):
            if slot >> (len(order) - 1 - level) & 1:
                mask |= bit
        masks.append(mask)
    return masks


def slots_of(orders, me):
    table = []
    for order in orders:
        inverse = [0] * (1 << len(order))
        for slot, mask in enumerate(masks_of(order)):
            inverse[mask] = slot
        table.append(inverse)
    size = len(table[0])
    here = jnp.arange(size, dtype=jnp.int32) ^ me
    match = here[:, None] == jnp.arange(size, dtype=jnp.int32)[None, :]
    pieces = jnp.array([masks_of(order) for order in orders], jnp.int32) ^ me
    slots = jnp.stack([jnp.sum(jnp.where(match, jnp.array(t, jnp.int32)[None, :], 0), axis=1) for t in table])
    return (slots, pieces)


def swap_dp(values, bit, n_dp):
    return lax.ppermute(values, "dp", [(i, i ^ bit) for i in range(n_dp)])


class Part:
    def __init__(self, buffer, first, rows):
        self.buffer, self.first, self.rows = buffer, first, rows

    def value(self):
        if self.rows == self.buffer.shape[0]:
            return self.buffer
        return self.buffer[self.first : self.first + self.rows]


def phases_of(order):
    return [("halve", b) for b in order[:-1]] + [("swap", order[-1])] + [("double", b) for b in order[-2::-1]]


class Chunk:
    def __init__(self, keep, send, order, done):
        self.phases, self.done = phases_of(order), done
        self.keep, self.send = keep, send
        self.at, self.last, self.parts = 0, -9, []

    @property
    def open(self):
        return self.at < len(self.phases)

    @property
    def bit(self):
        return self.phases[self.at][1]

    def outgoing(self):
        if self.phases[self.at][0] == "double":
            return [part.value() for part in self.parts]
        return [self.send]

    def next_rows(self):
        if self.phases[self.at][0] == "double":
            return sum(part.rows for part in self.parts)
        return self.send.shape[0]

    def incoming(self, buffer, first):
        rows = self.next_rows()
        kind = self.phases[self.at][0]
        self.at += 1
        got = Part(buffer, first, rows)
        if kind == "double":
            self.parts = self.parts + [got]
            return
        total = self.keep + got.value()
        following = self.phases[self.at][0]
        if following == "halve":
            self.keep, self.send = total[: rows // 2], total[rows // 2 :]
        elif following == "swap":
            self.keep = self.send = total
        else:
            self.parts = [Part(total, 0, rows)]


def in_rounds(work, chunks, n_dp, limit):
    placing = []
    wanted = next(work)
    before = None
    now = 0

    def finish(picks, got):
        for bit, members in picks.items():
            at = 0
            for chunk in members:
                rows = chunk.next_rows()
                chunk.incoming(got[bit], at)
                at += rows
                if not chunk.open:
                    placing.append(chunk)

    while wanted is not None or before is not None or placing or any(c.open for c in chunks):
        picks, loads = {}, {}
        for chunk in chunks:
            if not chunk.open or chunk.last > now - 2:
                continue
            bit, rows = chunk.bit, chunk.next_rows()
            if loads.get(bit, 0) and loads[bit] + rows > limit:
                continue
            loads[bit] = loads.get(bit, 0) + rows
            picks.setdefault(bit, []).append(chunk)
            chunk.last = now
        sends = {}
        for bit in sorted(picks):
            picks[bit].sort(key=lambda c: -c.next_rows())
            parts = [part for chunk in picks[bit] for part in chunk.outgoing()]
            sends[bit] = parts[0] if len(parts) == 1 else jnp.concatenate(parts, axis=0)
        buffers = [c.parts[-1].buffer for c in placing]
        held = (before[1] if before else {}, sends, buffers, wanted)
        got, _, buffers, wanted = lax.optimization_barrier(held)
        taken = {bit: swap_dp(values, bit, n_dp) for bit, values in sends.items()}
        finished, placing = placing, []
        if before:
            finish(before[0], got)
        for chunk, buffer in zip(finished, buffers):
            chunk.parts[-1].buffer = buffer
            chunk.done(chunk.parts)
        if wanted is not None:
            try:
                wanted = work.send(wanted)
            except StopIteration:
                wanted = None
        before = (picks, taken) if picks else None
        now += 1


def place_kernel(slots_ref, scale_ref, which, n_pieces, folds, n_outs, counts, *refs):
    outs = refs[-n_outs:]
    piece = refs[0].shape[0] // counts[0]
    scale = scale_ref[0]
    slot = 0
    for part_ref, count in zip(refs, counts):
        for j in range(count):
            rows = part_ref[j * piece : (j + 1) * piece, :].astype(F32) * scale
            place_at = slots_ref[which, slot]
            for lane, end, out, row, col in folds:
                to = pl.multiple_of(row + place_at * piece, piece)
                outs[out][pl.ds(to, piece), col : col + end - lane] = rows[:, lane:end]
            slot += 1


def place(parts, pieces, scale, which, folds, blocks, bases):
    given = [base for base in bases if base is not None]
    n_pieces = pieces.shape[1]
    least = min(part.rows for part in parts)
    rows_all = sum(part.rows for part in parts)
    piece = rows_all // n_pieces
    counts = [part.rows // piece for part in parts]
    index_map = lambda at: (lambda i, *_: at)
    return pl.pallas_call(
        lambda s, k, *refs: place_kernel(s, k, which, n_pieces, folds, len(blocks), counts, *refs),
        grid_spec=pltpu.PrefetchScalarGridSpec(
            num_scalar_prefetch=2,
            grid=(1,),
            in_specs=[pl.BlockSpec((p.rows, 1024), index_map((p.first // p.rows, 0))) for p in parts]
            + [pl.BlockSpec(memory_space=pl.ANY)] * len(given),
            out_specs=[pl.BlockSpec(dims, index_map(at)) for _, dims, at in blocks],
        ),
        out_shape=[shape_of(full, F32) for full, _, _ in blocks],
        input_output_aliases={2 + len(parts) + i: i for i in range(len(given))},
        compiler_params=params(16),
        name="place",
    )(pieces, scale, *[part.buffer for part in parts], *given)


def late_kernel(n_pieces, slots_ref, own_ref, rest_ref, dq_ref, dk_ref, dv_ref, *refs):
    out_refs, all_ref = refs[:-1], refs[-1]
    own, width = own_ref.shape
    cols = dq_ref.shape[1]
    rows = all_ref.shape[0]
    piece = rows // n_pieces
    for which, d_ref in enumerate((dq_ref, dk_ref, dv_ref)):
        for i in range(width // rows):
            lanes = slice(i * rows, (i + 1) * rows)
            grads = dot_tn(own_ref[:, lanes], d_ref[:own, :]) + dot_tn(rest_ref[:, lanes], d_ref[own:, :])
            all_ref[:, i * cols : (i + 1) * cols] = grads.astype(BF)
        to_slots(n_pieces, slots_ref, which, piece, all_ref, out_refs[2 * which], out_refs[2 * which + 1])


def to_slots(n_pieces, pieces_ref, which, piece, all_ref, keep_ref, send_ref):
    for slot in range(n_pieces):
        at = pl.multiple_of(pieces_ref[which, slot] * piece, piece)
        out_ref = keep_ref if slot < n_pieces // 2 else send_ref
        to = slot % (n_pieces // 2) * piece
        out_ref[to : to + piece, :] = all_ref[pl.ds(at, piece), :]


def late_grads(pieces, n_pieces, own, rest, backs, at, cols):
    width = own.shape[1]
    rows = width * cols // 1024
    strip = pl.BlockSpec((LEN, cols), lambda i, s: (0, at))
    return pl.pallas_call(
        functools.partial(late_kernel, n_pieces),
        grid_spec=pltpu.PrefetchScalarGridSpec(
            num_scalar_prefetch=1,
            grid=(1,),
            in_specs=[whole_of(own), whole_of(rest)] + [strip] * 3,
            out_specs=[pl.BlockSpec((rows // 2, 1024), lambda i, s: (0, 0))] * 6,
            scratch_shapes=[pltpu.VMEM((rows, 1024), BF)],
        ),
        out_shape=[shape_of((rows // 2, 1024), BF)] * 6,
        compiler_params=params(24),
        name="late_grads",
    )(pieces, own, rest, *backs)


def out_back_kernel(n_pieces, pieces_ref, do_ref, dr_ref, co_ref, cr_ref, w_ref, dc_ref, delta_ref, keep_ref, send_ref, all_ref):
    own = do_ref.shape[0]
    at = 0
    for d_ref, c_ref in ((do_ref, co_ref), (dr_ref, cr_ref)):
        count = d_ref.shape[0]
        d_context = dot_nt(d_ref[...], w_ref[...]).astype(BF)
        dc_ref[at : at + count, :] = d_context
        both = (d_context.astype(F32) * c_ref[...].astype(F32)).T
        for head in range(both.shape[0] // HD):
            sums = jnp.sum(both[head * HD : (head + 1) * HD, :], axis=0, keepdims=True)
            delta_ref[head // 2, head % 2 : head % 2 + 1, at : at + count] = sums
        at += count
    rows = all_ref.shape[0]
    step = min(256, rows)
    for first in range(0, rows, step):
        lanes = slice(first, first + step)
        grads = dot_tn(co_ref[:, lanes], do_ref[...]) + dot_tn(cr_ref[:, lanes], dr_ref[...])
        all_ref[lanes, :] = grads.astype(BF)
    if rows % (16 * n_pieces) == 0:
        to_slots(n_pieces, pieces_ref, 3, rows // n_pieces, all_ref, keep_ref, send_ref)
    else:
        keep_ref[...] = all_ref[: rows // 2, :]
        send_ref[...] = all_ref[rows // 2 :, :]


def out_back(pieces, n_pieces, d_own, d_rest, ctx_own, ctx_rest, w_out):
    cols, width = w_out.shape
    pairs = cols // LANES
    outs = [shape_of((LEN, cols), BF), shape_of((pairs, 2, LEN), F32)] + [shape_of((cols // 2, width), BF)] * 2
    arrays = (d_own, d_rest, ctx_own, ctx_rest, w_out)
    return pl.pallas_call(
        functools.partial(out_back_kernel, n_pieces),
        grid_spec=pltpu.PrefetchScalarGridSpec(
            num_scalar_prefetch=1,
            grid=(1,),
            in_specs=[whole_of(a) for a in arrays],
            out_specs=[whole_of(o) for o in outs],
            scratch_shapes=[pltpu.VMEM((cols, width), BF)],
        ),
        out_shape=outs,
        compiler_params=params(32),
        name="out_back",
    )(pieces, *arrays)


def per_device(
    tokens,
    cotangent,
    species_ids,
    species_counts,
    norm1_gain,
    norm1_bias,
    w_query,
    w_key,
    w_value,
    w_out,
    norm2_gain,
    norm2_bias,
    w_gate,
    w_up,
    w_down,
):
    own, width = tokens.shape
    group = lax.axis_size("tensor")
    member = lax.axis_index("tensor")
    n_dp = lax.axis_size("dp")
    me = lax.axis_index("dp")
    rest = LEN - own
    units = w_gate.shape[1]
    block = min(512, units)
    head_cols = w_query.shape[1]
    pairs = head_cols // LANES
    orders = orders_of(n_dp)
    n_pieces = n_dp // 2
    slots, pieces = slots_of([order[:-1] for order in orders], me % n_pieces)

    def from_member(values, step):
        return lax.ppermute(values, "tensor", [((i + step) % group, i) for i in range(group)])

    def rest_rows(values):
        parts = [from_member(values, step) for step in range(1, group)]
        return parts[0] if group == 2 else jnp.concatenate(parts, axis=0)

    def from_others(others):
        got = []
        for step in range(1, group):
            perm = [(i, (i + step) % group) for i in range(group)]
            got.append(lax.ppermute(others[(step - 1) * own : step * own], "tensor", perm))
        return got

    picked = species_ids[:, None] == jnp.arange(SPECIES, dtype=jnp.int32)[None, :]
    count = jnp.sum(jnp.where(picked, species_counts[None, :], 0), axis=1)
    inverse = 1000.0 / count.astype(F32)[0]
    sg_own = (cotangent.astype(F32) * inverse).astype(BF)

    in_own = norm_in(tokens, norm1_gain, norm1_bias)
    in_rest = rest_rows(in_own)
    sg_rest = rest_rows(sg_own)
    cos_tab, sin_tab = rope_tables(member * own)

    query, key, value = project(in_own, in_rest, cos_tab, sin_tab, w_query, w_key, w_value)
    ctx_rest, lse_rest = attend(query, key, value, own, rest, own)
    branch_rest = dot_nn(ctx_rest, w_out).astype(BF)
    got_branch = from_others(branch_rest)
    ctx_own, lse_own = attend(query, key, value, 0, own, own)
    mixed, mid_own = norm_mid(tokens, ctx_own, w_out, norm2_gain, norm2_bias, got_branch)
    mid_rest = rest_rows(mid_own)
    mid_turned, mid = turn(mid_own, mid_rest, slots, n_pieces)

    chunks, found = [], {}
    late_cols = min(256, head_cols)
    late_fits = width * late_cols // 1024 >= 16 * n_pieces and w_out.shape[0] % (16 * n_pieces) == 0

    def send_off(keep, send, which, folds, blocks, names):
        def done(parts):
            bases = [found.get(name) for name in names]
            results = place(parts, pieces, found["scale"], which, folds, blocks, bases)
            found.update(zip(names, results))

        chunks.append(Chunk(keep, send, orders[which], done))

    def work():
        kept = None
        gate_slots = slots
        total = jnp.broadcast_to(inverse, (1, LANES))
        for index in range(units // block):
            *kept, down_keep, down_send, a_keep, a_send, b_keep, b_send = feed_forward(
                index, block, n_pieces, gate_slots, mid, mid_turned, sg_own, sg_rest, w_gate, w_up, w_down, kept
            )
            send_off(
                down_keep, down_send, 0, [(0, width, 0, 0, 0)],
                [(w_down.shape, (block, width), (index, 0))], ["down"],
            )
            for at, (keep, send) in enumerate(((a_keep, a_send), (b_keep, b_send))):
                folds = [(0, block, 0, 0, 0), (block, 2 * block, 1, 0, 0)]
                blocks = [(w.shape, (width // 2, block), (at, index)) for w in (w_gate, w_up)]
                send_off(keep, send, 1 + at, folds, blocks, ["gate", "up"])
            if index < n_dp.bit_length() - 1:
                total = total + swap_dp(total, 1 << index, n_dp)
            gate_slots, kept, total = yield (gate_slots, kept, total)
        for level in range(units // block, n_dp.bit_length() - 1):
            total = total + swap_dp(total, 1 << level, n_dp)
        scale = n_dp / total[:, :1]
        found["scale"] = scale[0]
        hidden, d_gate, d_up = kept
        d_mid_part = dot_nt(d_gate, w_gate) + dot_nt(d_up, w_up)
        d_mid_part, hidden = yield (d_mid_part, hidden)
        got = from_others(d_mid_part[own:].astype(BF))
        out_part = dot_nn(hidden, w_down)
        got, out_part = yield (got, out_part)
        got_out = from_others(out_part[own:].astype(BF))
        d_mixed, d_branch_own, sums2 = norm_backward(
            "mid", mixed, sg_own, norm2_gain, scale, d_mid_part, got
        )
        d_branch_rest = rest_rows(d_branch_own)
        lse = jnp.concatenate([lse_own, lse_rest], axis=2)
        d_branch_rest, got_out = yield (d_branch_rest, got_out)
        output = mixed + out_part[:own]
        for part in got_out:
            output = output + part.astype(F32)
        found["output"] = output.astype(BF)
        d_context, delta, out_keep, out_send = out_back(
            pieces, n_pieces, d_branch_own, d_branch_rest, ctx_own, ctx_rest, w_out
        )
        if late_fits:
            send_off(
                out_keep, out_send, 3, [(0, width, 0, 0, 0)],
                [(w_out.shape, w_out.shape, (0, 0))], ["out"],
            )
        else:
            grad = jnp.concatenate([out_keep, out_send], axis=0)
            found["out"] = lax.psum(grad, "dp").astype(F32) * scale
        backs = ()
        for at in range(head_cols // late_cols):
            d_context, backs = yield (d_context, backs)
            per = late_cols // LANES
            backs = attend_back(
                query, key, value, d_context, delta, lse, cos_tab, sin_tab, at * per, per, backs
            )
            if late_fits:
                rows = width * late_cols // 1024
                folds = [(i * late_cols, (i + 1) * late_cols, 0, i * rows, 0) for i in range(width // rows)]
                late = late_grads(pieces, n_pieces, in_own, in_rest, backs, at, late_cols)
                for which, name in enumerate(("query", "key", "value")):
                    blocks = [(w_query.shape, (width, late_cols), (0, at))]
                    send_off(late[2 * which], late[2 * which + 1], which, folds, blocks, [name])
        if not late_fits:
            for name, d in zip(("query", "key", "value"), backs):
                grad = dot_tn(in_own, d[:own]) + dot_tn(in_rest, d[own:])
                found[name] = lax.psum(grad.astype(BF), "dp").astype(F32) * scale
        (backs,) = yield (backs,)
        d_in_part = sum(dot_nt(d, w) for d, w in zip(backs, (w_query, w_key, w_value)))
        got = from_others(d_in_part[own:].astype(BF))
        (got,) = yield (got,)
        found["input"], sums1 = norm_backward("in", tokens, d_mixed, norm1_gain, scale, d_in_part, got)
        vectors = jnp.concatenate([sums1, sums2], axis=0)
        total = vectors
        for step in range(1, group):
            total = total + from_member(vectors, step)
        for level in range(n_dp.bit_length() - 1):
            (total,) = yield (total,)
            total = total + swap_dp(total, 1 << level, n_dp)
        found["vectors"] = total * scale

    in_rounds(work(), chunks, n_dp, 512)
    vectors = found["vectors"]
    return (
        found["output"],
        found["input"],
        vectors[0],
        vectors[1],
        found["query"],
        found["key"],
        found["value"],
        found["out"],
        vectors[2],
        vectors[3],
        found["gate"],
        found["up"],
        found["down"],
    )


def solution(mesh):
    split = P(("dp", "tensor"), None)
    cols = P(None, "tensor")
    rows = P("tensor", None)
    return jax.shard_map(
        per_device,
        mesh=mesh,
        in_specs=(split, split, P("dp"), P(), P(), P(), cols, cols, cols, rows, P(), P(), cols, cols, rows),
        out_specs=(split, split, P(), P(), cols, cols, cols, rows, P(), P(), cols, cols, rows),
        check_vma=False,
    )
```

time: 567 us -> 435 us (0.77)
  other arithmetic: 87.6 us -> 21.3 us
  local copies, waits for them, and re-layouts: 79.9 us -> 18.2 us
  waiting for transfers between devices: 59.9 us -> 117 us
  starting transfers between devices: 118 us -> 94.5 us
  Pallas kernels: 169 us -> 150 us
  matrix products: 40.7 us -> 22.7 us
    ppermute x86 -> x76, waiting for transfers between devices: 59.8 us -> 113 us  [swap_dp(): return lax.ppermute(values, 'dp', [(i, i ^ bit) for i in range(n_dp)])]
    add x47 -> x50, other arithmetic: 45.5 us -> 10.1 us  [the longest x46 10.1 us: incoming(): total = self.keep + got.value()]
    pallas_call x4, Pallas kernels: 70.3 us -> 41.3 us  [feed_forward(): pl.pallas_call(functools.partial(ff_kernel, n_pieces), grid_spec=pltpu.Pr...]
    slice x71 -> x45, local copies, waits for them, and re-layouts: 27.1 us -> 1.11 us  [the longest x29 0.37 us: incoming(): self.keep, self.send = (total[:rows // 2], total[rows // 2:])]
    ppermute x86 -> x76, starting transfers between devices: 117 us -> 92.6 us  [swap_dp(): return lax.ppermute(values, 'dp', [(i, i ^ bit) for i in range(n_dp)])]
    unnamed x421 -> x142, local copies, waits for them, and re-layouts: 30.8 us -> 16.4 us
    dot_general x9 -> x5, matrix products: 30.3 us -> 16.5 us  [dot_nt(): lax.dot_general(left, right, (((1,), (1,)), ((), ())), preferred_element_...]
    pallas_call x20 -> x25, Pallas kernels: 37.9 us -> 51 us  [the longest x19 35.8 us: place(): pl.pallas_call(lambda s, k, *refs: place_kernel(s, k, which, n_pieces, fo...]
  transfers between devices with their start and end apart: 95 -> 85, of which waited for: 21 -> 24; matrix products, arithmetic and copies ran while one was open for 33% -> 11% of each run, Pallas kernels for 23% -> 26%
where the time goes in v3:
time: 435 us; the launch traced here: 427 us
  Pallas kernels  150 us (34%)
  waiting for transfers between devices  117 us (27%)
  starting transfers between devices  94.5 us (22%)
  matrix products  22.7 us (5%)
  other arithmetic  21.3 us (5%)
  local copies, waits for them, and re-layouts  18.2 us (4%)
    ppermute x76, waiting for transfers between devices, swap_dp(): return lax.ppermute(values, 'dp', [(i, i ^ bit) for i in range(n_dp)])  113 us
    ppermute x76, starting transfers between devices, swap_dp(): return lax.ppermute(values, 'dp', [(i, i ^ bit) for i in range(n_dp)])  92.6 us
    pallas_call x4, Pallas kernels, feed_forward(): pl.pallas_call(functools.partial(ff_kernel, n_pieces), grid_spec=pltpu.Pr...  41.3 us
    pallas_call x19, Pallas kernels, place(): pl.pallas_call(lambda s, k, *refs: place_kernel(s, k, which, n_pieces, fo...  35.8 us
    pallas_call x2, Pallas kernels, attend_back(): pl.pallas_call(functools.partial(attend_back_kernel, tile), grid=(pairs,)...  29.8 us
    pallas_call x2, Pallas kernels, attend(): pl.pallas_call(attend_kernel, grid=(pairs, count // tile), in_specs=[pl.B...  17.8 us
    dot_general x5, matrix products, dot_nt(): lax.dot_general(left, right, (((1,), (1,)), ((), ())), preferred_element_...  16.5 us
    unnamed x142, local copies, waits for them, and re-layouts  16.4 us
  transfers between devices with their start and end apart: 85, of which 24 were waited for; matrix products, arithmetic and copies ran while one was open for 11% of the time, Pallas kernels for 26%

profile of v3, /device:TPU:0, one launch (start us, length us, event | category | flops | bytes accessed | tf_op | source)
XLA Modules:
  0.0 427.2 jit_solution(14271428222892553087)
XLA Ops:
  9.6 4.5 %project.1 = (bf16[1024,512]{1,0:T(8,128)(2,1)S(1)}, bf16[1024,512]{1,0:T(8,128)(2,1)S(1)}, bf16[1024,512]{1,0:T(8,128)(2,1)S(1)}) custom-call(bf16[512,1024]{1,0:T(8,128)(2,1)S(1)} %norm_in.1.own_ref, bf16[512,1024]{1,0:T(8,128)(2,1)S(1)} %copy-done.8, f32[1024,128]{1,0:T(8,128)S(1)} %get-tuple-element.555.cos_ref, ...), custom_call_target="tpu_custom_call" | custom-call | tf_op jit(solution)/shard_map/project/pallas_call | solution.py:97
  15.7 8.8 %attend.3 = (bf16[512,512]{1,0:T(8,128)(2,1)S(1)}, f32[4,2,512]{2,1,0:T(2,128)S(1)}) custom-call(bf16[1024,512]{1,0:T(8,128)(2,1)S(1)} %get-tuple-element.228.q_ref, bf16[1024,512]{1,0:T(8,128)(2,1)S(1)} %get-tuple-element.229.k_ref, bf16[1024,512]{1,0:T(8,128)(2,1)S(1)} %get-tuple-element.230.v_ref), custom_call_target="tpu_custom_call" | custom-call | tf_op jit(solution)/shard_map/attend/pallas_call | solution.py:132
  30.5 9.0 %attend.2 = (bf16[512,512]{1,0:T(8,128)(2,1)S(1)}, f32[4,2,512]{2,1,0:T(2,128)S(1)}) custom-call(bf16[1024,512]{1,0:T(8,128)(2,1)S(1)} %get-tuple-element.228.q_ref, bf16[1024,512]{1,0:T(8,128)(2,1)S(1)} %get-tuple-element.229.k_ref, bf16[1024,512]{1,0:T(8,128)(2,1)S(1)} %copy-done.5), custom_call_target="tpu_custom_call" | custom-call | tf_op jit(solution)/shard_map/attend/pallas_call | solution.py:132
  42.2 3.6 norm_mid.1
  48.1 2.0 collective-permute-done.2.rest_ref
  50.2 2.9 turn.1
  53.1 9.7 %feed_forward.4 = (bf16[1024,2048]{1,0:T(8,128)(2,1)S(1)}, bf16[1024,2048]{1,0:T(8,128)(2,1)S(1)}, bf16[1024,2048]{1,0:T(8,128)(2,1)}, bf16[256,1024]{1,0:T(8,12...) custom-call(s32[4,8]{1,0:T(4,128)S(1)} %pad_add_fusion.slots_ref, ...), custom_call_target="tpu_custom_call" | custom-call | tf_op jit(solution)/shard_map/feed_forward/pallas_call | solution.py:362
  62.8 2.9 collective-permute-start.4
  69.4 8.7 %collective-permute-done.7 = f32[1,128]{1,0:T(1,128)S(1)} collective-permute-done((f32[1,128]{1,0:T(1,128)S(1)}, f32[1,128]{1,0:T(1,128)S(1)}, u32[]{:S(2)}, u32[]{:S(2)}) %collective-permute-start.7) | collective-permute-done | bytes 544 | tf_op jit(solution)/shard_map/ppermute | solution.py:416
  78.0 10.7 %feed_forward.5 = (bf16[1024,2048]{1,0:T(8,128)(2,1)S(1)}, bf16[1024,2048]{1,0:T(8,128)(2,1)S(1)}, bf16[1024,2048]{1,0:T(8,128)(2,1)}, bf16[256,1024]{1,0:T(8,12...) custom-call(s32[4,8]{1,0:T(4,128)S(1)} %pad_add_fusion.slots_ref, ...), custom_call_target="tpu_custom_call", output_to_operand_aliasing={{0}: (8, {}), {1}: (9, {}), {2}: (10, {})} | custom-call | tf_op jit(solution)/shard_map/feed_forward/pallas_call | solution.py:362
  92.0 2.0 collective-permute-done.8
  94.5 10.3 %feed_forward.6 = (bf16[1024,2048]{1,0:T(8,128)(2,1)S(1)}, bf16[1024,2048]{1,0:T(8,128)(2,1)S(1)}, bf16[1024,2048]{1,0:T(8,128)(2,1)}, bf16[256,1024]{1,0:T(8,12...) custom-call(s32[4,8]{1,0:T(4,128)S(1)} %pad_add_fusion.slots_ref, ...), custom_call_target="tpu_custom_call", output_to_operand_aliasing={{0}: (8, {}), {1}: (9, {}), {2}: (10, {})} | custom-call | tf_op jit(solution)/shard_map/feed_forward/pallas_call | solution.py:362
  109.7 9.5 %collective-permute-done.15 = f32[1,128]{1,0:T(1,128)S(1)} collective-permute-done((f32[1,128]{1,0:T(1,128)S(1)}, f32[1,128]{1,0:T(1,128)S(1)}, u32[]{:S(2)}, u32[]{:S(2)}) %collective-permute-start.15) | collective-permute-done | bytes 544 | tf_op jit(solution)/shard_map/ppermute | solution.py:416
  121.3 10.5 %feed_forward.7 = (bf16[1024,2048]{1,0:T(8,128)(2,1)S(1)}, bf16[1024,2048]{1,0:T(8,128)(2,1)S(1)}, bf16[1024,2048]{1,0:T(8,128)(2,1)}, bf16[256,1024]{1,0:T(8,12...) custom-call(s32[4,8]{1,0:T(4,128)S(1)} %pad_add_fusion.slots_ref, ...), custom_call_target="tpu_custom_call", output_to_operand_aliasing={{0}: (8, {}), {1}: (9, {}), {2}: (10, {})} | custom-call | tf_op jit(solution)/shard_map/feed_forward/pallas_call | solution.py:362
  134.6 2.6 collective-permute-start.16
  146.5 6.1 %fusion.19 = f32[1024,1024]{1,0:T(8,128)} fusion(bf16[1024,2048]{1,0:T(8,128)(2,1)S(1)} %copy-done.40, bf16[1024,2048]{1,0:T(8,128)(2,1)S(1)} %copy-done.37), kind=kOutput, calls=%fused_computation.212 | convolution fusion | flops 4294967296 | bytes 12582912 | tf_op jit(solution)/shard_map/dot_general | solution.py:32
  154.5 6.6 %convolution_add_fusion.part_ref = f32[1024,1024]{1,0:T(8,128)S(1)} fusion(f32[1024,1024]{1,0:T(8,128)} %fusion.19, bf16[1024,2048]{1,0:T(8,128)(2,1)S(1)} %get-tuple-element.295, bf16[1024,2048]{1,0:T(8,128)(2,1)S(1)} %copy-done.38), kind=kOutput, calls=%fused_computation.6 | convolution fusion | flops 4296015872 | bytes 16777216 | tf_op jit(solution)/shard_map/dot_general | solution.py:32
  165.5 4.5 %fusion.20 = f32[1024,1024]{1,0:T(8,128)S(1)} fusion(bf16[1024,2048]{1,0:T(8,128)(2,1)S(1)} %get-tuple-element.304, bf16[2048,1024]{1,0:T(8,128)(2,1)S(1)} %copy-done.39), kind=kOutput, calls=%fused_computation.213 | convolution fusion | flops 4294967296 | bytes 12582912 | tf_op jit(solution)/shard_map/dot_general | solution.py:28
  184.2 2.5 collective-permute-start.31
  190.6 3.1 out_back.1
  195.1 3.0 collective-permute-done.30
  198.1 7.5 %collective-permute-done.31 = bf16[192,1024]{1,0:T(8,128)(2,1)S(1)} collective-permute-done((bf16[192,1024]{1,0:T(8,128)(2,1)S(1)}, bf16[192,1024]{1,0:T(8,128)(2,1)S(1)}, u32[]{:S(2)}, u32[]{:S(2)}) %collective-permute-start.31) | collective-permute-done | bytes 393248 | tf_op jit(solution)/shard_map/ppermute | solution.py:416
  205.7 15.0 %attend_back.2 = (bf16[1024,512]{1,0:T(8,128)(2,1)S(1)}, bf16[1024,512]{1,0:T(8,128)(2,1)S(1)}, bf16[1024,512]{1,0:T(8,128)(2,1)S(1)}) custom-call(bf16[1024,512]{1,0:T(8,128)(2,1)S(1)} %copy-done.1, bf16[1024,512]{1,0:T(8,128)(2,1)S(1)} %copy-done.3, bf16[1024,512]{1,0:T(8,128)(2,1)S(1)} %copy-done.6, bf16[1024,512]{1,0:T(8,128)(2,1)S(1)} %get-tuple-element.333.d_ref, ...), custom_call_target="tpu_custom_call" | custom-call | tf_op jit(solution)/shard_map/attend_back/pallas_call | solution.py:190
  220.7 2.6 late_grads.2
  227.0 3.3 collective-permute-start.35
  231.3 14.8 %attend_back.3 = (bf16[1024,512]{1,0:T(8,128)(2,1)S(1)}, bf16[1024,512]{1,0:T(8,128)(2,1)S(1)}, bf16[1024,512]{1,0:T(8,128)(2,1)S(1)}) custom-call(bf16[1024,512]{1,0:T(8,128)(2,1)S(1)} %copy-done.1, bf16[1024,512]{1,0:T(8,128)(2,1)S(1)} %copy-done.3, bf16[1024,512]{1,0:T(8,128)(2,1)S(1)} %copy-done.6, ...), custom_call_target="tpu_custom_call", output_to_operand_aliasing={{0}: (8, {}), {1}: (9, {}), {2}: (10, {})} | custom-call | tf_op jit(solution)/shard_map/attend_back/pallas_call | solution.py:190
  246.1 2.6 late_grads.3
  258.5 7.7 %collective-permute-done.42 = bf16[192,1024]{1,0:T(8,128)(2,1)S(1)} collective-permute-done((bf16[192,1024]{1,0:T(8,128)(2,1)S(1)}, bf16[192,1024]{1,0:T(8,128)(2,1)S(1)}, u32[]{:S(2)}, u32[]{:S(2)}) %collective-permute-start.42) | collective-permute-done | bytes 393248 | tf_op jit(solution)/shard_map/ppermute | solution.py:416
  272.5 3.2 norm_back.3
  280.6 17.3 %collective-permute-done.51 = f32[4,1024]{1,0:T(4,128)S(1)} collective-permute-done((f32[4,1024]{1,0:T(4,128)S(1)}, f32[4,1024]{1,0:T(4,128)S(1)}, u32[]{:S(2)}, u32[]{:S(2)}) %collective-permute-start.51) | collective-permute-done | bytes 16416 | tf_op jit(solution)/shard_map/ppermute | solution.py:416
  301.5 17.1 %collective-permute-done.59 = f32[4,1024]{1,0:T(4,128)S(1)} collective-permute-done((f32[4,1024]{1,0:T(4,128)S(1)}, f32[4,1024]{1,0:T(4,128)S(1)}, u32[]{:S(2)}, u32[]{:S(2)}) %collective-permute-start.59) | collective-permute-done | bytes 16416 | tf_op jit(solution)/shard_map/ppermute | solution.py:416
  320.8 2.9 collective-permute-start.55
  324.2 14.2 %collective-permute-done.60 = f32[4,1024]{1,0:T(4,128)S(1)} collective-permute-done((f32[4,1024]{1,0:T(4,128)S(1)}, f32[4,1024]{1,0:T(4,128)S(1)}, u32[]{:S(2)}, u32[]{:S(2)}) %collective-permute-start.60) | collective-permute-done | bytes 16416 | tf_op jit(solution)/shard_map/ppermute | solution.py:416
  340.1 2.5 collective-permute-start.69
  344.4 8.9 %collective-permute-done.69 = bf16[96,1024]{1,0:T(8,128)(2,1)S(1)} collective-permute-done((bf16[96,1024]{1,0:T(8,128)(2,1)S(1)}, bf16[96,1024]{1,0:T(8,128)(2,1)S(1)}, u32[]{:S(2)}, u32[]{:S(2)}) %collective-permute-start.69) | collective-permute-done | bytes 196640 | tf_op jit(solution)/shard_map/ppermute | solution.py:416
  354.9 3.8 collective-permute-start.64
  358.8 2.9 collective-permute-start.65
  361.7 2.0 place.26
  363.7 2.0 place.34.refs_4_
  365.8 2.0 place.35.refs_4_
  367.8 2.0 place.27
  369.8 2.0 place.28
  376.1 2.1 collective-permute-start.71
  382.6 2.4 collective-permute-done.70.refs_1_.refs_2_
  393.9 6.7 %collective-permute-done.76.refs_3_ = bf16[256,1024]{1,0:T(8,128)(2,1)S(1)} collective-permute-done((bf16[256,1024]{1,0:T(8,128)(2,1)S(1)}, bf16[256,1024]{1,0:T(8,128)(2,1)S(1)}, u32[]{:S(2)}, u32[]{:S(2)}) %collective-permute-start.76) | collective-permute-done | bytes 524320 | tf_op jit(solution)/shard_map/ppermute | solution.py:416
  403.2 2.0 place.36.refs_4_
  405.2 2.0 place.37
  415.3 2.0 place.25
  (478 shorter events, 145.7 us)
Async XLA Ops:
  62.8 31.2 %collective-permute-start.4 = (bf16[256,1024]{1,0:T(8,128)(2,1)S(1)}, bf16[256,1024]{1,0:T(8,128)(2,1)S(1)}, u32[]{:S(2)}, u32[]{:S(2)}) collective-permute-start(bf16[256,1024]{1,0:T(8,128)(2,1)S(1)} %get-tuple-element.237), channel_id=1, source_target_pairs={{0,2},{2,0},{4,6},{6,4},{8,10},{10,8},{12,14},{14,12},{16,18},{18,... | collective-permute-start | bytes 1572872 | tf_op jit(solution)/shard_map/ppermute | solution.py:416
  65.7 28.3 %collective-permute-start.5 = (bf16[256,1024]{1,0:T(8,128)(2,1)S(1)}, bf16[256,1024]{1,0:T(8,128)(2,1)S(1)}, u32[]{:S(2)}, u32[]{:S(2)}) collective-permute-start(bf16[256,1024]{1,0:T(8,128)(2,1)S(1)} %get-tuple-element.238), channel_id=1, source_target_pairs={{0,4},{2,6},{4,0},{6,2},{8,12},{10,14},{12,8},{14,10},{16,20},{18,... | collective-permute-start | bytes 1572872 | tf_op jit(solution)/shard_map/ppermute | solution.py:416
  67.2 26.8 %collective-permute-start.6 = (bf16[256,1024]{1,0:T(8,128)(2,1)S(1)}, bf16[256,1024]{1,0:T(8,128)(2,1)S(1)}, u32[]{:S(2)}, u32[]{:S(2)}) collective-permute-start(bf16[256,1024]{1,0:T(8,128)(2,1)S(1)} %get-tuple-element.239), channel_id=1, source_target_pairs={{0,8},{2,10},{4,12},{6,14},{8,0},{10,2},{12,4},{14,6},{16,24},{18,... | collective-permute-start | bytes 1572872 | tf_op jit(solution)/shard_map/ppermute | solution.py:416
  88.8 20.7 %collective-permute-start.12 = (bf16[256,1024]{1,0:T(8,128)(2,1)S(1)}, bf16[256,1024]{1,0:T(8,128)(2,1)S(1)}, u32[]{:S(2)}, u32[]{:S(2)}) collective-permute-start(bf16[256,1024]{1,0:T(8,128)(2,1)S(1)} %get-tuple-element.247), channel_id=1, source_target_pairs={{0,2},{2,0},{4,6},{6,4},{8,10},{10,8},{12,14},{14,12},{16,18},{18,... | collective-permute-start | bytes 1572872 | tf_op jit(solution)/shard_map/ppermute | solution.py:416
  104.9 36.9 %collective-permute-start.9 = (bf16[512,1024]{1,0:T(8,128)(2,1)S(1)}, bf16[512,1024]{1,0:T(8,128)(2,1)S(1)}, u32[]{:S(2)}, u32[]{:S(2)}) collective-permute-start(bf16[512,1024]{1,0:T(8,128)(2,1)S(1)} %pad_maximum_fusion), channel_id=1, source_target_pairs={{0,2},{2,0},{4,6},{6,4},{8,10},{10,8},{12,14},{14,12},{16,18},{18,... | collective-permute-start | bytes 3145736 | tf_op jit(solution)/shard_map/ppermute | solution.py:416
  105.3 15.6 %collective-permute-start.13 = (bf16[256,1024]{1,0:T(8,128)(2,1)S(1)}, bf16[256,1024]{1,0:T(8,128)(2,1)S(1)}, u32[]{:S(2)}, u32[]{:S(2)}) collective-permute-start(bf16[256,1024]{1,0:T(8,128)(2,1)S(1)} %get-tuple-element.248), channel_id=1, source_target_pairs={{0,4},{2,6},{4,0},{6,2},{8,12},{10,14},{12,8},{14,10},{16,20},{18,... | collective-permute-start | bytes 1572872 | tf_op jit(solution)/shard_map/ppermute | solution.py:416
  108.9 32.9 %collective-permute-start.10 = (bf16[384,1024]{1,0:T(8,128)(2,1)S(1)}, bf16[384,1024]{1,0:T(8,128)(2,1)S(1)}, u32[]{:S(2)}, u32[]{:S(2)}) collective-permute-start(bf16[384,1024]{1,0:T(8,128)(2,1)S(1)} %pad_maximum_fusion.2), channel_id=1, source_target_pairs={{0,4},{2,6},{4,0},{6,2},{8,12},{10,14},{12,8},{14,10},{16,20},{18,... | collective-permute-start | bytes 2359304 | tf_op jit(solution)/shard_map/ppermute | solution.py:416
  119.2 20.9 %collective-permute-start.11 = (bf16[256,1024]{1,0:T(8,128)(2,1)S(1)}, bf16[256,1024]{1,0:T(8,128)(2,1)S(1)}, u32[]{:S(2)}, u32[]{:S(2)}) collective-permute-start(bf16[256,1024]{1,0:T(8,128)(2,1)S(1)} %get-tuple-element.267), channel_id=1, source_target_pairs={{0,8},{2,10},{4,12},{6,14},{8,0},{10,2},{12,4},{14,6},{16,24},{18,... | collective-permute-start | bytes 1572872 | tf_op jit(solution)/shard_map/ppermute | solution.py:416
  132.9 29.4 %collective-permute-start.20 = (bf16[512,1024]{1,0:T(8,128)(2,1)}, bf16[512,1024]{1,0:T(8,128)(2,1)S(1)}, u32[]{:S(2)}, u32[]{:S(2)}) collective-permute-start(bf16[512,1024]{1,0:T(8,128)(2,1)} %pad_maximum_fusion.1), channel_id=1, source_target_pairs={{0,2},{2,0},{4,6},{6,4},{8,10},{10,8},{12,14},{14,12},{16,18},{18,... | collective-permute-start | bytes 3145736 | tf_op jit(solution)/shard_map/ppermute | solution.py:416
  139.1 23.1 %collective-permute-start.21 = (bf16[384,1024]{1,0:T(8,128)(2,1)}, bf16[384,1024]{1,0:T(8,128)(2,1)}, u32[]{:S(2)}, u32[]{:S(2)}) collective-permute-start(bf16[384,1024]{1,0:T(8,128)(2,1)} %pad_maximum_fusion.3), channel_id=1, source_target_pairs={{0,4},{2,6},{4,0},{6,2},{8,12},{10,14},{12,8},{14,10},{16,20},{18,... | collective-permute-start | bytes 2359304 | tf_op jit(solution)/shard_map/ppermute | solution.py:416
  140.2 21.1 %collective-permute-start.22 = (bf16[256,1024]{1,0:T(8,128)(2,1)S(1)}, bf16[256,1024]{1,0:T(8,128)(2,1)S(1)}, u32[]{:S(2)}, u32[]{:S(2)}) collective-permute-start(bf16[256,1024]{1,0:T(8,128)(2,1)S(1)} %get-tuple-element.284), channel_id=1, source_target_pairs={{0,8},{2,10},{4,12},{6,14},{8,0},{10,2},{12,4},{14,6},{16,24},{18,... | collective-permute-start | bytes 1572872 | tf_op jit(solution)/shard_map/ppermute | solution.py:416
  152.6 21.5 %collective-permute-start.17 = (bf16[256,1024]{1,0:T(8,128)(2,1)S(1)}, bf16[256,1024]{1,0:T(8,128)(2,1)S(1)}, u32[]{:S(2)}, u32[]{:S(2)}) collective-permute-start(bf16[256,1024]{1,0:T(8,128)(2,1)S(1)} %pad_maximum_fusion.9), channel_id=1, source_target_pairs={{0,2},{2,0},{4,6},{6,4},{8,10},{10,8},{12,14},{14,12},{16,18},{18,... | collective-permute-start | bytes 1572872 | tf_op jit(solution)/shard_map/ppermute | solution.py:416
  154.0 18.9 %collective-permute-start.18 = (bf16[192,1024]{1,0:T(8,128)(2,1)}, bf16[192,1024]{1,0:T(8,128)(2,1)S(1)}, u32[]{:S(2)}, u32[]{:S(2)}) collective-permute-start(bf16[192,1024]{1,0:T(8,128)(2,1)} %pad_maximum_fusion.21), channel_id=1, source_target_pairs={{0,4},{2,6},{4,0},{6,2},{8,12},{10,14},{12,8},{14,10},{16,20},{18,... | collective-permute-start | bytes 1179656 | tf_op jit(solution)/shard_map/ppermute | solution.py:416
  163.6 20.5 %collective-permute-start.24 = (bf16[256,1024]{1,0:T(8,128)(2,1)S(1)}, bf16[256,1024]{1,0:T(8,128)(2,1)S(1)}, u32[]{:S(2)}, u32[]{:S(2)}) collective-permute-start(bf16[256,1024]{1,0:T(8,128)(2,1)S(1)} %pad_maximum_fusion.10), channel_id=1, source_target_pairs={{0,2},{2,0},{4,6},{6,4},{8,10},{10,8},{12,14},{14,12},{16,18},{18,... | collective-permute-start | bytes 1572872 | tf_op jit(solution)/shard_map/ppermute | solution.py:416
  184.2 21.5 %collective-permute-start.31 = (bf16[192,1024]{1,0:T(8,128)(2,1)S(1)}, bf16[192,1024]{1,0:T(8,128)(2,1)S(1)}, u32[]{:S(2)}, u32[]{:S(2)}) collective-permute-start(bf16[192,1024]{1,0:T(8,128)(2,1)S(1)} %pad_maximum_fusion.23), channel_id=1, source_target_pairs={{0,16},{2,18},{4,20},{6,22},{8,24},{10,26},{12,28},{14,30},{16,0},... | collective-permute-start | bytes 1179656 | tf_op jit(solution)/shard_map/ppermute | solution.py:416
  188.6 38.3 %collective-permute-start.36 = (bf16[64,1024]{1,0:T(8,128)(2,1)S(1)}, bf16[64,1024]{1,0:T(8,128)(2,1)S(1)}, u32[]{:S(2)}, u32[]{:S(2)}) collective-permute-start(bf16[64,1024]{1,0:T(8,128)(2,1)S(1)} %slice.789), channel_id=1, source_target_pairs={{0,4},{2,6},{4,0},{6,2},{8,12},{10,14},{12,8},{14,10},{16,20},{18,... | collective-permute-start | bytes 393224 | tf_op jit(solution)/shard_map/ppermute | solution.py:416
  193.7 36.6 %collective-permute-start.37 = (bf16[384,1024]{1,0:T(8,128)(2,1)S(1)}, bf16[384,1024]{1,0:T(8,128)(2,1)S(1)}, u32[]{:S(2)}, u32[]{:S(2)}) collective-permute-start(bf16[384,1024]{1,0:T(8,128)(2,1)S(1)} %pad_maximum_fusion.4), channel_id=1, source_target_pairs={{0,8},{2,10},{4,12},{6,14},{8,0},{10,2},{12,4},{14,6},{16,24},{18,... | collective-permute-start | bytes 2359304 | tf_op jit(solution)/shard_map/ppermute | solution.py:416
  194.6 32.3 %collective-permute-start.38 = (bf16[192,1024]{1,0:T(8,128)(2,1)S(1)}, bf16[192,1024]{1,0:T(8,128)(2,1)S(1)}, u32[]{:S(2)}, u32[]{:S(2)}) collective-permute-start(bf16[192,1024]{1,0:T(8,128)(2,1)S(1)} %pad_maximum_fusion.24), channel_id=1, source_target_pairs={{0,16},{2,18},{4,20},{6,22},{8,24},{10,26},{12,28},{14,30},{16,0},... | collective-permute-start | bytes 1179656 | tf_op jit(solution)/shard_map/ppermute | solution.py:416
  223.3 27.1 %collective-permute-start.32 = (bf16[128,1024]{1,0:T(8,128)(2,1)S(1)}, bf16[128,1024]{1,0:T(8,128)(2,1)S(1)}, u32[]{:S(2)}, u32[]{:S(2)}) collective-permute-start(bf16[128,1024]{1,0:T(8,128)(2,1)S(1)} %get-tuple-element.327), channel_id=1, source_target_pairs={{0,2},{2,0},{4,6},{6,4},{8,10},{10,8},{12,14},{14,12},{16,18},{18,... | collective-permute-start | bytes 786440 | tf_op jit(solution)/shard_map/ppermute | solution.py:416
  224.7 26.0 %collective-permute-start.33 = (bf16[192,1024]{1,0:T(8,128)(2,1)S(1)}, bf16[192,1024]{1,0:T(8,128)(2,1)S(1)}, u32[]{:S(2)}, u32[]{:S(2)}) collective-permute-start(bf16[192,1024]{1,0:T(8,128)(2,1)S(1)} %pad_maximum_fusion.25), channel_id=1, source_target_pairs={{0,4},{2,6},{4,0},{6,2},{8,12},{10,14},{12,8},{14,10},{16,20},{18,... | collective-permute-start | bytes 1179656 | tf_op jit(solution)/shard_map/ppermute | solution.py:416
  226.9 25.3 %collective-permute-start.34 = (bf16[256,1024]{1,0:T(8,128)(2,1)S(1)}, bf16[256,1024]{1,0:T(8,128)(2,1)S(1)}, u32[]{:S(2)}, u32[]{:S(2)}) collective-permute-start(bf16[256,1024]{1,0:T(8,128)(2,1)S(1)} %pad_maximum_fusion.11), channel_id=1, source_target_pairs={{0,8},{2,10},{4,12},{6,14},{8,0},{10,2},{12,4},{14,6},{16,24},{18,... | collective-permute-start | bytes 1572872 | tf_op jit(solution)/shard_map/ppermute | solution.py:416
  227.0 23.8 %collective-permute-start.35 = (bf16[192,1024]{1,0:T(8,128)(2,1)S(1)}, bf16[192,1024]{1,0:T(8,128)(2,1)S(1)}, u32[]{:S(2)}, u32[]{:S(2)}) collective-permute-start(bf16[192,1024]{1,0:T(8,128)(2,1)S(1)} %pad_maximum_fusion.26), channel_id=1, source_target_pairs={{0,16},{2,18},{4,20},{6,22},{8,24},{10,26},{12,28},{14,30},{16,0},... | collective-permute-start | bytes 1179656 | tf_op jit(solution)/shard_map/ppermute | solution.py:416
  250.4 19.6 %collective-permute-start.40 = (bf16[320,1024]{1,0:T(8,128)(2,1)S(1)}, bf16[320,1024]{1,0:T(8,128)(2,1)S(1)}, u32[]{:S(2)}, u32[]{:S(2)}) collective-permute-start(bf16[320,1024]{1,0:T(8,128)(2,1)S(1)} %pad_maximum_fusion.5), channel_id=1, source_target_pairs={{0,4},{2,6},{4,0},{6,2},{8,12},{10,14},{12,8},{14,10},{16,20},{18,... | collective-permute-start | bytes 1966088 | tf_op jit(solution)/shard_map/ppermute | solution.py:416
  250.7 17.5 %collective-permute-start.41 = (bf16[256,1024]{1,0:T(8,128)(2,1)S(1)}, bf16[256,1024]{1,0:T(8,128)(2,1)S(1)}, u32[]{:S(2)}, u32[]{:S(2)}) collective-permute-start(bf16[256,1024]{1,0:T(8,128)(2,1)S(1)} %pad_maximum_fusion.12), channel_id=1, source_target_pairs={{0,8},{2,10},{4,12},{6,14},{8,0},{10,2},{12,4},{14,6},{16,24},{18,... | collective-permute-start | bytes 1572872 | tf_op jit(solution)/shard_map/ppermute | solution.py:416
  257.5 20.7 %collective-permute-start.47 = (bf16[384,1024]{1,0:T(8,128)(2,1)S(1)}, bf16[384,1024]{1,0:T(8,128)(2,1)S(1)}, u32[]{:S(2)}, u32[]{:S(2)}) collective-permute-start(bf16[384,1024]{1,0:T(8,128)(2,1)S(1)} %slice_dynamic-update-slice_fusion.9), channel_id=1, source_target_pairs={{0,2},{2,0},{4,6},{6,4},{8,10},{10,8},{12,14},{14,12},{16,18},{18,... | collective-permute-start | bytes 2359304 | tf_op jit(solution)/shard_map/ppermute | solution.py:416
  270.9 29.4 %collective-permute-start.44 = (bf16[448,1024]{1,0:T(8,128)(2,1)S(1)}, bf16[448,1024]{1,0:T(8,128)(2,1)S(1)}, u32[]{:S(2)}, u32[]{:S(2)}) collective-permute-start(bf16[448,1024]{1,0:T(8,128)(2,1)S(1)} %slice_dynamic-update-slice_fusion.6), channel_id=1, source_target_pairs={{0,2},{2,0},{4,6},{6,4},{8,10},{10,8},{12,14},{14,12},{16,18},{18,... | collective-permute-start | bytes 2752520 | tf_op jit(solution)/shard_map/ppermute | solution.py:416
  277.1 23.2 %collective-permute-start.45 = (bf16[256,1024]{1,0:T(8,128)(2,1)S(1)}, bf16[256,1024]{1,0:T(8,128)(2,1)S(1)}, u32[]{:S(2)}, u32[]{:S(2)}) collective-permute-start(bf16[256,1024]{1,0:T(8,128)(2,1)S(1)} %pad_maximum_fusion.14), channel_id=1, source_target_pairs={{0,4},{2,6},{4,0},{6,2},{8,12},{10,14},{12,8},{14,10},{16,20},{18,... | collective-permute-start | bytes 1572872 | tf_op jit(solution)/shard_map/ppermute | solution.py:416
  278.1 21.7 %collective-permute-start.46 = (bf16[128,1024]{1,0:T(8,128)(2,1)S(1)}, bf16[128,1024]{1,0:T(8,128)(2,1)S(1)}, u32[]{:S(2)}, u32[]{:S(2)}) collective-permute-start(bf16[128,1024]{1,0:T(8,128)(2,1)S(1)} %pad_maximum_fusion.33), channel_id=1, source_target_pairs={{0,8},{2,10},{4,12},{6,14},{8,0},{10,2},{12,4},{14,6},{16,24},{18,... | collective-permute-start | bytes 786440 | tf_op jit(solution)/shard_map/ppermute | solution.py:416
  278.4 19.5 %collective-permute-start.51 = (f32[4,1024]{1,0:T(4,128)S(1)}, f32[4,1024]{1,0:T(4,128)S(1)}, u32[]{:S(2)}, u32[]{:S(2)}) collective-permute-start(f32[4,1024]{1,0:T(4,128)S(1)} %fusion.7), channel_id=1, source_target_pairs={{0,2},{2,0},{4,6},{6,4},{8,10},{10,8},{12,14},{14,12},{16,18},{18,... | collective-permute-start | bytes 49160 | tf_op jit(solution)/shard_map/ppermute | solution.py:416
  279.3 44.5 %collective-permute-start.56 = (bf16[512,1024]{1,0:T(8,128)(2,1)S(1)}, bf16[512,1024]{1,0:T(8,128)(2,1)S(1)}, u32[]{:S(2)}, u32[]{:S(2)}) collective-permute-start(bf16[512,1024]{1,0:T(8,128)(2,1)S(1)} %get-tuple-element.490), channel_id=1, source_target_pairs={{0,2},{2,0},{4,6},{6,4},{8,10},{10,8},{12,14},{14,12},{16,18},{18,... | collective-permute-start | bytes 3145736 | tf_op jit(solution)/shard_map/ppermute | solution.py:416
  297.9 22.9 %collective-permute-start.57 = (bf16[416,1024]{1,0:T(8,128)(2,1)S(1)}, bf16[416,1024]{1,0:T(8,128)(2,1)S(1)}, u32[]{:S(2)}, u32[]{:S(2)}) collective-permute-start(bf16[416,1024]{1,0:T(8,128)(2,1)S(1)} %constant_dynamic-update-slice_fusion.12), channel_id=1, source_target_pairs={{0,4},{2,6},{4,0},{6,2},{8,12},{10,14},{12,8},{14,10},{16,20},{18,... | collective-permute-start | bytes 2555912 | tf_op jit(solution)/shard_map/ppermute | solution.py:416
  299.8 20.5 %collective-permute-start.58 = (bf16[320,1024]{1,0:T(8,128)(2,1)S(1)}, bf16[320,1024]{1,0:T(8,128)(2,1)S(1)}, u32[]{:S(2)}, u32[]{:S(2)}) collective-permute-start(bf16[320,1024]{1,0:T(8,128)(2,1)S(1)} %constant_dynamic-update-slice_fusion.16), channel_id=1, source_target_pairs={{0,8},{2,10},{4,12},{6,14},{8,0},{10,2},{12,4},{14,6},{16,24},{18,... | collective-permute-start | bytes 1966088 | tf_op jit(solution)/shard_map/ppermute | solution.py:416
  300.6 42.3 %collective-permute-start.52 = (bf16[512,1024]{1,0:T(8,128)(2,1)S(1)}, bf16[512,1024]{1,0:T(8,128)(2,1)S(1)}, u32[]{:S(2)}, u32[]{:S(2)}) collective-permute-start(bf16[512,1024]{1,0:T(8,128)(2,1)S(1)} %get-tuple-element.487), channel_id=1, source_target_pairs={{0,2},{2,0},{4,6},{6,4},{8,10},{10,8},{12,14},{14,12},{16,18},{18,... | collective-permute-start | bytes 3145736 | tf_op jit(solution)/shard_map/ppermute | solution.py:416
  301.2 17.5 %collective-permute-start.59 = (f32[4,1024]{1,0:T(4,128)S(1)}, f32[4,1024]{1,0:T(4,128)S(1)}, u32[]{:S(2)}, u32[]{:S(2)}) collective-permute-start(f32[4,1024]{1,0:T(4,128)S(1)} %add.367), channel_id=1, source_target_pairs={{0,4},{2,6},{4,0},{6,2},{8,12},{10,14},{12,8},{14,10},{16,20},{18,... | collective-permute-start | bytes 49160 | tf_op jit(solution)/shard_map/ppermute | solution.py:416
  318.6 21.4 %collective-permute-start.53 = (bf16[416,1024]{1,0:T(8,128)(2,1)S(1)}, bf16[416,1024]{1,0:T(8,128)(2,1)S(1)}, u32[]{:S(2)}, u32[]{:S(2)}) collective-permute-start(bf16[416,1024]{1,0:T(8,128)(2,1)S(1)} %constant_dynamic-update-slice_fusion.25), channel_id=1, source_target_pairs={{0,4},{2,6},{4,0},{6,2},{8,12},{10,14},{12,8},{14,10},{16,20},{18,... | collective-permute-start | bytes 2555912 | tf_op jit(solution)/shard_map/ppermute | solution.py:416
  320.4 19.1 %collective-permute-start.54 = (bf16[320,1024]{1,0:T(8,128)(2,1)S(1)}, bf16[320,1024]{1,0:T(8,128)(2,1)S(1)}, u32[]{:S(2)}, u32[]{:S(2)}) collective-permute-start(bf16[320,1024]{1,0:T(8,128)(2,1)S(1)} %constant_dynamic-update-slice_fusion.29), channel_id=1, source_target_pairs={{0,8},{2,10},{4,12},{6,14},{8,0},{10,2},{12,4},{14,6},{16,24},{18,... | collective-permute-start | bytes 1966088 | tf_op jit(solution)/shard_map/ppermute | solution.py:416
  320.8 18.0 %collective-permute-start.55 = (bf16[64,1024]{1,0:T(8,128)(2,1)S(1)}, bf16[64,1024]{1,0:T(8,128)(2,1)S(1)}, u32[]{:S(2)}, u32[]{:S(2)}) collective-permute-start(bf16[64,1024]{1,0:T(8,128)(2,1)S(1)} %get-tuple-element.467), channel_id=1, source_target_pairs={{0,16},{2,18},{4,20},{6,22},{8,24},{10,26},{12,28},{14,30},{16,0},... | collective-permute-start | bytes 393224 | tf_op jit(solution)/shard_map/ppermute | solution.py:416
  338.4 16.5 %collective-permute-start.66 = (bf16[256,1024]{1,0:T(8,128)(2,1)S(1)}, bf16[256,1024]{1,0:T(8,128)(2,1)S(1)}, u32[]{:S(2)}, u32[]{:S(2)}) collective-permute-start(bf16[256,1024]{1,0:T(8,128)(2,1)S(1)} %pad_maximum_fusion.15), channel_id=1, source_target_pairs={{0,2},{2,0},{4,6},{6,4},{8,10},{10,8},{12,14},{14,12},{16,18},{18,... | collective-permute-start | bytes 1572872 | tf_op jit(solution)/shard_map/ppermute | solution.py:416
  338.9 19.8 %collective-permute-start.67 = (bf16[256,1024]{1,0:T(8,128)(2,1)S(1)}, bf16[256,1024]{1,0:T(8,128)(2,1)S(1)}, u32[]{:S(2)}, u32[]{:S(2)}) collective-permute-start(bf16[256,1024]{1,0:T(8,128)(2,1)S(1)} %pad_maximum_fusion.16), channel_id=1, source_target_pairs={{0,4},{2,6},{4,0},{6,2},{8,12},{10,14},{12,8},{14,10},{16,20},{18,... | collective-permute-start | bytes 1572872 | tf_op jit(solution)/shard_map/ppermute | solution.py:416
  339.4 19.4 %collective-permute-start.68 = (bf16[256,1024]{1,0:T(8,128)(2,1)S(1)}, bf16[256,1024]{1,0:T(8,128)(2,1)S(1)}, u32[]{:S(2)}, u32[]{:S(2)}) collective-permute-start(bf16[256,1024]{1,0:T(8,128)(2,1)S(1)} %pad_maximum_fusion.17), channel_id=1, source_target_pairs={{0,8},{2,10},{4,12},{6,14},{8,0},{10,2},{12,4},{14,6},{16,24},{18,... | collective-permute-start | bytes 1572872 | tf_op jit(solution)/shard_map/ppermute | solution.py:416
  343.0 32.3 %collective-permute-start.62 = (bf16[320,1024]{1,0:T(8,128)(2,1)S(1)}, bf16[320,1024]{1,0:T(8,128)(2,1)S(1)}, u32[]{:S(2)}, u32[]{:S(2)}) collective-permute-start(bf16[320,1024]{1,0:T(8,128)(2,1)S(1)} %pad_maximum_fusion.6), channel_id=1, source_target_pairs={{0,2},{2,0},{4,6},{6,4},{8,10},{10,8},{12,14},{14,12},{16,18},{18,... | collective-permute-start | bytes 1966088 | tf_op jit(solution)/shard_map/ppermute | solution.py:416
  353.3 21.0 %collective-permute-start.63 = (bf16[256,1024]{1,0:T(8,128)(2,1)S(1)}, bf16[256,1024]{1,0:T(8,128)(2,1)S(1)}, u32[]{:S(2)}, u32[]{:S(2)}) collective-permute-start(bf16[256,1024]{1,0:T(8,128)(2,1)S(1)} %pad_maximum_fusion.18), channel_id=1, source_target_pairs={{0,4},{2,6},{4,0},{6,2},{8,12},{10,14},{12,8},{14,10},{16,20},{18,... | collective-permute-start | bytes 1572872 | tf_op jit(solution)/shard_map/ppermute | solution.py:416
  354.9 20.4 %collective-permute-start.64 = (bf16[256,1024]{1,0:T(8,128)(2,1)S(1)}, bf16[256,1024]{1,0:T(8,128)(2,1)S(1)}, u32[]{:S(2)}, u32[]{:S(2)}) collective-permute-start(bf16[256,1024]{1,0:T(8,128)(2,1)S(1)} %pad_maximum_fusion.19), channel_id=1, source_target_pairs={{0,8},{2,10},{4,12},{6,14},{8,0},{10,2},{12,4},{14,6},{16,24},{18,... | collective-permute-start | bytes 1572872 | tf_op jit(solution)/shard_map/ppermute | solution.py:416
  358.7 42.1 %collective-permute-start.61 = (f32[4,1024]{1,0:T(4,128)S(1)}, f32[4,1024]{1,0:T(4,128)S(1)}, u32[]{:S(2)}, u32[]{:S(2)}) collective-permute-start(f32[4,1024]{1,0:T(4,128)S(1)} %add.376), channel_id=1, source_target_pairs={{0,16},{2,18},{4,20},{6,22},{8,24},{10,26},{12,28},{14,30},{16,0},... | collective-permute-start | bytes 49160 | tf_op jit(solution)/shard_map/ppermute | solution.py:416
  391.1 24.2 %collective-permute-start.83 = (bf16[128,1024]{1,0:T(8,128)(2,1)S(1)}, bf16[128,1024]{1,0:T(8,128)(2,1)S(1)}, u32[]{:S(2)}, u32[]{:S(2)}) collective-permute-start(bf16[128,1024]{1,0:T(8,128)(2,1)S(1)} %pad_maximum_fusion.39), channel_id=1, source_target_pairs={{0,4},{2,6},{4,0},{6,2},{8,12},{10,14},{12,8},{14,10},{16,20},{18,... | collective-permute-start | bytes 786440 | tf_op jit(solution)/shard_map/ppermute | solution.py:416
  392.7 22.6 %collective-permute-start.84 = (bf16[128,1024]{1,0:T(8,128)(2,1)S(1)}, bf16[128,1024]{1,0:T(8,128)(2,1)S(1)}, u32[]{:S(2)}, u32[]{:S(2)}) collective-permute-start(bf16[128,1024]{1,0:T(8,128)(2,1)S(1)} %pad_maximum_fusion.40), channel_id=1, source_target_pairs={{0,8},{2,10},{4,12},{6,14},{8,0},{10,2},{12,4},{14,6},{16,24},{18,... | collective-permute-start | bytes 786440 | tf_op jit(solution)/shard_map/ppermute | solution.py:416
  400.6 16.7 %collective-permute-start.79 = (bf16[128,1024]{1,0:T(8,128)(2,1)S(1)}, bf16[128,1024]{1,0:T(8,128)(2,1)S(1)}, u32[]{:S(2)}, u32[]{:S(2)}) collective-permute-start(bf16[128,1024]{1,0:T(8,128)(2,1)S(1)} %pad_maximum_fusion.41), channel_id=1, source_target_pairs={{0,2},{2,0},{4,6},{6,4},{8,10},{10,8},{12,14},{14,12},{16,18},{18,... | collective-permute-start | bytes 786440 | tf_op jit(solution)/shard_map/ppermute | solution.py:416
  400.8 16.5 %collective-permute-start.80 = (bf16[128,1024]{1,0:T(8,128)(2,1)S(1)}, bf16[128,1024]{1,0:T(8,128)(2,1)S(1)}, u32[]{:S(2)}, u32[]{:S(2)}) collective-permute-start(bf16[128,1024]{1,0:T(8,128)(2,1)S(1)} %pad_maximum_fusion.42), channel_id=1, source_target_pairs={{0,4},{2,6},{4,0},{6,2},{8,12},{10,14},{12,8},{14,10},{16,20},{18,... | collective-permute-start | bytes 786440 | tf_op jit(solution)/shard_map/ppermute | solution.py:416
  (98 other events, 913.0 us)

commit v4 on v3

--- a/solution.py
+++ b/solution.py
@@ -18,6 +18,13 @@
 F32 = jnp.float32
 EXP_SCALE = HD ** (-0.5) * math.log2(math.e)
 MIB = 1024 * 1024
+WIDE_ORDERS = (2, 4)
+DOWN_ORDERS = (0, 0, 0, 0)
+OUT_ORDER = 2
+LATE_ORDERS = ((0, 2, 4), (0, 2, 4))
+EARLY = (0, 0, 0, 0, 0, 0, 1, 0, 0, 1, 0, 0, 0, 0, 0, 0, 0, 0, 0, 0, 0, 0, 0, 1, 0, 1, 1, 0, 0, 0)
+LIMITS = (256, 640, 768, 320, 64, 256, 128, 192, 512, 384, 320, 320, 320, 512, 384, 320, 448, 512, 768, 448, 448, 384, 512, 384, 320, 64, 192, 768, 768, 320)
+RANKS = (1, 3, 1, 0, 1, 0, 2, 2, 2, 2, 2, 3, 1, 1, 3, 3, 1, 1, 3, 0, 0, 3, 3, 3, 1, 3, 1, 3, 3, 2)
 
 
 def shape_of(dims, dtype):
@@ -280,8 +287,7 @@
         turned = x_ref[...].T
         half = turned.shape[0] // 2
         piece = half // n_pieces
-        for which in (1, 2):
-            first = (which - 1) * half
+        for first, which in zip((0, half), WIDE_ORDERS):
             for p in range(n_pieces):
                 to = pl.multiple_of(first + slots_ref[which, p] * piece, piece)
                 turned_ref[pl.ds(to, piece), at : at + count] = turned[
@@ -306,7 +312,7 @@
     )(slots, own, rest)
 
 
-def ff_kernel(n_pieces, slots_ref, nm_ref, nt_ref, so_ref, sr_ref, wg_ref, wu_ref, wd_ref, *refs):
+def ff_kernel(n_pieces, down_order, slots_ref, nm_ref, nt_ref, so_ref, sr_ref, wg_ref, wu_ref, wd_ref, *refs):
     hid_ref, dg_ref, du_ref, *grad_refs, ht_ref = refs[-10:]
     block = wg_ref.shape[1]
     own = so_ref.shape[0]
@@ -327,7 +333,7 @@
             hid_ref[rows, :] = hidden
             turned = hidden.T
             for p in range(n_pieces):
-                to = pl.multiple_of(slots_ref[0, p] * piece, piece)
+                to = pl.multiple_of(slots_ref[down_order, p] * piece, piece)
                 ht_ref[pl.ds(to, piece), rows] = turned[p * piece : (p + 1) * piece, :]
             dg_ref[rows, :] = (d_hidden * up * (sig * (1.0 + gate * (1.0 - sig)))).astype(BF)
             du_ref[rows, :] = (d_hidden * silu).astype(BF)
@@ -352,7 +358,46 @@
         out_ref[:, block:] = dot_nn(left, du_ref[...]).astype(BF)
 
 
-def feed_forward(index, block, n_pieces, slots, nm, nt, sg_own, sg_rest, w_gate, w_up, w_down, kept):
+def d_mid_kernel(dg_ref, du_ref, wg_ref, wu_ref, own_ref, rest_ref, sum_ref):
+    step = pl.program_id(0)
+    own = own_ref.shape[0]
+    tile = min(512, own)
+    for at in range(0, LEN, tile):
+        rows = slice(at, at + tile)
+        part = dot_nt(dg_ref[rows, :], wg_ref[...]) + dot_nt(du_ref[rows, :], wu_ref[...])
+
+        @pl.when(step == 0)
+        def _():
+            sum_ref[rows, :] = part
+
+        @pl.when(step > 0)
+        def _():
+            sum_ref[rows, :] += part
+
+    @pl.when(step == pl.num_programs(0) - 1)
+    def _():
+        own_ref[...] = sum_ref[:own, :]
+        rest_ref[...] = sum_ref[own:, :].astype(BF)
+
+
+def d_mid_parts(d_gate, d_up, w_gate, w_up, own):
+    width, units = w_gate.shape
+    block = min(512, units)
+    d_spec = pl.BlockSpec((LEN, block), lambda i: (0, i))
+    w_spec = pl.BlockSpec((width, block), lambda i: (0, i))
+    return pl.pallas_call(
+        d_mid_kernel,
+        grid=(units // block,),
+        in_specs=[d_spec, d_spec, w_spec, w_spec],
+        out_specs=[pl.BlockSpec((own, width), lambda i: (0, 0)), pl.BlockSpec((LEN - own, width), lambda i: (0, 0))],
+        out_shape=[shape_of((own, width), F32), shape_of((LEN - own, width), BF)],
+        scratch_shapes=[pltpu.VMEM((LEN, width), F32)],
+        compiler_params=params(30),
+        name="d_mid",
+    )(d_gate, d_up, w_gate, w_up)
+
+
+def feed_forward(index, block, n_pieces, down_order, slots, nm, nt, sg_own, sg_rest, w_gate, w_up, w_down, kept):
     width, units = w_gate.shape
     cols = pl.BlockSpec((width, block), lambda i, s: (0, index))
     kept_spec = pl.BlockSpec((LEN, block), lambda i, s: (0, index))
@@ -360,7 +405,7 @@
     previous = list(kept) if kept is not None else []
     in_vmem = pl.BlockSpec(memory_space=pltpu.VMEM)
     return pl.pallas_call(
-        functools.partial(ff_kernel, n_pieces),
+        functools.partial(ff_kernel, n_pieces, down_order),
         grid_spec=pltpu.PrefetchScalarGridSpec(
             num_scalar_prefetch=1,
             grid=(1,),
@@ -380,9 +425,9 @@
 def orders_of(n_dp):
     bits = [1 << i for i in range(n_dp.bit_length() - 1)]
     if len(bits) < 4:
-        return [bits] * 4
-    a, b, c = bits[:3]
-    return [o + bits[3:] for o in ([a, b, c], [b, a, c], [c, a, b], [c, b, a])]
+        return [bits] * 6
+    x, y, z = bits[:3]
+    return [o + bits[3:] for o in ([x, y, z], [x, z, y], [y, x, z], [y, z, x], [z, x, y], [z, y, x])]
 
 
 def masks_of(order):
@@ -431,14 +476,18 @@
 
 
 class Chunk:
-    def __init__(self, keep, send, order, done):
-        self.phases, self.done = phases_of(order), done
+    def __init__(self, keep, send, order, target):
+        self.phases, self.target = phases_of(order), target
         self.keep, self.send = keep, send
-        self.at, self.last, self.parts = 0, -9, []
+        self.at, self.parts = 0, []
 
     @property
     def open(self):
         return self.at < len(self.phases)
+
+    @property
+    def left(self):
+        return len(self.phases) - self.at
 
     @property
     def bit(self):
@@ -472,11 +521,11 @@
             self.parts = [Part(total, 0, rows)]
 
 
-def in_rounds(work, chunks, n_dp, limit):
-    placing = []
+def in_rounds(work, chunks, n_dp, found, place):
+    placing, recent = [], set()
     wanted = next(work)
-    before = None
-    now = 0
+    before = ({}, {})
+    now = 1
 
     def finish(picks, got):
         for bit, members in picks.items():
@@ -488,81 +537,121 @@
                 if not chunk.open:
                     placing.append(chunk)
 
-    while wanted is not None or before is not None or placing or any(c.open for c in chunks):
+    while wanted is not None or before[0] or placing or any(c.open for c in chunks):
+        early, limit, rank = (row[min(now, len(row) - 1)] for row in (EARLY, LIMITS, RANKS))
+        if early and before[0]:
+            got, wanted = lax.optimization_barrier((before[1], wanted))
+            finish(before[0], got)
+            before = ({}, {})
         picks, loads = {}, {}
-        for chunk in chunks:
-            if not chunk.open or chunk.last > now - 2:
-                continue
+        busy = [chunk for members in before[0].values() for chunk in members]
+        free = [chunk for chunk in chunks if chunk.open and chunk not in busy]
+        free.sort(key=lambda c: (0, -c.left, -c.next_rows(), c.next_rows())[rank])
+        for chunk in free:
             bit, rows = chunk.bit, chunk.next_rows()
             if loads.get(bit, 0) and loads[bit] + rows > limit:
                 continue
             loads[bit] = loads.get(bit, 0) + rows
             picks.setdefault(bit, []).append(chunk)
-            chunk.last = now
         sends = {}
         for bit in sorted(picks):
             picks[bit].sort(key=lambda c: -c.next_rows())
             parts = [part for chunk in picks[bit] for part in chunk.outgoing()]
             sends[bit] = parts[0] if len(parts) == 1 else jnp.concatenate(parts, axis=0)
         buffers = [c.parts[-1].buffer for c in placing]
-        held = (before[1] if before else {}, sends, buffers, wanted)
-        got, _, buffers, wanted = lax.optimization_barrier(held)
+        placed = {name: found[name] for name in recent}
+        held = (before[1], sends, buffers, placed, wanted)
+        got, _, buffers, placed, wanted = lax.optimization_barrier(held)
+        found.update(placed)
+        recent = set()
         taken = {bit: swap_dp(values, bit, n_dp) for bit, values in sends.items()}
         finished, placing = placing, []
-        if before:
-            finish(before[0], got)
+        finish(before[0], got)
         for chunk, buffer in zip(finished, buffers):
             chunk.parts[-1].buffer = buffer
-            chunk.done(chunk.parts)
+        while finished:
+            recent.update(place(finished[:4]))
+            finished = finished[4:]
         if wanted is not None:
             try:
                 wanted = work.send(wanted)
             except StopIteration:
                 wanted = None
-        before = (picks, taken) if picks else None
+        before = (picks, taken)
         now += 1
 
 
-def place_kernel(slots_ref, scale_ref, which, n_pieces, folds, n_outs, counts, *refs):
-    outs = refs[-n_outs:]
-    piece = refs[0].shape[0] // counts[0]
+def place_kernel(plans, n_outs, n_given, slots_ref, scale_ref, *refs):
+    outs, wide_ref, sems = refs[-n_outs - 2 : -2], refs[-2], refs[-1]
     scale = scale_ref[0]
-    slot = 0
-    for part_ref, count in zip(refs, counts):
-        for j in range(count):
-            rows = part_ref[j * piece : (j + 1) * piece, :].astype(F32) * scale
-            place_at = slots_ref[which, slot]
-            for lane, end, out, row, col in folds:
-                to = pl.multiple_of(row + place_at * piece, piece)
-                outs[out][pl.ds(to, piece), col : col + end - lane] = rows[:, lane:end]
-            slot += 1
-
-
-def place(parts, pieces, scale, which, folds, blocks, bases):
-    given = [base for base in bases if base is not None]
+    copies = []
+    at_ref = done_rows = 0
+    for which, counts, folds in plans:
+        slot = 0
+        for count in counts:
+            part_ref = refs[at_ref]
+            at_ref += 1
+            piece = part_ref.shape[0] // count
+            for j in range(count):
+                here = slice(done_rows, done_rows + piece)
+                done_rows += piece
+                wide_ref[here, :] = part_ref[j * piece : (j + 1) * piece, :].astype(F32) * scale
+                place_at = slots_ref[which, slot]
+                for lane, end, out, row, col in folds:
+                    to = pl.multiple_of(row + place_at * piece, piece)
+                    copy = pltpu.make_async_copy(
+                        wide_ref.at[here, lane:end],
+                        outs[out].at[pl.ds(to, piece), col : col + end - lane],
+                        sems.at[len(copies)],
+                    )
+                    copy.start()
+                    copies.append(copy)
+                slot += 1
+    for copy in copies:
+        copy.wait()
+
+
+def place(chunks, pieces, scale, found):
+    names, plans, parts = {}, [], []
     n_pieces = pieces.shape[1]
-    least = min(part.rows for part in parts)
+    for chunk in chunks:
+        which, folds, shapes = chunk.target
+        for name, dims in shapes:
+            names.setdefault(name, dims)
+        order = list(names)
+        mine = [order.index(name) for name, _ in shapes]
+        piece = sum(part.rows for part in chunk.parts) // n_pieces
+        counts = tuple(part.rows // piece for part in chunk.parts)
+        plans.append((which, counts, tuple((l, e, mine[o], r, c) for l, e, o, r, c in folds)))
+        parts += chunk.parts
+    given = [name for name in names if name in found]
+    at = {name: i for i, name in enumerate(names)}
+    index_map = lambda block: (lambda i, *_: block)
+    anywhere = pl.BlockSpec(memory_space=pl.ANY)
     rows_all = sum(part.rows for part in parts)
-    piece = rows_all // n_pieces
-    counts = [part.rows // piece for part in parts]
-    index_map = lambda at: (lambda i, *_: at)
-    return pl.pallas_call(
-        lambda s, k, *refs: place_kernel(s, k, which, n_pieces, folds, len(blocks), counts, *refs),
+    results = pl.pallas_call(
+        lambda s, k, *refs: place_kernel(plans, len(names), len(given), s, k, *refs),
         grid_spec=pltpu.PrefetchScalarGridSpec(
             num_scalar_prefetch=2,
             grid=(1,),
             in_specs=[pl.BlockSpec((p.rows, 1024), index_map((p.first // p.rows, 0))) for p in parts]
-            + [pl.BlockSpec(memory_space=pl.ANY)] * len(given),
-            out_specs=[pl.BlockSpec(dims, index_map(at)) for _, dims, at in blocks],
+            + [anywhere] * len(given),
+            out_specs=[anywhere] * len(names),
+            scratch_shapes=[
+                pltpu.VMEM((rows_all, 1024), F32),
+                pltpu.SemaphoreType.DMA((n_pieces * sum(len(plan[2]) for plan in plans),)),
+            ],
         ),
-        out_shape=[shape_of(full, F32) for full, _, _ in blocks],
-        input_output_aliases={2 + len(parts) + i: i for i in range(len(given))},
-        compiler_params=params(16),
+        out_shape=[shape_of(dims, F32) for dims in names.values()],
+        input_output_aliases={2 + len(parts) + i: at[name] for i, name in enumerate(given)},
+        compiler_params=params(4 + 8 * rows_all * 1024 // MIB),
         name="place",
-    )(pieces, scale, *[part.buffer for part in parts], *given)
-
-
-def late_kernel(n_pieces, slots_ref, own_ref, rest_ref, dq_ref, dk_ref, dv_ref, *refs):
+    )(pieces, scale, *[part.buffer for part in parts], *[found[name] for name in given])
+    found.update(zip(names, results))
+    return list(names)
+
+
+def late_kernel(n_pieces, table, slots_ref, own_ref, rest_ref, dq_ref, dk_ref, dv_ref, *refs):
     out_refs, all_ref = refs[:-1], refs[-1]
     own, width = own_ref.shape
     cols = dq_ref.shape[1]
@@ -573,7 +662,7 @@
             lanes = slice(i * rows, (i + 1) * rows)
             grads = dot_tn(own_ref[:, lanes], d_ref[:own, :]) + dot_tn(rest_ref[:, lanes], d_ref[own:, :])
             all_ref[:, i * cols : (i + 1) * cols] = grads.astype(BF)
-        to_slots(n_pieces, slots_ref, which, piece, all_ref, out_refs[2 * which], out_refs[2 * which + 1])
+        to_slots(n_pieces, slots_ref, table[which], piece, all_ref, out_refs[2 * which], out_refs[2 * which + 1])
 
 
 def to_slots(n_pieces, pieces_ref, which, piece, all_ref, keep_ref, send_ref):
@@ -584,12 +673,12 @@
         out_ref[to : to + piece, :] = all_ref[pl.ds(at, piece), :]
 
 
-def late_grads(pieces, n_pieces, own, rest, backs, at, cols):
+def late_grads(pieces, n_pieces, table, own, rest, backs, at, cols):
     width = own.shape[1]
     rows = width * cols // 1024
     strip = pl.BlockSpec((LEN, cols), lambda i, s: (0, at))
     return pl.pallas_call(
-        functools.partial(late_kernel, n_pieces),
+        functools.partial(late_kernel, n_pieces, table),
         grid_spec=pltpu.PrefetchScalarGridSpec(
             num_scalar_prefetch=1,
             grid=(1,),
@@ -622,7 +711,7 @@
         grads = dot_tn(co_ref[:, lanes], do_ref[...]) + dot_tn(cr_ref[:, lanes], dr_ref[...])
         all_ref[lanes, :] = grads.astype(BF)
     if rows % (16 * n_pieces) == 0:
-        to_slots(n_pieces, pieces_ref, 3, rows // n_pieces, all_ref, keep_ref, send_ref)
+        to_slots(n_pieces, pieces_ref, OUT_ORDER, rows // n_pieces, all_ref, keep_ref, send_ref)
     else:
         keep_ref[...] = all_ref[: rows // 2, :]
         send_ref[...] = all_ref[rows // 2 :, :]
@@ -703,54 +792,56 @@
     sg_rest = rest_rows(sg_own)
     cos_tab, sin_tab = rope_tables(member * own)
 
+    share = jnp.broadcast_to(inverse, (1, LANES))
+    levels = [1 << level for level in range(n_dp.bit_length() - 1)]
+
+    def hop(values):
+        nonlocal share
+        if levels:
+            share = share + swap_dp(share, levels.pop(0), n_dp)
+        values, share = lax.optimization_barrier((values, share))
+        return values
+
     query, key, value = project(in_own, in_rest, cos_tab, sin_tab, w_query, w_key, w_value)
+    query = hop(query)
     ctx_rest, lse_rest = attend(query, key, value, own, rest, own)
-    branch_rest = dot_nn(ctx_rest, w_out).astype(BF)
+    branch_rest = hop(dot_nn(ctx_rest, w_out).astype(BF))
     got_branch = from_others(branch_rest)
     ctx_own, lse_own = attend(query, key, value, 0, own, own)
+    ctx_own = hop(ctx_own)
     mixed, mid_own = norm_mid(tokens, ctx_own, w_out, norm2_gain, norm2_bias, got_branch)
     mid_rest = rest_rows(mid_own)
     mid_turned, mid = turn(mid_own, mid_rest, slots, n_pieces)
-
-    chunks, found = [], {}
+    while levels:
+        mid = hop(mid)
+    scale = n_dp / share[:, :1]
+
+    chunks, found = [], {"scale": scale[0]}
     late_cols = min(256, head_cols)
     late_fits = width * late_cols // 1024 >= 16 * n_pieces and w_out.shape[0] % (16 * n_pieces) == 0
 
-    def send_off(keep, send, which, folds, blocks, names):
-        def done(parts):
-            bases = [found.get(name) for name in names]
-            results = place(parts, pieces, found["scale"], which, folds, blocks, bases)
-            found.update(zip(names, results))
-
-        chunks.append(Chunk(keep, send, orders[which], done))
+    def send_off(keep, send, which, folds, shapes):
+        chunks.append(Chunk(keep, send, orders[which], (which, folds, shapes)))
 
     def work():
         kept = None
         gate_slots = slots
-        total = jnp.broadcast_to(inverse, (1, LANES))
         for index in range(units // block):
+            down_order = DOWN_ORDERS[index % len(DOWN_ORDERS)]
             *kept, down_keep, down_send, a_keep, a_send, b_keep, b_send = feed_forward(
-                index, block, n_pieces, gate_slots, mid, mid_turned, sg_own, sg_rest, w_gate, w_up, w_down, kept
+                index, block, n_pieces, down_order, gate_slots, mid, mid_turned, sg_own, sg_rest, w_gate, w_up, w_down, kept
             )
-            send_off(
-                down_keep, down_send, 0, [(0, width, 0, 0, 0)],
-                [(w_down.shape, (block, width), (index, 0))], ["down"],
-            )
+            folds = [(0, width, 0, index * block, 0)]
+            send_off(down_keep, down_send, down_order, folds, [("down", w_down.shape)])
             for at, (keep, send) in enumerate(((a_keep, a_send), (b_keep, b_send))):
-                folds = [(0, block, 0, 0, 0), (block, 2 * block, 1, 0, 0)]
-                blocks = [(w.shape, (width // 2, block), (at, index)) for w in (w_gate, w_up)]
-                send_off(keep, send, 1 + at, folds, blocks, ["gate", "up"])
-            if index < n_dp.bit_length() - 1:
-                total = total + swap_dp(total, 1 << index, n_dp)
-            gate_slots, kept, total = yield (gate_slots, kept, total)
-        for level in range(units // block, n_dp.bit_length() - 1):
-            total = total + swap_dp(total, 1 << level, n_dp)
-        scale = n_dp / total[:, :1]
-        found["scale"] = scale[0]
+                row, col = at * width // 2, index * block
+                folds = [(0, block, 0, row, col), (block, 2 * block, 1, row, col)]
+                send_off(keep, send, WIDE_ORDERS[at], folds, [("gate", w_gate.shape), ("up", w_up.shape)])
+            gate_slots, kept = yield (gate_slots, kept)
         hidden, d_gate, d_up = kept
-        d_mid_part = dot_nt(d_gate, w_gate) + dot_nt(d_up, w_up)
-        d_mid_part, hidden = yield (d_mid_part, hidden)
-        got = from_others(d_mid_part[own:].astype(BF))
+        d_mid_part, d_mid_rest = d_mid_parts(d_gate, d_up, w_gate, w_up, own)
+        d_mid_part, d_mid_rest, hidden = yield (d_mid_part, d_mid_rest, hidden)
+        got = from_others(d_mid_rest)
         out_part = dot_nn(hidden, w_down)
         got, out_part = yield (got, out_part)
         got_out = from_others(out_part[own:].astype(BF))
@@ -768,10 +859,7 @@
             pieces, n_pieces, d_branch_own, d_branch_rest, ctx_own, ctx_rest, w_out
         )
         if late_fits:
-            send_off(
-                out_keep, out_send, 3, [(0, width, 0, 0, 0)],
-                [(w_out.shape, w_out.shape, (0, 0))], ["out"],
-            )
+            send_off(out_keep, out_send, OUT_ORDER, [(0, width, 0, 0, 0)], [("out", w_out.shape)])
         else:
             grad = jnp.concatenate([out_keep, out_send], axis=0)
             found["out"] = lax.psum(grad, "dp").astype(F32) * scale
@@ -784,11 +872,12 @@
             )
             if late_fits:
                 rows = width * late_cols // 1024
-                folds = [(i * late_cols, (i + 1) * late_cols, 0, i * rows, 0) for i in range(width // rows)]
-                late = late_grads(pieces, n_pieces, in_own, in_rest, backs, at, late_cols)
+                lanes = [i * late_cols for i in range(width // rows + 1)]
+                folds = [(lanes[i], lanes[i + 1], 0, i * rows, at * late_cols) for i in range(width // rows)]
+                late_orders = LATE_ORDERS[at % len(LATE_ORDERS)]
+                late = late_grads(pieces, n_pieces, late_orders, in_own, in_rest, backs, at, late_cols)
                 for which, name in enumerate(("query", "key", "value")):
-                    blocks = [(w_query.shape, (width, late_cols), (0, at))]
-                    send_off(late[2 * which], late[2 * which + 1], which, folds, blocks, [name])
+                    send_off(late[2 * which], late[2 * which + 1], late_orders[which], folds, [(name, w_query.shape)])
         if not late_fits:
             for name, d in zip(("query", "key", "value"), backs):
                 grad = dot_tn(in_own, d[:own]) + dot_tn(in_rest, d[own:])
@@ -804,10 +893,12 @@
             total = total + from_member(vectors, step)
         for level in range(n_dp.bit_length() - 1):
             (total,) = yield (total,)
-            total = total + swap_dp(total, 1 << level, n_dp)
+            other = swap_dp(total, 1 << level, n_dp)
+            yield ()
+            total = total + other
         found["vectors"] = total * scale
 
-    in_rounds(work(), chunks, n_dp, 512)
+    in_rounds(work(), chunks, n_dp, found, lambda done: place(done, pieces, found["scale"], found))
     vectors = found["vectors"]
     return (
         found["output"],

time: 435 us -> 413 us (0.949)
  matrix products: 22.7 us -> 11.4 us
  waiting for transfers between devices: 117 us -> 110 us
    dot_general x5 -> x3, matrix products: 16.5 us -> 3.94 us  [dot_nt(): lax.dot_general(left, right, (((1,), (1,)), ((), ())), preferred_element_...]
    ppermute x76 -> x78, waiting for transfers between devices: 113 us -> 109 us  [swap_dp(): return lax.ppermute(values, 'dp', [(i, i ^ bit) for i in range(n_dp)])]
    add x46 -> x40, other arithmetic: 10.1 us -> 6.51 us  [incoming(): total = self.keep + got.value()]
    ppermute x76 -> x78, starting transfers between devices: 92.6 us -> 89.2 us  [swap_dp(): return lax.ppermute(values, 'dp', [(i, i ^ bit) for i in range(n_dp)])]
    pallas_call x25 -> x16, Pallas kernels: 82.3 us -> 85.6 us  [the longest x4 42.1 us: feed_forward(): pl.pallas_call(functools.partial(ff_kernel, n_pieces, down_order), grid_s...]
    unnamed x142 -> x204, local copies, waits for them, and re-layouts: 16.4 us -> 17.3 us
  transfers between devices with their start and end apart: 85 -> 87, of which waited for: 24 -> 22; matrix products, arithmetic and copies ran while one was open for 11% -> 7% of each run, Pallas kernels for 26% -> 31%
where the time goes in v4:
time: 413 us; the launch traced here: 405 us
  Pallas kernels  151 us (37%)
  waiting for transfers between devices  110 us (27%)
  starting transfers between devices  90.7 us (22%)
  local copies, waits for them, and re-layouts  19.5 us (5%)
  other arithmetic  17.5 us (4%)
  matrix products  11.4 us (3%)
  between operations  5.17 us (1%)
    ppermute x78, waiting for transfers between devices, swap_dp(): return lax.ppermute(values, 'dp', [(i, i ^ bit) for i in range(n_dp)])  109 us
    ppermute x78, starting transfers between devices, swap_dp(): return lax.ppermute(values, 'dp', [(i, i ^ bit) for i in range(n_dp)])  89.2 us
    pallas_call x4, Pallas kernels, feed_forward(): pl.pallas_call(functools.partial(ff_kernel, n_pieces, down_order), grid_s...  42.1 us
    pallas_call x2, Pallas kernels, attend_back(): pl.pallas_call(functools.partial(attend_back_kernel, tile), grid=(pairs,)...  29.4 us
    pallas_call x9, Pallas kernels, place(): pl.pallas_call(lambda s, k, *refs: place_kernel(plans, len(names), len(gi...  25.1 us
    pallas_call x2, Pallas kernels, attend(): pl.pallas_call(attend_kernel, grid=(pairs, count // tile), in_specs=[pl.B...  17.8 us
    unnamed x204, local copies, waits for them, and re-layouts  17.3 us
    pallas_call x1, Pallas kernels, d_mid_parts(): pl.pallas_call(d_mid_kernel, grid=(units // block,), in_specs=[d_spec, d_...  13.2 us
  transfers between devices with their start and end apart: 87, of which 22 were waited for; matrix products, arithmetic and copies ran while one was open for 7% of the time, Pallas kernels for 31%

profile of v4, /device:TPU:0, one launch (start us, length us, event | category | flops | bytes accessed | tf_op | source)
XLA Modules:
  0.0 405.4 jit_solution(4321835469611848529)
XLA Ops:
  6.5 2.6 collective-permute-start.1
  12.1 4.5 %project.1 = (bf16[1024,512]{1,0:T(8,128)(2,1)S(1)}, bf16[1024,512]{1,0:T(8,128)(2,1)S(1)}, bf16[1024,512]{1,0:T(8,128)(2,1)S(1)}) custom-call(bf16[512,1024]{1,0:T(8,128)(2,1)S(1)} %norm_in.1.own_ref, bf16[512,1024]{1,0:T(8,128)(2,1)S(1)} %collective-permute-done.rest_ref, f32[1024,128]{1,0:T(8,128)S(1)} %get-tuple-element.632.cos_ref, ...), custom_call_target="tpu_custom_call" | custom-call | tf_op jit(solution)/shard_map/project/pallas_call | solution.py:104
  18.2 8.8 %attend.3 = (bf16[512,512]{1,0:T(8,128)(2,1)S(1)}, f32[4,2,512]{2,1,0:T(2,128)S(1)}) custom-call(bf16[1024,512]{1,0:T(8,128)(2,1)S(1)} %get-tuple-element.266.q_ref, bf16[1024,512]{1,0:T(8,128)(2,1)S(1)} %get-tuple-element.267.k_ref, bf16[1024,512]{1,0:T(8,128)(2,1)S(1)} %get-tuple-element.268.v_ref), custom_call_target="tpu_custom_call" | custom-call | tf_op jit(solution)/shard_map/attend/pallas_call | solution.py:139
  29.6 9.0 %attend.2 = (bf16[512,512]{1,0:T(8,128)(2,1)S(1)}, f32[4,2,512]{2,1,0:T(2,128)S(1)}) custom-call(bf16[1024,512]{1,0:T(8,128)(2,1)S(1)} %get-tuple-element.266.q_ref, bf16[1024,512]{1,0:T(8,128)(2,1)S(1)} %get-tuple-element.267.k_ref, bf16[1024,512]{1,0:T(8,128)(2,1)S(1)} %get-tuple-element.268.v_ref), custom_call_target="tpu_custom_call" | custom-call | tf_op jit(solution)/shard_map/attend/pallas_call | solution.py:139
  38.7 2.4 norm_mid.1
  43.5 2.7 collective-permute-start.6
  48.0 2.9 turn.1
  54.4 9.9 %feed_forward.4 = (bf16[1024,2048]{1,0:T(8,128)(2,1)S(1)}, bf16[1024,2048]{1,0:T(8,128)(2,1)S(1)}, bf16[1024,2048]{1,0:T(8,128)(2,1)}, bf16[256,1024]{1,0:T(8,12...) custom-call(s32[6,8]{1,0:T(8,128)S(1)} %stack.27.slots_ref, ...), custom_call_target="tpu_custom_call" | custom-call | tf_op jit(solution)/shard_map/feed_forward/pallas_call | solution.py:407
  65.9 10.7 %feed_forward.5 = (bf16[1024,2048]{1,0:T(8,128)(2,1)S(1)}, bf16[1024,2048]{1,0:T(8,128)(2,1)S(1)}, bf16[1024,2048]{1,0:T(8,128)(2,1)}, bf16[256,1024]{1,0:T(8,12...) custom-call(s32[6,8]{1,0:T(8,128)S(1)} %stack.27.slots_ref, ...), custom_call_target="tpu_custom_call", output_to_operand_aliasing={{0}: (8, {}), {1}: (9, {}), {2}: (10, {})} | custom-call | tf_op jit(solution)/shard_map/feed_forward/pallas_call | solution.py:407
  83.2 10.4 %feed_forward.6 = (bf16[1024,2048]{1,0:T(8,128)(2,1)S(1)}, bf16[1024,2048]{1,0:T(8,128)(2,1)S(1)}, bf16[1024,2048]{1,0:T(8,128)(2,1)}, bf16[256,1024]{1,0:T(8,12...) custom-call(s32[6,8]{1,0:T(8,128)S(1)} %stack.27.slots_ref, ...), custom_call_target="tpu_custom_call", output_to_operand_aliasing={{0}: (8, {}), {1}: (9, {}), {2}: (10, {})} | custom-call | tf_op jit(solution)/shard_map/feed_forward/pallas_call | solution.py:407
  98.3 11.2 %feed_forward.7 = (bf16[1024,2048]{1,0:T(8,128)(2,1)S(1)}, bf16[1024,2048]{1,0:T(8,128)(2,1)S(1)}, bf16[1024,2048]{1,0:T(8,128)(2,1)}, bf16[256,1024]{1,0:T(8,12...) custom-call(s32[6,8]{1,0:T(8,128)S(1)} %stack.27.slots_ref, ...), custom_call_target="tpu_custom_call", output_to_operand_aliasing={{0}: (8, {}), {1}: (9, {}), {2}: (10, {})} | custom-call | tf_op jit(solution)/shard_map/feed_forward/pallas_call | solution.py:407
  117.1 2.2 copy-done.2
  119.2 13.2 %d_mid.1 = (f32[512,1024]{1,0:T(8,128)S(1)}, bf16[512,1024]{1,0:T(8,128)(2,1)S(1)}) custom-call(bf16[1024,2048]{1,0:T(8,128)(2,1)S(1)} %get-tuple-element.331.dg_ref, bf16[1024,2048]{1,0:T(8,128)(2,1)S(1)} %copy-done.2, bf16[1024,2048]{1,0:T(8,128)(2,1)S(1)} %copy-done, bf16[1024,2048]{1,0:T(8,128)(2,1)S(1)} %copy-done.1), custom_call_target="tpu_custom_call" | custom-call | tf_op jit(solution)/shard_map/d_mid/pallas_call | solution.py:388
  133.2 6.7 %fusion.17 = f32[1024,1024]{1,0:T(8,128)S(1)} fusion(bf16[1024,2048]{1,0:T(8,128)(2,1)S(1)} %copy-done.4, bf16[2048,1024]{1,0:T(8,128)(2,1)} %wd_ref.7), kind=kOutput, calls=%fused_computation.199 | convolution fusion | flops 4294967296 | bytes 12582912 | tf_op jit(solution)/shard_map/dot_general | solution.py:35
  150.8 2.7 collective-permute-start.27
  153.4 6.1 %collective-permute-done.24 = bf16[256,1024]{1,0:T(8,128)(2,1)S(1)} collective-permute-done((bf16[256,1024]{1,0:T(8,128)(2,1)S(1)}, bf16[256,1024]{1,0:T(8,128)(2,1)S(1)}, u32[]{:S(2)}, u32[]{:S(2)}) %collective-permute-start.24) | collective-permute-done | bytes 524320 | tf_op jit(solution)/shard_map/ppermute | solution.py:461
  162.7 2.7 collective-permute-done.27
  165.4 7.0 %collective-permute-done.26 = bf16[128,1024]{1,0:T(8,128)(2,1)S(1)} collective-permute-done((bf16[128,1024]{1,0:T(8,128)(2,1)S(1)}, bf16[128,1024]{1,0:T(8,128)(2,1)S(1)}, u32[]{:S(2)}, u32[]{:S(2)}) %collective-permute-start.26) | collective-permute-done | bytes 262176 | tf_op jit(solution)/shard_map/ppermute | solution.py:461
  174.5 3.0 collective-permute-start.33
  177.7 2.5 collective-permute-start.32
  180.2 3.1 out_back.1
  185.4 14.6 %attend_back.2 = (bf16[1024,512]{1,0:T(8,128)(2,1)S(1)}, bf16[1024,512]{1,0:T(8,128)(2,1)S(1)}, bf16[1024,512]{1,0:T(8,128)(2,1)S(1)}) custom-call(bf16[1024,512]{1,0:T(8,128)(2,1)S(1)} %copy-done.11, bf16[1024,512]{1,0:T(8,128)(2,1)S(1)} %copy-done.13, bf16[1024,512]{1,0:T(8,128)(2,1)S(1)} %copy-done.15, bf16[1024,512]{1,0:T(8,128)(2,1)S(1)} %get-tuple-element.389.d_ref, ...), custom_call_target="tpu_custom_call" | custom-call | tf_op jit(solution)/shard_map/attend_back/pallas_call | solution.py:197
  200.0 2.6 late_grads.2
  207.1 3.7 collective-permute-start.40
  210.8 14.8 %attend_back.3 = (bf16[1024,512]{1,0:T(8,128)(2,1)S(1)}, bf16[1024,512]{1,0:T(8,128)(2,1)S(1)}, bf16[1024,512]{1,0:T(8,128)(2,1)S(1)}) custom-call(bf16[1024,512]{1,0:T(8,128)(2,1)S(1)} %copy-done.11, bf16[1024,512]{1,0:T(8,128)(2,1)S(1)} %copy-done.13, ...), custom_call_target="tpu_custom_call", output_to_operand_aliasing={{0}: (8, {}), {1}: (9, {}), {2}: (10, {})} | custom-call | tf_op jit(solution)/shard_map/attend_back/pallas_call | solution.py:197
  225.6 2.6 late_grads.3
  241.4 2.4 collective-permute-done.43
  244.8 3.2 norm_back.3
  251.0 18.6 %collective-permute-done.48 = bf16[192,1024]{1,0:T(8,128)(2,1)S(1)} collective-permute-done((bf16[192,1024]{1,0:T(8,128)(2,1)S(1)}, bf16[192,1024]{1,0:T(8,128)(2,1)S(1)}, u32[]{:S(2)}, u32[]{:S(2)}) %collective-permute-start.48) | collective-permute-done | bytes 393248 | tf_op jit(solution)/shard_map/ppermute | solution.py:461
  271.7 2.7 collective-permute-done.57
  275.5 5.3 %collective-permute-done.56 = bf16[192,1024]{1,0:T(8,128)(2,1)S(1)} collective-permute-done((bf16[192,1024]{1,0:T(8,128)(2,1)S(1)}, bf16[192,1024]{1,0:T(8,128)(2,1)S(1)}, u32[]{:S(2)}, u32[]{:S(2)}) %collective-permute-start.56) | collective-permute-done | bytes 393248 | tf_op jit(solution)/shard_map/ppermute | solution.py:461
  282.9 3.9 collective-permute-done.55.refs_3_
  287.1 2.1 collective-permute-start.64
  290.1 19.8 %collective-permute-done.50.refs_7_.refs_2_ = bf16[384,1024]{1,0:T(8,128)(2,1)S(1)} collective-permute-done((bf16[384,1024]{1,0:T(8,128)(2,1)S(1)}, bf16[384,1024]{1,0:T(8,128)(2,1)S(1)}, u32[]{:S(2)}, u32[]{:S(2)}) %collective-permute-start.50) | collective-permute-done | bytes 786464 | tf_op jit(solution)/shard_map/ppermute | solution.py:461
  311.3 2.1 place.9
  318.4 2.8 place.10
  323.7 6.1 %collective-permute-done.58.refs_2_.refs_6_ = bf16[256,1024]{1,0:T(8,128)(2,1)S(1)} collective-permute-done((bf16[256,1024]{1,0:T(8,128)(2,1)S(1)}, bf16[256,1024]{1,0:T(8,128)(2,1)S(1)}, u32[]{:S(2)}, u32[]{:S(2)}) %collective-permute-start.58) | collective-permute-done | bytes 524320 | tf_op jit(solution)/shard_map/ppermute | solution.py:461
  329.8 5.7 %collective-permute-done.60.refs_3_.refs_1_ = bf16[320,1024]{1,0:T(8,128)(2,1)S(1)} collective-permute-done((bf16[320,1024]{1,0:T(8,128)(2,1)S(1)}, bf16[320,1024]{1,0:T(8,128)(2,1)S(1)}, u32[]{:S(2)}, u32[]{:S(2)}) %collective-permute-start.60) | collective-permute-done | bytes 655392 | tf_op jit(solution)/shard_map/ppermute | solution.py:461
  337.0 2.8 place.11
  339.8 2.1 collective-permute-start.68
  347.5 4.8 %collective-permute-done.67.refs_7_.refs_9_ = bf16[288,1024]{1,0:T(8,128)(2,1)S(1)} collective-permute-done((bf16[288,1024]{1,0:T(8,128)(2,1)S(1)}, bf16[288,1024]{1,0:T(8,128)(2,1)S(1)}, u32[]{:S(2)}, u32[]{:S(2)}) %collective-permute-start.67) | collective-permute-done | bytes 589856 | tf_op jit(solution)/shard_map/ppermute | solution.py:461
  354.3 3.3 collective-permute-done.68.refs_3_.refs_1_.refs_5_
  357.6 4.9 %collective-permute-done.66.refs_11_.refs_2_ = bf16[384,1024]{1,0:T(8,128)(2,1)S(1)} collective-permute-done((bf16[384,1024]{1,0:T(8,128)(2,1)S(1)}, bf16[384,1024]{1,0:T(8,128)(2,1)S(1)}, u32[]{:S(2)}, u32[]{:S(2)}) %collective-permute-start.66) | collective-permute-done | bytes 786464 | tf_op jit(solution)/shard_map/ppermute | solution.py:461
  365.4 8.4 %collective-permute-done.76.refs_11_ = bf16[256,1024]{1,0:T(8,128)(2,1)S(1)} collective-permute-done((bf16[256,1024]{1,0:T(8,128)(2,1)S(1)}, bf16[256,1024]{1,0:T(8,128)(2,1)S(1)}, u32[]{:S(2)}, u32[]{:S(2)}) %collective-permute-start.76) | collective-permute-done | bytes 524320 | tf_op jit(solution)/shard_map/ppermute | solution.py:461
  376.6 3.6 place.13
  380.3 3.6 place.14
  398.7 3.7 place.16
  402.4 2.5 place.17
  (537 shorter events, 123.4 us)
Async XLA Ops:
  65.0 16.1 %collective-permute-start.12 = (bf16[256,1024]{1,0:T(8,128)(2,1)S(1)}, bf16[256,1024]{1,0:T(8,128)(2,1)S(1)}, u32[]{:S(2)}, u32[]{:S(2)}) collective-permute-start(bf16[256,1024]{1,0:T(8,128)(2,1)S(1)} %get-tuple-element.282), channel_id=1, source_target_pairs={{0,4},{2,6},{4,0},{6,2},{8,12},{10,14},{12,8},{14,10},{16,20},{18,... | collective-permute-start | bytes 1572872 | tf_op jit(solution)/shard_map/ppermute | solution.py:461
  76.6 17.6 %collective-permute-start.8 = (bf16[256,1024]{1,0:T(8,128)(2,1)S(1)}, bf16[256,1024]{1,0:T(8,128)(2,1)S(1)}, u32[]{:S(2)}, u32[]{:S(2)}) collective-permute-start(bf16[256,1024]{1,0:T(8,128)(2,1)S(1)} %get-tuple-element.291), channel_id=1, source_target_pairs={{0,2},{2,0},{4,6},{6,4},{8,10},{10,8},{12,14},{14,12},{16,18},{18,... | collective-permute-start | bytes 1572872 | tf_op jit(solution)/shard_map/ppermute | solution.py:461
  78.0 16.9 %collective-permute-start.9 = (bf16[256,1024]{1,0:T(8,128)(2,1)S(1)}, bf16[256,1024]{1,0:T(8,128)(2,1)S(1)}, u32[]{:S(2)}, u32[]{:S(2)}) collective-permute-start(bf16[256,1024]{1,0:T(8,128)(2,1)S(1)} %get-tuple-element.292), channel_id=1, source_target_pairs={{0,4},{2,6},{4,0},{6,2},{8,12},{10,14},{12,8},{14,10},{16,20},{18,... | collective-permute-start | bytes 1572872 | tf_op jit(solution)/shard_map/ppermute | solution.py:461
  82.5 31.2 %collective-permute-start.15 = (bf16[256,1024]{1,0:T(8,128)(2,1)}, bf16[256,1024]{1,0:T(8,128)(2,1)}, u32[]{:S(2)}, u32[]{:S(2)}) collective-permute-start(bf16[256,1024]{1,0:T(8,128)(2,1)} %pad_maximum_fusion.9), channel_id=1, source_target_pairs={{0,2},{2,0},{4,6},{6,4},{8,10},{10,8},{12,14},{14,12},{16,18},{18,... | collective-permute-start | bytes 1572872 | tf_op jit(solution)/shard_map/ppermute | solution.py:461
  93.5 21.8 %collective-permute-start.17 = (bf16[256,1024]{1,0:T(8,128)(2,1)S(1)}, bf16[256,1024]{1,0:T(8,128)(2,1)}, u32[]{:S(2)}, u32[]{:S(2)}) collective-permute-start(bf16[256,1024]{1,0:T(8,128)(2,1)S(1)} %get-tuple-element.307), channel_id=1, source_target_pairs={{0,8},{2,10},{4,12},{6,14},{8,0},{10,2},{12,4},{14,6},{16,24},{18,... | collective-permute-start | bytes 1572872 | tf_op jit(solution)/shard_map/ppermute | solution.py:461
  94.2 18.9 %collective-permute-start.16 = (bf16[128,1024]{1,0:T(8,128)(2,1)S(1)}, bf16[128,1024]{1,0:T(8,128)(2,1)S(1)}, u32[]{:S(2)}, u32[]{:S(2)}) collective-permute-start(bf16[128,1024]{1,0:T(8,128)(2,1)S(1)} %slice.727), channel_id=1, source_target_pairs={{0,4},{2,6},{4,0},{6,2},{8,12},{10,14},{12,8},{14,10},{16,20},{18,... | collective-permute-start | bytes 786440 | tf_op jit(solution)/shard_map/ppermute | solution.py:461
  96.9 43.1 %collective-permute-start.14 = (bf16[256,1024]{1,0:T(8,128)(2,1)}, bf16[256,1024]{1,0:T(8,128)(2,1)}, u32[]{:S(2)}, u32[]{:S(2)}) collective-permute-start(bf16[256,1024]{1,0:T(8,128)(2,1)} %pad_maximum_fusion.10), channel_id=1, source_target_pairs={{0,2},{2,0},{4,6},{6,4},{8,10},{10,8},{12,14},{14,12},{16,18},{18,... | collective-permute-start | bytes 1572872 | tf_op jit(solution)/shard_map/ppermute | solution.py:461
  111.5 21.1 %collective-permute-start.22 = (bf16[256,1024]{1,0:T(8,128)(2,1)S(1)}, bf16[256,1024]{1,0:T(8,128)(2,1)S(1)}, u32[]{:S(2)}, u32[]{:S(2)}) collective-permute-start(bf16[256,1024]{1,0:T(8,128)(2,1)S(1)} %get-tuple-element.325), channel_id=1, source_target_pairs={{0,8},{2,10},{4,12},{6,14},{8,0},{10,2},{12,4},{14,6},{16,24},{18,... | collective-permute-start | bytes 1572872 | tf_op jit(solution)/shard_map/ppermute | solution.py:461
  113.1 20.0 %collective-permute-start.20 = (bf16[256,1024]{1,0:T(8,128)(2,1)}, bf16[256,1024]{1,0:T(8,128)(2,1)S(1)}, u32[]{:S(2)}, u32[]{:S(2)}) collective-permute-start(bf16[256,1024]{1,0:T(8,128)(2,1)} %get-tuple-element.323), channel_id=1, source_target_pairs={{0,2},{2,0},{4,6},{6,4},{8,10},{10,8},{12,14},{14,12},{16,18},{18,... | collective-permute-start | bytes 1572872 | tf_op jit(solution)/shard_map/ppermute | solution.py:461
  113.8 19.3 %collective-permute-start.21 = (bf16[256,1024]{1,0:T(8,128)(2,1)S(1)}, bf16[256,1024]{1,0:T(8,128)(2,1)S(1)}, u32[]{:S(2)}, u32[]{:S(2)}) collective-permute-start(bf16[256,1024]{1,0:T(8,128)(2,1)S(1)} %get-tuple-element.324), channel_id=1, source_target_pairs={{0,4},{2,6},{4,0},{6,2},{8,12},{10,14},{12,8},{14,10},{16,20},{18,... | collective-permute-start | bytes 1572872 | tf_op jit(solution)/shard_map/ppermute | solution.py:461
  116.5 23.4 %collective-permute-start.19 = (bf16[128,1024]{1,0:T(8,128)(2,1)S(1)}, bf16[128,1024]{1,0:T(8,128)(2,1)S(1)}, u32[]{:S(2)}, u32[]{:S(2)}) collective-permute-start(bf16[128,1024]{1,0:T(8,128)(2,1)S(1)} %pad_maximum_fusion.26), channel_id=1, source_target_pairs={{0,8},{2,10},{4,12},{6,14},{8,0},{10,2},{12,4},{14,6},{16,24},{18,... | collective-permute-start | bytes 786440 | tf_op jit(solution)/shard_map/ppermute | solution.py:461
  141.8 31.5 %collective-permute-start.29 = (bf16[512,1024]{1,0:T(8,128)(2,1)S(1)}, bf16[512,1024]{1,0:T(8,128)(2,1)S(1)}, u32[]{:S(2)}, u32[]{:S(2)}) collective-permute-start(bf16[512,1024]{1,0:T(8,128)(2,1)S(1)} %slice.929), channel_id=1, source_target_pairs={{0,1},{1,0},{2,3},{3,2},{4,5},{5,4},{6,7},{7,6},{8,9},{9,8},{10,11... | collective-permute-start | bytes 3145736 | tf_op jit(solution)/shard_map/ppermute | solution.py:782
  145.1 28.2 %collective-permute-start.28 = (bf16[512,1024]{1,0:T(8,128)(2,1)S(1)}, bf16[512,1024]{1,0:T(8,128)(2,1)S(1)}, u32[]{:S(2)}, u32[]{:S(2)}) collective-permute-start(bf16[512,1024]{1,0:T(8,128)(2,1)S(1)} %get-tuple-element.351.do_ref), channel_id=1, source_target_pairs={{1,0},{0,1},{3,2},{2,3},{5,4},{4,5},{7,6},{6,7},{9,8},{8,9},{11,10... | collective-permute-start | bytes 3145736 | tf_op jit(solution)/shard_map/ppermute | solution.py:772
  161.2 22.3 %collective-permute-start.34 = (bf16[128,1024]{1,0:T(8,128)(2,1)S(1)}, bf16[128,1024]{1,0:T(8,128)(2,1)S(1)}, u32[]{:S(2)}, u32[]{:S(2)}) collective-permute-start(bf16[128,1024]{1,0:T(8,128)(2,1)S(1)} %slice.743), channel_id=1, source_target_pairs={{0,2},{2,0},{4,6},{6,4},{8,10},{10,8},{12,14},{14,12},{16,18},{18,... | collective-permute-start | bytes 786440 | tf_op jit(solution)/shard_map/ppermute | solution.py:461
  165.4 19.3 %collective-permute-start.36 = (bf16[64,1024]{1,0:T(8,128)(2,1)S(1)}, bf16[64,1024]{1,0:T(8,128)(2,1)S(1)}, u32[]{:S(2)}, u32[]{:S(2)}) collective-permute-start(bf16[64,1024]{1,0:T(8,128)(2,1)S(1)} %slice_add_fusion.35), channel_id=1, source_target_pairs={{0,16},{2,18},{4,20},{6,22},{8,24},{10,26},{12,28},{14,30},{16,0},... | collective-permute-start | bytes 393224 | tf_op jit(solution)/shard_map/ppermute | solution.py:461
  174.5 28.9 %collective-permute-start.33 = (bf16[128,1024]{1,0:T(8,128)(2,1)S(1)}, bf16[128,1024]{1,0:T(8,128)(2,1)S(1)}, u32[]{:S(2)}, u32[]{:S(2)}) collective-permute-start(bf16[128,1024]{1,0:T(8,128)(2,1)S(1)} %pad_maximum_fusion.30), channel_id=1, source_target_pairs={{0,16},{2,18},{4,20},{6,22},{8,24},{10,26},{12,28},{14,30},{16,0},... | collective-permute-start | bytes 786440 | tf_op jit(solution)/shard_map/ppermute | solution.py:461
  177.7 25.8 %collective-permute-start.32 = (bf16[128,1024]{1,0:T(8,128)(2,1)S(1)}, bf16[128,1024]{1,0:T(8,128)(2,1)S(1)}, u32[]{:S(2)}, u32[]{:S(2)}) collective-permute-start(bf16[128,1024]{1,0:T(8,128)(2,1)S(1)} %pad_maximum_fusion.29), channel_id=1, source_target_pairs={{0,8},{2,10},{4,12},{6,14},{8,0},{10,2},{12,4},{14,6},{16,24},{18,... | collective-permute-start | bytes 786440 | tf_op jit(solution)/shard_map/ppermute | solution.py:461
  183.5 20.0 %collective-permute-start.31 = (bf16[384,1024]{1,0:T(8,128)(2,1)S(1)}, bf16[384,1024]{1,0:T(8,128)(2,1)S(1)}, u32[]{:S(2)}, u32[]{:S(2)}) collective-permute-start(bf16[384,1024]{1,0:T(8,128)(2,1)S(1)} %pad_maximum_fusion.1), channel_id=1, source_target_pairs={{0,4},{2,6},{4,0},{6,2},{8,12},{10,14},{12,8},{14,10},{16,20},{18,... | collective-permute-start | bytes 2359304 | tf_op jit(solution)/shard_map/ppermute | solution.py:461
  184.7 18.8 %collective-permute-start.30 = (bf16[384,1024]{1,0:T(8,128)(2,1)S(1)}, bf16[384,1024]{1,0:T(8,128)(2,1)S(1)}, u32[]{:S(2)}, u32[]{:S(2)}) collective-permute-start(bf16[384,1024]{1,0:T(8,128)(2,1)S(1)} %pad_maximum_fusion), channel_id=1, source_target_pairs={{0,2},{2,0},{4,6},{6,4},{8,10},{10,8},{12,14},{14,12},{16,18},{18,... | collective-permute-start | bytes 2359304 | tf_op jit(solution)/shard_map/ppermute | solution.py:461
  204.5 27.3 %collective-permute-start.39 = (bf16[384,1024]{1,0:T(8,128)(2,1)S(1)}, bf16[384,1024]{1,0:T(8,128)(2,1)S(1)}, u32[]{:S(2)}, u32[]{:S(2)}) collective-permute-start(bf16[384,1024]{1,0:T(8,128)(2,1)S(1)} %slice_dynamic-update-slice_fusion.6), channel_id=1, source_target_pairs={{0,8},{2,10},{4,12},{6,14},{8,0},{10,2},{12,4},{14,6},{16,24},{18,... | collective-permute-start | bytes 2359304 | tf_op jit(solution)/shard_map/ppermute | solution.py:461
  204.7 27.2 %collective-permute-start.37 = (bf16[384,1024]{1,0:T(8,128)(2,1)S(1)}, bf16[384,1024]{1,0:T(8,128)(2,1)S(1)}, u32[]{:S(2)}, u32[]{:S(2)}) collective-permute-start(bf16[384,1024]{1,0:T(8,128)(2,1)S(1)} %pad_maximum_fusion.2), channel_id=1, source_target_pairs={{0,2},{2,0},{4,6},{6,4},{8,10},{10,8},{12,14},{14,12},{16,18},{18,... | collective-permute-start | bytes 2359304 | tf_op jit(solution)/shard_map/ppermute | solution.py:461
  206.1 25.7 %collective-permute-start.38 = (bf16[384,1024]{1,0:T(8,128)(2,1)S(1)}, bf16[384,1024]{1,0:T(8,128)(2,1)S(1)}, u32[]{:S(2)}, u32[]{:S(2)}) collective-permute-start(bf16[384,1024]{1,0:T(8,128)(2,1)S(1)} %slice_dynamic-update-slice_fusion.8), channel_id=1, source_target_pairs={{0,4},{2,6},{4,0},{6,2},{8,12},{10,14},{12,8},{14,10},{16,20},{18,... | collective-permute-start | bytes 2359304 | tf_op jit(solution)/shard_map/ppermute | solution.py:461
  207.1 23.4 %collective-permute-start.40 = (bf16[64,1024]{1,0:T(8,128)(2,1)S(1)}, bf16[64,1024]{1,0:T(8,128)(2,1)S(1)}, u32[]{:S(2)}, u32[]{:S(2)}) collective-permute-start(bf16[64,1024]{1,0:T(8,128)(2,1)S(1)} %slice_add_fusion.32), channel_id=1, source_target_pairs={{0,16},{2,18},{4,20},{6,22},{8,24},{10,26},{12,28},{14,30},{16,0},... | collective-permute-start | bytes 393224 | tf_op jit(solution)/shard_map/ppermute | solution.py:461
  232.7 16.9 %collective-permute-start.47 = (bf16[64,1024]{1,0:T(8,128)(2,1)}, bf16[64,1024]{1,0:T(8,128)(2,1)S(1)}, u32[]{:S(2)}, u32[]{:S(2)}) collective-permute-start(bf16[64,1024]{1,0:T(8,128)(2,1)} %slice.773), channel_id=1, source_target_pairs={{0,8},{2,10},{4,12},{6,14},{8,0},{10,2},{12,4},{14,6},{16,24},{18,... | collective-permute-start | bytes 393224 | tf_op jit(solution)/shard_map/ppermute | solution.py:461
  240.3 29.3 %collective-permute-start.48 = (bf16[192,1024]{1,0:T(8,128)(2,1)S(1)}, bf16[192,1024]{1,0:T(8,128)(2,1)S(1)}, u32[]{:S(2)}, u32[]{:S(2)}) collective-permute-start(bf16[192,1024]{1,0:T(8,128)(2,1)S(1)} %pad_maximum_fusion.23), channel_id=1, source_target_pairs={{0,16},{2,18},{4,20},{6,22},{8,24},{10,26},{12,28},{14,30},{16,0},... | collective-permute-start | bytes 1179656 | tf_op jit(solution)/shard_map/ppermute | solution.py:461
  240.4 30.0 %collective-permute-start.46 = (bf16[256,1024]{1,0:T(8,128)(2,1)S(1)}, bf16[256,1024]{1,0:T(8,128)(2,1)S(1)}, u32[]{:S(2)}, u32[]{:S(2)}) collective-permute-start(bf16[256,1024]{1,0:T(8,128)(2,1)S(1)} %pad_maximum_fusion.13), channel_id=1, source_target_pairs={{0,4},{2,6},{4,0},{6,2},{8,12},{10,14},{12,8},{14,10},{16,20},{18,... | collective-permute-start | bytes 1572872 | tf_op jit(solution)/shard_map/ppermute | solution.py:461
  243.8 26.7 %collective-permute-start.45 = (bf16[256,1024]{1,0:T(8,128)(2,1)S(1)}, bf16[256,1024]{1,0:T(8,128)(2,1)S(1)}, u32[]{:S(2)}, u32[]{:S(2)}) collective-permute-start(bf16[256,1024]{1,0:T(8,128)(2,1)S(1)} %pad_maximum_fusion.12), channel_id=1, source_target_pairs={{0,2},{2,0},{4,6},{6,4},{8,10},{10,8},{12,14},{14,12},{16,18},{18,... | collective-permute-start | bytes 1572872 | tf_op jit(solution)/shard_map/ppermute | solution.py:461
  249.3 31.6 %collective-permute-start.56 = (bf16[192,1024]{1,0:T(8,128)(2,1)S(1)}, bf16[192,1024]{1,0:T(8,128)(2,1)S(1)}, u32[]{:S(2)}, u32[]{:S(2)}) collective-permute-start(bf16[192,1024]{1,0:T(8,128)(2,1)S(1)} %pad_maximum_fusion.24), channel_id=1, source_target_pairs={{0,16},{2,18},{4,20},{6,22},{8,24},{10,26},{12,28},{14,30},{16,0},... | collective-permute-start | bytes 1179656 | tf_op jit(solution)/shard_map/ppermute | solution.py:461
  249.6 31.9 %collective-permute-start.54 = (bf16[256,1024]{1,0:T(8,128)(2,1)S(1)}, bf16[256,1024]{1,0:T(8,128)(2,1)S(1)}, u32[]{:S(2)}, u32[]{:S(2)}) collective-permute-start(bf16[256,1024]{1,0:T(8,128)(2,1)S(1)} %pad_maximum_fusion.15), channel_id=1, source_target_pairs={{0,2},{2,0},{4,6},{6,4},{8,10},{10,8},{12,14},{14,12},{16,18},{18,... | collective-permute-start | bytes 1572872 | tf_op jit(solution)/shard_map/ppermute | solution.py:461
  269.6 17.2 %collective-permute-start.55 = (bf16[320,1024]{1,0:T(8,128)(2,1)S(1)}, bf16[320,1024]{1,0:T(8,128)(2,1)S(1)}, u32[]{:S(2)}, u32[]{:S(2)}) collective-permute-start(bf16[320,1024]{1,0:T(8,128)(2,1)S(1)} %pad_maximum_fusion.3), channel_id=1, source_target_pairs={{0,4},{2,6},{4,0},{6,2},{8,12},{10,14},{12,8},{14,10},{16,20},{18,... | collective-permute-start | bytes 1966088 | tf_op jit(solution)/shard_map/ppermute | solution.py:461
  271.3 15.8 %collective-permute-start.53 = (bf16[64,1024]{1,0:T(8,128)(2,1)S(1)}, bf16[64,1024]{1,0:T(8,128)(2,1)S(1)}, u32[]{:S(2)}, u32[]{:S(2)}) collective-permute-start(bf16[64,1024]{1,0:T(8,128)(2,1)S(1)} %slice_add_fusion.22), channel_id=1, source_target_pairs={{0,16},{2,18},{4,20},{6,22},{8,24},{10,26},{12,28},{14,30},{16,0},... | collective-permute-start | bytes 393224 | tf_op jit(solution)/shard_map/ppermute | solution.py:461
  280.8 34.0 %collective-permute-start.62 = (bf16[256,1024]{1,0:T(8,128)(2,1)S(1)}, bf16[256,1024]{1,0:T(8,128)(2,1)S(1)}, u32[]{:S(2)}, u32[]{:S(2)}) collective-permute-start(bf16[256,1024]{1,0:T(8,128)(2,1)S(1)} %pad_maximum_fusion.16), channel_id=1, source_target_pairs={{0,2},{2,0},{4,6},{6,4},{8,10},{10,8},{12,14},{14,12},{16,18},{18,... | collective-permute-start | bytes 1572872 | tf_op jit(solution)/shard_map/ppermute | solution.py:461
  281.5 28.5 %collective-permute-start.50 = (bf16[384,1024]{1,0:T(8,128)(2,1)S(1)}, bf16[384,1024]{1,0:T(8,128)(2,1)S(1)}, u32[]{:S(2)}, u32[]{:S(2)}) collective-permute-start(bf16[384,1024]{1,0:T(8,128)(2,1)S(1)} %get-tuple-element.586), channel_id=1, source_target_pairs={{0,2},{2,0},{4,6},{6,4},{8,10},{10,8},{12,14},{14,12},{16,18},{18,... | collective-permute-start | bytes 2359304 | tf_op jit(solution)/shard_map/ppermute | solution.py:461
  286.8 23.2 %collective-permute-start.52 = (bf16[448,1024]{1,0:T(8,128)(2,1)S(1)}, bf16[448,1024]{1,0:T(8,128)(2,1)S(1)}, u32[]{:S(2)}, u32[]{:S(2)}) collective-permute-start(bf16[448,1024]{1,0:T(8,128)(2,1)S(1)} %constant_dynamic-update-slice_fusion.11), channel_id=1, source_target_pairs={{0,8},{2,10},{4,12},{6,14},{8,0},{10,2},{12,4},{14,6},{16,24},{18,... | collective-permute-start | bytes 2752520 | tf_op jit(solution)/shard_map/ppermute | solution.py:461
  287.1 28.4 %collective-permute-start.64 = (bf16[192,1024]{1,0:T(8,128)(2,1)S(1)}, bf16[192,1024]{1,0:T(8,128)(2,1)S(1)}, u32[]{:S(2)}, u32[]{:S(2)}) collective-permute-start(bf16[192,1024]{1,0:T(8,128)(2,1)S(1)} %pad_maximum_fusion.25), channel_id=1, source_target_pairs={{0,8},{2,10},{4,12},{6,14},{8,0},{10,2},{12,4},{14,6},{16,24},{18,... | collective-permute-start | bytes 1179656 | tf_op jit(solution)/shard_map/ppermute | solution.py:461
  289.2 27.2 %collective-permute-start.63 = (bf16[352,1024]{1,0:T(8,128)(2,1)S(1)}, bf16[352,1024]{1,0:T(8,128)(2,1)S(1)}, u32[]{:S(2)}, u32[]{:S(2)}) collective-permute-start(bf16[352,1024]{1,0:T(8,128)(2,1)S(1)} %constant_dynamic-update-slice_fusion.17), channel_id=1, source_target_pairs={{0,4},{2,6},{4,0},{6,2},{8,12},{10,14},{12,8},{14,10},{16,20},{18,... | collective-permute-start | bytes 2162696 | tf_op jit(solution)/shard_map/ppermute | solution.py:461
  315.6 19.9 %collective-permute-start.60 = (bf16[320,1024]{1,0:T(8,128)(2,1)S(1)}, bf16[320,1024]{1,0:T(8,128)(2,1)S(1)}, u32[]{:S(2)}, u32[]{:S(2)}) collective-permute-start(bf16[320,1024]{1,0:T(8,128)(2,1)S(1)} %pad_maximum_fusion.4), channel_id=1, source_target_pairs={{0,8},{2,10},{4,12},{6,14},{8,0},{10,2},{12,4},{14,6},{16,24},{18,... | collective-permute-start | bytes 1966088 | tf_op jit(solution)/shard_map/ppermute | solution.py:461
  316.5 25.4 %collective-permute-start.71 = (bf16[96,1024]{1,0:T(8,128)(2,1)S(1)}, bf16[96,1024]{1,0:T(8,128)(2,1)S(1)}, u32[]{:S(2)}, u32[]{:S(2)}) collective-permute-start(bf16[96,1024]{1,0:T(8,128)(2,1)S(1)} %pad_maximum_fusion.45), channel_id=1, source_target_pairs={{0,16},{2,18},{4,20},{6,22},{8,24},{10,26},{12,28},{14,30},{16,0},... | collective-permute-start | bytes 589832 | tf_op jit(solution)/shard_map/ppermute | solution.py:461
  321.3 22.2 %collective-permute-start.70 = (bf16[128,1024]{1,0:T(8,128)(2,1)S(1)}, bf16[128,1024]{1,0:T(8,128)(2,1)S(1)}, u32[]{:S(2)}, u32[]{:S(2)}) collective-permute-start(bf16[128,1024]{1,0:T(8,128)(2,1)S(1)} %pad_maximum_fusion.32), channel_id=1, source_target_pairs={{0,4},{2,6},{4,0},{6,2},{8,12},{10,14},{12,8},{14,10},{16,20},{18,... | collective-permute-start | bytes 786440 | tf_op jit(solution)/shard_map/ppermute | solution.py:461
  322.3 21.3 %collective-permute-start.69 = (bf16[256,1024]{1,0:T(8,128)(2,1)S(1)}, bf16[256,1024]{1,0:T(8,128)(2,1)S(1)}, u32[]{:S(2)}, u32[]{:S(2)}) collective-permute-start(bf16[256,1024]{1,0:T(8,128)(2,1)S(1)} %pad_maximum_fusion.18), channel_id=1, source_target_pairs={{0,2},{2,0},{4,6},{6,4},{8,10},{10,8},{12,14},{14,12},{16,18},{18,... | collective-permute-start | bytes 1572872 | tf_op jit(solution)/shard_map/ppermute | solution.py:461
  336.0 16.3 %collective-permute-start.67 = (bf16[288,1024]{1,0:T(8,128)(2,1)S(1)}, bf16[288,1024]{1,0:T(8,128)(2,1)S(1)}, u32[]{:S(2)}, u32[]{:S(2)}) collective-permute-start(bf16[288,1024]{1,0:T(8,128)(2,1)S(1)} %pad_maximum_fusion.5), channel_id=1, source_target_pairs={{0,4},{2,6},{4,0},{6,2},{8,12},{10,14},{12,8},{14,10},{16,20},{18,... | collective-permute-start | bytes 1769480 | tf_op jit(solution)/shard_map/ppermute | solution.py:461
  339.8 17.7 %collective-permute-start.68 = (bf16[320,1024]{1,0:T(8,128)(2,1)S(1)}, bf16[320,1024]{1,0:T(8,128)(2,1)S(1)}, u32[]{:S(2)}, u32[]{:S(2)}) collective-permute-start(bf16[320,1024]{1,0:T(8,128)(2,1)S(1)} %get-tuple-element.531), channel_id=1, source_target_pairs={{0,8},{2,10},{4,12},{6,14},{8,0},{10,2},{12,4},{14,6},{16,24},{18,... | collective-permute-start | bytes 1966088 | tf_op jit(solution)/shard_map/ppermute | solution.py:461
  341.9 20.5 %collective-permute-start.66 = (bf16[384,1024]{1,0:T(8,128)(2,1)S(1)}, bf16[384,1024]{1,0:T(8,128)(2,1)S(1)}, u32[]{:S(2)}, u32[]{:S(2)}) collective-permute-start(bf16[384,1024]{1,0:T(8,128)(2,1)S(1)} %get-tuple-element.580), channel_id=1, source_target_pairs={{0,2},{2,0},{4,6},{6,4},{8,10},{10,8},{12,14},{14,12},{16,18},{18,... | collective-permute-start | bytes 2359304 | tf_op jit(solution)/shard_map/ppermute | solution.py:461
  343.6 30.1 %collective-permute-start.76 = (bf16[256,1024]{1,0:T(8,128)(2,1)S(1)}, bf16[256,1024]{1,0:T(8,128)(2,1)S(1)}, u32[]{:S(2)}, u32[]{:S(2)}) collective-permute-start(bf16[256,1024]{1,0:T(8,128)(2,1)S(1)} %pad_maximum_fusion.19), channel_id=1, source_target_pairs={{0,2},{2,0},{4,6},{6,4},{8,10},{10,8},{12,14},{14,12},{16,18},{18,... | collective-permute-start | bytes 1572872 | tf_op jit(solution)/shard_map/ppermute | solution.py:461
  344.3 29.4 %collective-permute-start.77 = (bf16[288,1024]{1,0:T(8,128)(2,1)S(1)}, bf16[288,1024]{1,0:T(8,128)(2,1)S(1)}, u32[]{:S(2)}, u32[]{:S(2)}) collective-permute-start(bf16[288,1024]{1,0:T(8,128)(2,1)S(1)} %pad_maximum_fusion.6), channel_id=1, source_target_pairs={{0,4},{2,6},{4,0},{6,2},{8,12},{10,14},{12,8},{14,10},{16,20},{18,... | collective-permute-start | bytes 1769480 | tf_op jit(solution)/shard_map/ppermute | solution.py:461
  352.3 21.4 %collective-permute-start.78 = (bf16[320,1024]{1,0:T(8,128)(2,1)S(1)}, bf16[320,1024]{1,0:T(8,128)(2,1)S(1)}, u32[]{:S(2)}, u32[]{:S(2)}) collective-permute-start(bf16[320,1024]{1,0:T(8,128)(2,1)S(1)} %get-tuple-element.525), channel_id=1, source_target_pairs={{0,8},{2,10},{4,12},{6,14},{8,0},{10,2},{12,4},{14,6},{16,24},{18,... | collective-permute-start | bytes 1966088 | tf_op jit(solution)/shard_map/ppermute | solution.py:461
  362.6 17.6 %collective-permute-start.75 = (bf16[320,1024]{1,0:T(8,128)(2,1)S(1)}, bf16[320,1024]{1,0:T(8,128)(2,1)S(1)}, u32[]{:S(2)}, u32[]{:S(2)}) collective-permute-start(bf16[320,1024]{1,0:T(8,128)(2,1)S(1)} %get-tuple-element.575), channel_id=1, source_target_pairs={{0,4},{2,6},{4,0},{6,2},{8,12},{10,14},{12,8},{14,10},{16,20},{18,... | collective-permute-start | bytes 1966088 | tf_op jit(solution)/shard_map/ppermute | solution.py:461
  363.7 16.5 %collective-permute-start.74 = (bf16[128,1024]{1,0:T(8,128)(2,1)S(1)}, bf16[128,1024]{1,0:T(8,128)(2,1)S(1)}, u32[]{:S(2)}, u32[]{:S(2)}) collective-permute-start(bf16[128,1024]{1,0:T(8,128)(2,1)S(1)} %pad_maximum_fusion.33), channel_id=1, source_target_pairs={{0,2},{2,0},{4,6},{6,4},{8,10},{10,8},{12,14},{14,12},{16,18},{18,... | collective-permute-start | bytes 786440 | tf_op jit(solution)/shard_map/ppermute | solution.py:461
  (134 other events, 937.9 us)

commit v5 on v4

--- a/solution.py
+++ b/solution.py
@@ -22,9 +22,9 @@
 DOWN_ORDERS = (0, 0, 0, 0)
 OUT_ORDER = 2
 LATE_ORDERS = ((0, 2, 4), (0, 2, 4))
-EARLY = (0, 0, 0, 0, 0, 0, 1, 0, 0, 1, 0, 0, 0, 0, 0, 0, 0, 0, 0, 0, 0, 0, 0, 1, 0, 1, 1, 0, 0, 0)
-LIMITS = (256, 640, 768, 320, 64, 256, 128, 192, 512, 384, 320, 320, 320, 512, 384, 320, 448, 512, 768, 448, 448, 384, 512, 384, 320, 64, 192, 768, 768, 320)
-RANKS = (1, 3, 1, 0, 1, 0, 2, 2, 2, 2, 2, 3, 1, 1, 3, 3, 1, 1, 3, 0, 0, 3, 3, 3, 1, 3, 1, 3, 3, 2)
+EARLY = (1, 1, 1, 1, 1, 1, 1, 1, 1, 1, 1, 1, 0, 0, 0, 0, 0, 0, 0, 0, 0, 0, 0, 0, 0, 0, 0, 0, 0, 0)
+LIMITS = (384, 384, 384, 384, 384, 384, 384, 384, 384, 384, 384, 384, 384, 384, 384, 384, 384, 384, 384, 384, 384, 384, 384, 384, 384, 384, 384, 384, 384, 384)
+RANKS = (0, 0, 0, 0, 0, 0, 0, 1, 1, 1, 1, 1, 1, 1, 1, 1, 1, 1, 1, 1, 1, 1, 1, 1, 1, 1, 1, 1, 1, 1)
 
 
 def shape_of(dims, dtype):
@@ -549,9 +549,10 @@
         free.sort(key=lambda c: (0, -c.left, -c.next_rows(), c.next_rows())[rank])
         for chunk in free:
             bit, rows = chunk.bit, chunk.next_rows()
-            if loads.get(bit, 0) and loads[bit] + rows > limit:
+            cost = rows * (2 if bit == n_dp // 2 else 1)
+            if loads.get(bit, 0) and loads[bit] + cost > limit:
                 continue
-            loads[bit] = loads.get(bit, 0) + rows
+            loads[bit] = loads.get(bit, 0) + cost
             picks.setdefault(bit, []).append(chunk)
         sends = {}
         for bit in sorted(picks):
@@ -843,18 +844,18 @@
         d_mid_part, d_mid_rest, hidden = yield (d_mid_part, d_mid_rest, hidden)
         got = from_others(d_mid_rest)
         out_part = dot_nn(hidden, w_down)
-        got, out_part = yield (got, out_part)
         got_out = from_others(out_part[own:].astype(BF))
+        got, out_part = lax.optimization_barrier((got, out_part))
         d_mixed, d_branch_own, sums2 = norm_backward(
             "mid", mixed, sg_own, norm2_gain, scale, d_mid_part, got
         )
         d_branch_rest = rest_rows(d_branch_own)
         lse = jnp.concatenate([lse_own, lse_rest], axis=2)
-        d_branch_rest, got_out = yield (d_branch_rest, got_out)
         output = mixed + out_part[:own]
         for part in got_out:
             output = output + part.astype(F32)
-        found["output"] = output.astype(BF)
+        output = output.astype(BF)
+        d_branch_rest, found["output"] = lax.optimization_barrier((d_branch_rest, output))
         d_context, delta, out_keep, out_send = out_back(
             pieces, n_pieces, d_branch_own, d_branch_rest, ctx_own, ctx_rest, w_out
         )
@@ -865,7 +866,7 @@
             found["out"] = lax.psum(grad, "dp").astype(F32) * scale
         backs = ()
         for at in range(head_cols // late_cols):
-            d_context, backs = yield (d_context, backs)
+            d_context, *backs = yield (d_context, *backs)
             per = late_cols // LANES
             backs = attend_back(
                 query, key, value, d_context, delta, lse, cos_tab, sin_tab, at * per, per, backs
@@ -877,15 +878,15 @@
                 late_orders = LATE_ORDERS[at % len(LATE_ORDERS)]
                 late = late_grads(pieces, n_pieces, late_orders, in_own, in_rest, backs, at, late_cols)
                 for which, name in enumerate(("query", "key", "value")):
-                    send_off(late[2 * which], late[2 * which + 1], late_orders[which], folds, [(name, w_query.shape)])
+                    target = [(name, w_query.shape)]
+                    send_off(late[2 * which], late[2 * which + 1], late_orders[which], folds, target)
         if not late_fits:
             for name, d in zip(("query", "key", "value"), backs):
                 grad = dot_tn(in_own, d[:own]) + dot_tn(in_rest, d[own:])
                 found[name] = lax.psum(grad.astype(BF), "dp").astype(F32) * scale
-        (backs,) = yield (backs,)
+        backs = yield (*backs,)
         d_in_part = sum(dot_nt(d, w) for d, w in zip(backs, (w_query, w_key, w_value)))
         got = from_others(d_in_part[own:].astype(BF))
-        (got,) = yield (got,)
         found["input"], sums1 = norm_backward("in", tokens, d_mixed, norm1_gain, scale, d_in_part, got)
         vectors = jnp.concatenate([sums1, sums2], axis=0)
         total = vectors
@@ -893,9 +894,7 @@
             total = total + from_member(vectors, step)
         for level in range(n_dp.bit_length() - 1):
             (total,) = yield (total,)
-            other = swap_dp(total, 1 << level, n_dp)
-            yield ()
-            total = total + other
+            total = total + swap_dp(total, 1 << level, n_dp)
         found["vectors"] = total * scale
 
     in_rounds(work(), chunks, n_dp, found, lambda done: place(done, pieces, found["scale"], found))

time: 413 us -> 394 us (0.954)
  starting transfers between devices: 90.7 us -> 71.6 us
  waiting for transfers between devices: 110 us -> 117 us
    ppermute x78 -> x65, starting transfers between devices: 89.2 us -> 69.1 us  [swap_dp(): return lax.ppermute(values, 'dp', [(i, i ^ bit) for i in range(n_dp)])]
    ppermute x78 -> x65, waiting for transfers between devices: 109 us -> 116 us  [swap_dp(): return lax.ppermute(values, 'dp', [(i, i ^ bit) for i in range(n_dp)])]
    unnamed x204 -> x161, local copies, waits for them, and re-layouts: 17.3 us -> 13.9 us
    pallas_call x9 -> x8, Pallas kernels: 25.1 us -> 23.8 us  [place(): pl.pallas_call(lambda s, k, *refs: place_kernel(plans, len(names), len(gi...]
  transfers between devices with their start and end apart: 87 -> 74, of which waited for: 22 -> 28; matrix products, arithmetic and copies ran while one was open for 7% -> 5% of each run, Pallas kernels for 31% -> 32%
where the time goes in v5:
time: 394 us; the launch traced here: 386 us
  Pallas kernels  150 us (38%)
  waiting for transfers between devices  117 us (30%)
  starting transfers between devices  71.6 us (18%)
  other arithmetic  17.2 us (4%)
  local copies, waits for them, and re-layouts  16.3 us (4%)
  matrix products  9.23 us (2%)
  between operations  4.65 us (1%)
    ppermute x65, waiting for transfers between devices, swap_dp(): return lax.ppermute(values, 'dp', [(i, i ^ bit) for i in range(n_dp)])  116 us
    ppermute x65, starting transfers between devices, swap_dp(): return lax.ppermute(values, 'dp', [(i, i ^ bit) for i in range(n_dp)])  69.1 us
    pallas_call x4, Pallas kernels, feed_forward(): pl.pallas_call(functools.partial(ff_kernel, n_pieces, down_order), grid_s...  41.4 us
    pallas_call x2, Pallas kernels, attend_back(): pl.pallas_call(functools.partial(attend_back_kernel, tile), grid=(pairs,)...  29.8 us
    pallas_call x8, Pallas kernels, place(): pl.pallas_call(lambda s, k, *refs: place_kernel(plans, len(names), len(gi...  23.8 us
    pallas_call x2, Pallas kernels, attend(): pl.pallas_call(attend_kernel, grid=(pairs, count // tile), in_specs=[pl.B...  17.8 us
    unnamed x161, local copies, waits for them, and re-layouts  13.9 us
    pallas_call x1, Pallas kernels, d_mid_parts(): pl.pallas_call(d_mid_kernel, grid=(units // block,), in_specs=[d_spec, d_...  13.2 us
  transfers between devices with their start and end apart: 74, of which 28 were waited for; matrix products, arithmetic and copies ran while one was open for 5% of the time, Pallas kernels for 32%

profile of v5, /device:TPU:0, one launch (start us, length us, event | category | flops | bytes accessed | tf_op | source)
XLA Modules:
  0.0 386.3 jit_solution(18296622814485942976)
XLA Ops:
  6.5 2.6 collective-permute-start.1
  12.1 4.5 %project.1 = (bf16[1024,512]{1,0:T(8,128)(2,1)S(1)}, bf16[1024,512]{1,0:T(8,128)(2,1)S(1)}, bf16[1024,512]{1,0:T(8,128)(2,1)S(1)}) custom-call(bf16[512,1024]{1,0:T(8,128)(2,1)S(1)} %norm_in.1.own_ref, bf16[512,1024]{1,0:T(8,128)(2,1)S(1)} %collective-permute-done.rest_ref, f32[1024,128]{1,0:T(8,128)S(1)} %get-tuple-element.669.cos_ref, ...), custom_call_target="tpu_custom_call" | custom-call | tf_op jit(solution)/shard_map/project/pallas_call | solution.py:104
  18.2 8.8 %attend.3 = (bf16[512,512]{1,0:T(8,128)(2,1)S(1)}, f32[4,2,512]{2,1,0:T(2,128)S(1)}) custom-call(bf16[1024,512]{1,0:T(8,128)(2,1)S(1)} %get-tuple-element.274.q_ref, bf16[1024,512]{1,0:T(8,128)(2,1)S(1)} %get-tuple-element.275.k_ref, bf16[1024,512]{1,0:T(8,128)(2,1)S(1)} %get-tuple-element.276.v_ref), custom_call_target="tpu_custom_call" | custom-call | tf_op jit(solution)/shard_map/attend/pallas_call | solution.py:139
  29.6 9.0 %attend.2 = (bf16[512,512]{1,0:T(8,128)(2,1)S(1)}, f32[4,2,512]{2,1,0:T(2,128)S(1)}) custom-call(bf16[1024,512]{1,0:T(8,128)(2,1)S(1)} %get-tuple-element.274.q_ref, bf16[1024,512]{1,0:T(8,128)(2,1)S(1)} %get-tuple-element.275.k_ref, bf16[1024,512]{1,0:T(8,128)(2,1)S(1)} %get-tuple-element.276.v_ref), custom_call_target="tpu_custom_call" | custom-call | tf_op jit(solution)/shard_map/attend/pallas_call | solution.py:139
  38.7 2.4 norm_mid.1
  43.5 2.6 collective-permute-start.6
  48.0 2.9 turn.1
  50.9 9.8 %feed_forward.4 = (bf16[1024,2048]{1,0:T(8,128)(2,1)S(1)}, bf16[1024,2048]{1,0:T(8,128)(2,1)S(1)}, bf16[1024,2048]{1,0:T(8,128)(2,1)}, bf16[256,1024]{1,0:T(8,12...) custom-call(s32[6,8]{1,0:T(8,128)S(1)} %stack.27.slots_ref, ...), custom_call_target="tpu_custom_call" | custom-call | tf_op jit(solution)/shard_map/feed_forward/pallas_call | solution.py:407
  62.4 10.7 %feed_forward.5 = (bf16[1024,2048]{1,0:T(8,128)(2,1)S(1)}, bf16[1024,2048]{1,0:T(8,128)(2,1)S(1)}, bf16[1024,2048]{1,0:T(8,128)(2,1)}, bf16[256,1024]{1,0:T(8,12...) custom-call(s32[6,8]{1,0:T(8,128)S(1)} %stack.27.slots_ref, ...), custom_call_target="tpu_custom_call", output_to_operand_aliasing={{0}: (8, {}), {1}: (9, {}), {2}: (10, {})} | custom-call | tf_op jit(solution)/shard_map/feed_forward/pallas_call | solution.py:407
  78.5 10.4 %feed_forward.6 = (bf16[1024,2048]{1,0:T(8,128)(2,1)S(1)}, bf16[1024,2048]{1,0:T(8,128)(2,1)S(1)}, bf16[1024,2048]{1,0:T(8,128)(2,1)}, bf16[256,1024]{1,0:T(8,12...) custom-call(s32[6,8]{1,0:T(8,128)S(1)} %stack.27.slots_ref, ...), custom_call_target="tpu_custom_call", output_to_operand_aliasing={{0}: (8, {}), {1}: (9, {}), {2}: (10, {})} | custom-call | tf_op jit(solution)/shard_map/feed_forward/pallas_call | solution.py:407
  88.9 2.7 collective-permute-done.12
  97.9 10.5 %feed_forward.7 = (bf16[1024,2048]{1,0:T(8,128)(2,1)S(1)}, bf16[1024,2048]{1,0:T(8,128)(2,1)S(1)}, bf16[1024,2048]{1,0:T(8,128)(2,1)}, bf16[256,1024]{1,0:T(8,12...) custom-call(s32[6,8]{1,0:T(8,128)S(1)} %stack.27.slots_ref, ...), custom_call_target="tpu_custom_call", output_to_operand_aliasing={{0}: (8, {}), {1}: (9, {}), {2}: (10, {})} | custom-call | tf_op jit(solution)/shard_map/feed_forward/pallas_call | solution.py:407
  108.9 3.5 collective-permute-done.14
  117.0 2.6 collective-permute-start.20
  119.8 2.4 copy-done
  122.2 2.2 copy-done.2
  124.3 13.2 %d_mid.1 = (f32[512,1024]{1,0:T(8,128)S(1)}, bf16[512,1024]{1,0:T(8,128)(2,1)S(1)}) custom-call(bf16[1024,2048]{1,0:T(8,128)(2,1)S(1)} %get-tuple-element.354.dg_ref, bf16[1024,2048]{1,0:T(8,128)(2,1)S(1)} %copy-done.2, bf16[1024,2048]{1,0:T(8,128)(2,1)S(1)} %copy-done, bf16[1024,2048]{1,0:T(8,128)(2,1)S(1)} %copy-done.1), custom_call_target="tpu_custom_call" | custom-call | tf_op jit(solution)/shard_map/d_mid/pallas_call | solution.py:388
  139.3 2.0 constant_dynamic-update-slice_fusion.3
  142.5 4.5 %fusion.22 = f32[1024,1024]{1,0:T(8,128)S(1)} fusion(bf16[1024,2048]{1,0:T(8,128)(2,1)S(1)} %get-tuple-element.369, bf16[2048,1024]{1,0:T(8,128)(2,1)S(1)} %copy-done.37), kind=kOutput, calls=%fused_computation.235 | convolution fusion | flops 4294967296 | bytes 12582912 | tf_op jit(solution)/shard_map/dot_general | solution.py:35
  158.6 3.1 out_back.1
  161.7 4.2 %collective-permute-done.27 = bf16[64,1024]{1,0:T(8,128)(2,1)S(1)} collective-permute-done((bf16[64,1024]{1,0:T(8,128)(2,1)S(1)}, bf16[64,1024]{1,0:T(8,128)(2,1)S(1)}, u32[]{:S(2)}, u32[]{:S(2)}) %collective-permute-start.27) | collective-permute-done | bytes 131104 | tf_op jit(solution)/shard_map/ppermute | solution.py:461
  168.1 4.0 %collective-permute-done.24 = bf16[384,1024]{1,0:T(8,128)(2,1)S(1)} collective-permute-done((bf16[384,1024]{1,0:T(8,128)(2,1)}, bf16[384,1024]{1,0:T(8,128)(2,1)S(1)}, u32[]{:S(2)}, u32[]{:S(2)}) %collective-permute-start.24) | collective-permute-done | bytes 786464 | tf_op jit(solution)/shard_map/ppermute | solution.py:461
  177.2 14.8 %attend_back.2 = (bf16[1024,512]{1,0:T(8,128)(2,1)S(1)}, bf16[1024,512]{1,0:T(8,128)(2,1)S(1)}, bf16[1024,512]{1,0:T(8,128)(2,1)S(1)}) custom-call(bf16[1024,512]{1,0:T(8,128)(2,1)S(1)} %get-tuple-element.274.q_ref, bf16[1024,512]{1,0:T(8,128)(2,1)S(1)} %copy-done.4, bf16[1024,512]{1,0:T(8,128)(2,1)S(1)} %copy-done.6, ...), custom_call_target="tpu_custom_call" | custom-call | tf_op jit(solution)/shard_map/attend_back/pallas_call | solution.py:197
  192.0 2.6 late_grads.2
  197.2 2.6 collective-permute-start.35
  201.3 15.0 %attend_back.3 = (bf16[1024,512]{1,0:T(8,128)(2,1)S(1)}, bf16[1024,512]{1,0:T(8,128)(2,1)S(1)}, bf16[1024,512]{1,0:T(8,128)(2,1)S(1)}) custom-call(bf16[1024,512]{1,0:T(8,128)(2,1)S(1)} %get-tuple-element.274.q_ref, bf16[1024,512]{1,0:T(8,128)(2,1)S(1)} %copy-done.4, ...), custom_call_target="tpu_custom_call", output_to_operand_aliasing={{0}: (8, {}), {1}: (9, {}), {2}: (10, {})} | custom-call | tf_op jit(solution)/shard_map/attend_back/pallas_call | solution.py:197
  216.3 2.6 late_grads.3
  229.0 3.2 norm_back.3
  233.5 3.3 collective-permute-done.40
  236.8 7.5 %collective-permute-done.39.refs_1_.refs_5_ = bf16[256,1024]{1,0:T(8,128)(2,1)S(1)} collective-permute-done((bf16[256,1024]{1,0:T(8,128)(2,1)S(1)}, bf16[256,1024]{1,0:T(8,128)(2,1)S(1)}, u32[]{:S(2)}, u32[]{:S(2)}) %collective-permute-start.39) | collective-permute-done | bytes 524320 | tf_op jit(solution)/shard_map/ppermute | solution.py:461
  251.6 15.4 %collective-permute-done.46 = f32[4,1024]{1,0:T(4,128)S(1)} collective-permute-done((f32[4,1024]{1,0:T(4,128)S(1)}, f32[4,1024]{1,0:T(4,128)S(1)}, u32[]{:S(2)}, u32[]{:S(2)}) %collective-permute-start.46) | collective-permute-done | bytes 16416 | tf_op jit(solution)/shard_map/ppermute | solution.py:461
  272.4 5.8 %collective-permute-done.51 = f32[4,1024]{1,0:T(4,128)S(1)} collective-permute-done((f32[4,1024]{1,0:T(4,128)S(1)}, f32[4,1024]{1,0:T(4,128)S(1)}, u32[]{:S(2)}, u32[]{:S(2)}) %collective-permute-start.51) | collective-permute-done | bytes 16416 | tf_op jit(solution)/shard_map/ppermute | solution.py:461
  278.9 10.5 %collective-permute-done.50 = bf16[192,1024]{1,0:T(8,128)(2,1)S(1)} collective-permute-done((bf16[192,1024]{1,0:T(8,128)(2,1)S(1)}, bf16[192,1024]{1,0:T(8,128)(2,1)S(1)}, u32[]{:S(2)}, u32[]{:S(2)}) %collective-permute-start.50) | collective-permute-done | bytes 393248 | tf_op jit(solution)/shard_map/ppermute | solution.py:461
  294.5 2.0 collective-permute-start.56
  296.6 2.1 place.8
  298.7 8.5 %collective-permute-done.56 = f32[4,1024]{1,0:T(4,128)S(1)} collective-permute-done((f32[4,1024]{1,0:T(4,128)S(1)}, f32[4,1024]{1,0:T(4,128)S(1)}, u32[]{:S(2)}, u32[]{:S(2)}) %collective-permute-start.56) | collective-permute-done | bytes 16416 | tf_op jit(solution)/shard_map/ppermute | solution.py:461
  313.5 8.6 %collective-permute-done.62.refs_7_ = bf16[256,1024]{1,0:T(8,128)(2,1)S(1)} collective-permute-done((bf16[256,1024]{1,0:T(8,128)(2,1)S(1)}, bf16[256,1024]{1,0:T(8,128)(2,1)S(1)}, u32[]{:S(2)}, u32[]{:S(2)}) %collective-permute-start.62) | collective-permute-done | bytes 524320 | tf_op jit(solution)/shard_map/ppermute | solution.py:461
  323.9 11.5 %collective-permute-done.63.refs_11_ = bf16[256,1024]{1,0:T(8,128)(2,1)S(1)} collective-permute-done((bf16[256,1024]{1,0:T(8,128)(2,1)S(1)}, bf16[256,1024]{1,0:T(8,128)(2,1)S(1)}, u32[]{:S(2)}, u32[]{:S(2)}) %collective-permute-start.63) | collective-permute-done | bytes 524320 | tf_op jit(solution)/shard_map/ppermute | solution.py:461
  335.7 2.8 place.9
  341.6 3.6 place.10
  345.4 4.9 %collective-permute-done.66.refs_3_ = bf16[256,1024]{1,0:T(8,128)(2,1)S(1)} collective-permute-done((bf16[256,1024]{1,0:T(8,128)(2,1)S(1)}, bf16[256,1024]{1,0:T(8,128)(2,1)S(1)}, u32[]{:S(2)}, u32[]{:S(2)}) %collective-permute-start.66) | collective-permute-done | bytes 524320 | tf_op jit(solution)/shard_map/ppermute | solution.py:461
  351.4 2.1 place.11
  353.4 10.9 %collective-permute-done.64.refs_3_.refs_2_.refs_6_.refs_14_ = bf16[320,1024]{1,0:T(8,128)(2,1)S(1)} collective-permute-done((bf16[320,1024]{1,0:T(8,128)(2,1)S(1)}, bf16[320,1024]{1,0:T(8,128)(2,1)S(1)}, u32[]{:S(2)}, u32[]{:S(2)}) %collective-permute-start.64) | collective-permute-done | bytes 655392 | tf_op jit(solution)/shard_map/ppermute | solution.py:461
  366.5 3.6 place.12
  370.1 5.0 %collective-permute-done.72.refs_3_ = bf16[256,1024]{1,0:T(8,128)(2,1)S(1)} collective-permute-done((bf16[256,1024]{1,0:T(8,128)(2,1)S(1)}, bf16[256,1024]{1,0:T(8,128)(2,1)S(1)}, u32[]{:S(2)}, u32[]{:S(2)}) %collective-permute-start.72) | collective-permute-done | bytes 524320 | tf_op jit(solution)/shard_map/ppermute | solution.py:461
  375.4 2.7 place.13
  379.0 3.3 place.14
  382.3 3.7 place.15
  (458 shorter events, 104.7 us)
Async XLA Ops:
  74.5 17.1 %collective-permute-start.12 = (bf16[384,1024]{1,0:T(8,128)(2,1)S(1)}, bf16[384,1024]{1,0:T(8,128)(2,1)S(1)}, u32[]{:S(2)}, u32[]{:S(2)}) collective-permute-start(bf16[384,1024]{1,0:T(8,128)(2,1)S(1)} %pad_maximum_fusion), channel_id=1, source_target_pairs={{0,4},{2,6},{4,0},{6,2},{8,12},{10,14},{12,8},{14,10},{16,20},{18,... | collective-permute-start | bytes 2359304 | tf_op jit(solution)/shard_map/ppermute | solution.py:461
  91.9 20.5 %collective-permute-start.14 = (bf16[384,1024]{1,0:T(8,128)(2,1)S(1)}, bf16[384,1024]{1,0:T(8,128)(2,1)S(1)}, u32[]{:S(2)}, u32[]{:S(2)}) collective-permute-start(bf16[384,1024]{1,0:T(8,128)(2,1)S(1)} %pad_maximum_fusion.1), channel_id=1, source_target_pairs={{0,2},{2,0},{4,6},{6,4},{8,10},{10,8},{12,14},{14,12},{16,18},{18,... | collective-permute-start | bytes 2359304 | tf_op jit(solution)/shard_map/ppermute | solution.py:461
  93.4 19.0 %collective-permute-start.16 = (bf16[384,1024]{1,0:T(8,128)(2,1)S(1)}, bf16[384,1024]{1,0:T(8,128)(2,1)S(1)}, u32[]{:S(2)}, u32[]{:S(2)}) collective-permute-start(bf16[384,1024]{1,0:T(8,128)(2,1)S(1)} %pad_maximum_fusion.2), channel_id=1, source_target_pairs={{0,8},{2,10},{4,12},{6,14},{8,0},{10,2},{12,4},{14,6},{16,24},{18,... | collective-permute-start | bytes 2359304 | tf_op jit(solution)/shard_map/ppermute | solution.py:461
  95.4 13.5 %collective-permute-start.15 = (bf16[320,1024]{1,0:T(8,128)(2,1)}, bf16[320,1024]{1,0:T(8,128)(2,1)S(1)}, u32[]{:S(2)}, u32[]{:S(2)}) collective-permute-start(bf16[320,1024]{1,0:T(8,128)(2,1)} %pad_maximum_fusion.10), channel_id=1, source_target_pairs={{0,4},{2,6},{4,0},{6,2},{8,12},{10,14},{12,8},{14,10},{16,20},{18,... | collective-permute-start | bytes 1966088 | tf_op jit(solution)/shard_map/ppermute | solution.py:461
  97.2 40.3 %collective-permute-start.17 = (bf16[384,1024]{1,0:T(8,128)(2,1)S(1)}, bf16[384,1024]{1,0:T(8,128)(2,1)S(1)}, u32[]{:S(2)}, u32[]{:S(2)}) collective-permute-start(bf16[384,1024]{1,0:T(8,128)(2,1)S(1)} %pad_maximum_fusion.3), channel_id=1, source_target_pairs={{0,2},{2,0},{4,6},{6,4},{8,10},{10,8},{12,14},{14,12},{16,18},{18,... | collective-permute-start | bytes 2359304 | tf_op jit(solution)/shard_map/ppermute | solution.py:461
  113.5 24.1 %collective-permute-start.19 = (bf16[320,1024]{1,0:T(8,128)(2,1)}, bf16[320,1024]{1,0:T(8,128)(2,1)}, u32[]{:S(2)}, u32[]{:S(2)}) collective-permute-start(bf16[320,1024]{1,0:T(8,128)(2,1)} %pad_maximum_fusion.11), channel_id=1, source_target_pairs={{0,8},{2,10},{4,12},{6,14},{8,0},{10,2},{12,4},{14,6},{16,24},{18,... | collective-permute-start | bytes 1966088 | tf_op jit(solution)/shard_map/ppermute | solution.py:461
  114.6 23.0 %collective-permute-start.18 = (bf16[384,1024]{1,0:T(8,128)(2,1)S(1)}, bf16[384,1024]{1,0:T(8,128)(2,1)S(1)}, u32[]{:S(2)}, u32[]{:S(2)}) collective-permute-start(bf16[384,1024]{1,0:T(8,128)(2,1)S(1)} %pad_maximum_fusion.4), channel_id=1, source_target_pairs={{0,4},{2,6},{4,0},{6,2},{8,12},{10,14},{12,8},{14,10},{16,20},{18,... | collective-permute-start | bytes 2359304 | tf_op jit(solution)/shard_map/ppermute | solution.py:461
  117.0 20.6 %collective-permute-start.20 = (bf16[192,1024]{1,0:T(8,128)(2,1)}, bf16[192,1024]{1,0:T(8,128)(2,1)}, u32[]{:S(2)}, u32[]{:S(2)}) collective-permute-start(bf16[192,1024]{1,0:T(8,128)(2,1)} %pad_maximum_fusion.27), channel_id=1, source_target_pairs={{0,16},{2,18},{4,20},{6,22},{8,24},{10,26},{12,28},{14,30},{16,0},... | collective-permute-start | bytes 1179656 | tf_op jit(solution)/shard_map/ppermute | solution.py:461
  152.3 19.8 %collective-permute-start.24 = (bf16[384,1024]{1,0:T(8,128)(2,1)}, bf16[384,1024]{1,0:T(8,128)(2,1)S(1)}, u32[]{:S(2)}, u32[]{:S(2)}) collective-permute-start(bf16[384,1024]{1,0:T(8,128)(2,1)} %pad_maximum_fusion.5), channel_id=1, source_target_pairs={{0,2},{2,0},{4,6},{6,4},{8,10},{10,8},{12,14},{14,12},{16,18},{18,... | collective-permute-start | bytes 2359304 | tf_op jit(solution)/shard_map/ppermute | solution.py:461
  153.8 13.7 %collective-permute-start.26 = (bf16[192,1024]{1,0:T(8,128)(2,1)S(1)}, bf16[192,1024]{1,0:T(8,128)(2,1)S(1)}, u32[]{:S(2)}, u32[]{:S(2)}) collective-permute-start(bf16[192,1024]{1,0:T(8,128)(2,1)S(1)} %fusion.3), channel_id=1, source_target_pairs={{0,8},{2,10},{4,12},{6,14},{8,0},{10,2},{12,4},{14,6},{16,24},{18,... | collective-permute-start | bytes 1179656 | tf_op jit(solution)/shard_map/ppermute | solution.py:461
  173.4 23.5 %collective-permute-start.28 = (bf16[384,1024]{1,0:T(8,128)(2,1)S(1)}, bf16[384,1024]{1,0:T(8,128)(2,1)S(1)}, u32[]{:S(2)}, u32[]{:S(2)}) collective-permute-start(bf16[384,1024]{1,0:T(8,128)(2,1)S(1)} %slice_dynamic-update-slice_fusion), channel_id=1, source_target_pairs={{0,2},{2,0},{4,6},{6,4},{8,10},{10,8},{12,14},{14,12},{16,18},{18,... | collective-permute-start | bytes 2359304 | tf_op jit(solution)/shard_map/ppermute | solution.py:461
  175.1 21.9 %collective-permute-start.30 = (bf16[256,1024]{1,0:T(8,128)(2,1)S(1)}, bf16[256,1024]{1,0:T(8,128)(2,1)S(1)}, u32[]{:S(2)}, u32[]{:S(2)}) collective-permute-start(bf16[256,1024]{1,0:T(8,128)(2,1)S(1)} %fusion.1), channel_id=1, source_target_pairs={{0,8},{2,10},{4,12},{6,14},{8,0},{10,2},{12,4},{14,6},{16,24},{18,... | collective-permute-start | bytes 1572872 | tf_op jit(solution)/shard_map/ppermute | solution.py:461
  176.0 20.9 %collective-permute-start.29 = (bf16[192,1024]{1,0:T(8,128)(2,1)S(1)}, bf16[192,1024]{1,0:T(8,128)(2,1)S(1)}, u32[]{:S(2)}, u32[]{:S(2)}) collective-permute-start(bf16[192,1024]{1,0:T(8,128)(2,1)S(1)} %fusion.4), channel_id=1, source_target_pairs={{0,4},{2,6},{4,0},{6,2},{8,12},{10,14},{12,8},{14,10},{16,20},{18,... | collective-permute-start | bytes 1179656 | tf_op jit(solution)/shard_map/ppermute | solution.py:461
  176.7 19.5 %collective-permute-start.31 = (bf16[128,1024]{1,0:T(8,128)(2,1)S(1)}, bf16[128,1024]{1,0:T(8,128)(2,1)S(1)}, u32[]{:S(2)}, u32[]{:S(2)}) collective-permute-start(bf16[128,1024]{1,0:T(8,128)(2,1)S(1)} %pad_maximum_fusion.33), channel_id=1, source_target_pairs={{0,16},{2,18},{4,20},{6,22},{8,24},{10,26},{12,28},{14,30},{16,0},... | collective-permute-start | bytes 786440 | tf_op jit(solution)/shard_map/ppermute | solution.py:461
  194.7 24.2 %collective-permute-start.33 = (bf16[384,1024]{1,0:T(8,128)(2,1)S(1)}, bf16[384,1024]{1,0:T(8,128)(2,1)S(1)}, u32[]{:S(2)}, u32[]{:S(2)}) collective-permute-start(bf16[384,1024]{1,0:T(8,128)(2,1)S(1)} %constant_dynamic-update-slice_fusion.8), channel_id=1, source_target_pairs={{0,4},{2,6},{4,0},{6,2},{8,12},{10,14},{12,8},{14,10},{16,20},{18,... | collective-permute-start | bytes 2359304 | tf_op jit(solution)/shard_map/ppermute | solution.py:461
  196.2 22.7 %collective-permute-start.32 = (bf16[384,1024]{1,0:T(8,128)(2,1)S(1)}, bf16[384,1024]{1,0:T(8,128)(2,1)S(1)}, u32[]{:S(2)}, u32[]{:S(2)}) collective-permute-start(bf16[384,1024]{1,0:T(8,128)(2,1)S(1)} %constant_dynamic-update-slice_fusion.6), channel_id=1, source_target_pairs={{0,2},{2,0},{4,6},{6,4},{8,10},{10,8},{12,14},{14,12},{16,18},{18,... | collective-permute-start | bytes 2359304 | tf_op jit(solution)/shard_map/ppermute | solution.py:461
  197.2 21.8 %collective-permute-start.35 = (bf16[192,1024]{1,0:T(8,128)(2,1)S(1)}, bf16[192,1024]{1,0:T(8,128)(2,1)S(1)}, u32[]{:S(2)}, u32[]{:S(2)}) collective-permute-start(bf16[192,1024]{1,0:T(8,128)(2,1)S(1)} %pad_maximum_fusion.29), channel_id=1, source_target_pairs={{0,16},{2,18},{4,20},{6,22},{8,24},{10,26},{12,28},{14,30},{16,0},... | collective-permute-start | bytes 1179656 | tf_op jit(solution)/shard_map/ppermute | solution.py:461
  199.9 19.0 %collective-permute-start.34 = (bf16[192,1024]{1,0:T(8,128)(2,1)S(1)}, bf16[192,1024]{1,0:T(8,128)(2,1)S(1)}, u32[]{:S(2)}, u32[]{:S(2)}) collective-permute-start(bf16[192,1024]{1,0:T(8,128)(2,1)S(1)} %pad_maximum_fusion.28), channel_id=1, source_target_pairs={{0,8},{2,10},{4,12},{6,14},{8,0},{10,2},{12,4},{14,6},{16,24},{18,... | collective-permute-start | bytes 1179656 | tf_op jit(solution)/shard_map/ppermute | solution.py:461
  225.7 20.0 %collective-permute-start.38 = (bf16[384,1024]{1,0:T(8,128)(2,1)S(1)}, bf16[384,1024]{1,0:T(8,128)(2,1)S(1)}, u32[]{:S(2)}, u32[]{:S(2)}) collective-permute-start(bf16[384,1024]{1,0:T(8,128)(2,1)S(1)} %pad_maximum_fusion.7), channel_id=1, source_target_pairs={{0,4},{2,6},{4,0},{6,2},{8,12},{10,14},{12,8},{14,10},{16,20},{18,... | collective-permute-start | bytes 2359304 | tf_op jit(solution)/shard_map/ppermute | solution.py:461
  226.3 19.6 %collective-permute-start.37 = (bf16[384,1024]{1,0:T(8,128)(2,1)S(1)}, bf16[384,1024]{1,0:T(8,128)(2,1)S(1)}, u32[]{:S(2)}, u32[]{:S(2)}) collective-permute-start(bf16[384,1024]{1,0:T(8,128)(2,1)S(1)} %pad_maximum_fusion.6), channel_id=1, source_target_pairs={{0,2},{2,0},{4,6},{6,4},{8,10},{10,8},{12,14},{14,12},{16,18},{18,... | collective-permute-start | bytes 2359304 | tf_op jit(solution)/shard_map/ppermute | solution.py:461
  228.1 16.2 %collective-permute-start.39 = (bf16[256,1024]{1,0:T(8,128)(2,1)S(1)}, bf16[256,1024]{1,0:T(8,128)(2,1)S(1)}, u32[]{:S(2)}, u32[]{:S(2)}) collective-permute-start(bf16[256,1024]{1,0:T(8,128)(2,1)S(1)} %pad_maximum_fusion.16), channel_id=1, source_target_pairs={{0,8},{2,10},{4,12},{6,14},{8,0},{10,2},{12,4},{14,6},{16,24},{18,... | collective-permute-start | bytes 1572872 | tf_op jit(solution)/shard_map/ppermute | solution.py:461
  246.4 20.5 %collective-permute-start.43 = (bf16[352,1024]{1,0:T(8,128)(2,1)S(1)}, bf16[352,1024]{1,0:T(8,128)(2,1)S(1)}, u32[]{:S(2)}, u32[]{:S(2)}) collective-permute-start(bf16[352,1024]{1,0:T(8,128)(2,1)S(1)} %constant_dynamic-update-slice_fusion.16), channel_id=1, source_target_pairs={{0,4},{2,6},{4,0},{6,2},{8,12},{10,14},{12,8},{14,10},{16,20},{18,... | collective-permute-start | bytes 2162696 | tf_op jit(solution)/shard_map/ppermute | solution.py:461
  248.0 19.0 %collective-permute-start.42 = (bf16[384,1024]{1,0:T(8,128)(2,1)S(1)}, bf16[384,1024]{1,0:T(8,128)(2,1)S(1)}, u32[]{:S(2)}, u32[]{:S(2)}) collective-permute-start(bf16[384,1024]{1,0:T(8,128)(2,1)S(1)} %constant_dynamic-update-slice_fusion.10), channel_id=1, source_target_pairs={{0,2},{2,0},{4,6},{6,4},{8,10},{10,8},{12,14},{14,12},{16,18},{18,... | collective-permute-start | bytes 2359304 | tf_op jit(solution)/shard_map/ppermute | solution.py:461
  249.5 17.4 %collective-permute-start.44 = (bf16[256,1024]{1,0:T(8,128)(2,1)S(1)}, bf16[256,1024]{1,0:T(8,128)(2,1)S(1)}, u32[]{:S(2)}, u32[]{:S(2)}) collective-permute-start(bf16[256,1024]{1,0:T(8,128)(2,1)S(1)} %constant_dynamic-update-slice_fusion.22), channel_id=1, source_target_pairs={{0,8},{2,10},{4,12},{6,14},{8,0},{10,2},{12,4},{14,6},{16,24},{18,... | collective-permute-start | bytes 1572872 | tf_op jit(solution)/shard_map/ppermute | solution.py:461
  250.4 16.5 %collective-permute-start.45 = (bf16[64,1024]{1,0:T(8,128)(2,1)S(1)}, bf16[64,1024]{1,0:T(8,128)(2,1)S(1)}, u32[]{:S(2)}, u32[]{:S(2)}) collective-permute-start(bf16[64,1024]{1,0:T(8,128)(2,1)S(1)} %get-tuple-element.586), channel_id=1, source_target_pairs={{0,16},{2,18},{4,20},{6,22},{8,24},{10,26},{12,28},{14,30},{16,0},... | collective-permute-start | bytes 393224 | tf_op jit(solution)/shard_map/ppermute | solution.py:461
  250.8 16.1 %collective-permute-start.46 = (f32[4,1024]{1,0:T(4,128)S(1)}, f32[4,1024]{1,0:T(4,128)S(1)}, u32[]{:S(2)}, u32[]{:S(2)}) collective-permute-start(f32[4,1024]{1,0:T(4,128)S(1)} %fusion.12), channel_id=1, source_target_pairs={{0,2},{2,0},{4,6},{6,4},{8,10},{10,8},{12,14},{14,12},{16,18},{18,... | collective-permute-start | bytes 49160 | tf_op jit(solution)/shard_map/ppermute | solution.py:461
  267.1 22.2 %collective-permute-start.48 = (bf16[224,1024]{1,0:T(8,128)(2,1)S(1)}, bf16[224,1024]{1,0:T(8,128)(2,1)S(1)}, u32[]{:S(2)}, u32[]{:S(2)}) collective-permute-start(bf16[224,1024]{1,0:T(8,128)(2,1)S(1)} %pad_maximum_fusion.26), channel_id=1, source_target_pairs={{0,4},{2,6},{4,0},{6,2},{8,12},{10,14},{12,8},{14,10},{16,20},{18,... | collective-permute-start | bytes 1376264 | tf_op jit(solution)/shard_map/ppermute | solution.py:461
  267.9 23.1 %collective-permute-start.49 = (bf16[320,1024]{1,0:T(8,128)(2,1)S(1)}, bf16[320,1024]{1,0:T(8,128)(2,1)S(1)}, u32[]{:S(2)}, u32[]{:S(2)}) collective-permute-start(bf16[320,1024]{1,0:T(8,128)(2,1)S(1)} %constant_dynamic-update-slice_fusion.33), channel_id=1, source_target_pairs={{0,8},{2,10},{4,12},{6,14},{8,0},{10,2},{12,4},{14,6},{16,24},{18,... | collective-permute-start | bytes 1966088 | tf_op jit(solution)/shard_map/ppermute | solution.py:461
  269.0 22.0 %collective-permute-start.47 = (bf16[384,1024]{1,0:T(8,128)(2,1)S(1)}, bf16[384,1024]{1,0:T(8,128)(2,1)S(1)}, u32[]{:S(2)}, u32[]{:S(2)}) collective-permute-start(bf16[384,1024]{1,0:T(8,128)(2,1)S(1)} %get-tuple-element.616), channel_id=1, source_target_pairs={{0,2},{2,0},{4,6},{6,4},{8,10},{10,8},{12,14},{14,12},{16,18},{18,... | collective-permute-start | bytes 2359304 | tf_op jit(solution)/shard_map/ppermute | solution.py:461
  270.4 18.9 %collective-permute-start.50 = (bf16[192,1024]{1,0:T(8,128)(2,1)S(1)}, bf16[192,1024]{1,0:T(8,128)(2,1)S(1)}, u32[]{:S(2)}, u32[]{:S(2)}) collective-permute-start(bf16[192,1024]{1,0:T(8,128)(2,1)S(1)} %pad_maximum_fusion.30), channel_id=1, source_target_pairs={{0,16},{2,18},{4,20},{6,22},{8,24},{10,26},{12,28},{14,30},{16,0},... | collective-permute-start | bytes 1179656 | tf_op jit(solution)/shard_map/ppermute | solution.py:461
  278.2 30.3 %collective-permute-start.53 = (bf16[256,1024]{1,0:T(8,128)(2,1)S(1)}, bf16[256,1024]{1,0:T(8,128)(2,1)S(1)}, u32[]{:S(2)}, u32[]{:S(2)}) collective-permute-start(bf16[256,1024]{1,0:T(8,128)(2,1)S(1)} %pad_maximum_fusion.17), channel_id=1, source_target_pairs={{0,4},{2,6},{4,0},{6,2},{8,12},{10,14},{12,8},{14,10},{16,20},{18,... | collective-permute-start | bytes 1572872 | tf_op jit(solution)/shard_map/ppermute | solution.py:461
  291.1 17.5 %collective-permute-start.52 = (bf16[384,1024]{1,0:T(8,128)(2,1)S(1)}, bf16[384,1024]{1,0:T(8,128)(2,1)S(1)}, u32[]{:S(2)}, u32[]{:S(2)}) collective-permute-start(bf16[384,1024]{1,0:T(8,128)(2,1)S(1)} %get-tuple-element.630), channel_id=1, source_target_pairs={{0,2},{2,0},{4,6},{6,4},{8,10},{10,8},{12,14},{14,12},{16,18},{18,... | collective-permute-start | bytes 2359304 | tf_op jit(solution)/shard_map/ppermute | solution.py:461
  292.6 15.9 %collective-permute-start.54 = (bf16[192,1024]{1,0:T(8,128)(2,1)S(1)}, bf16[192,1024]{1,0:T(8,128)(2,1)S(1)}, u32[]{:S(2)}, u32[]{:S(2)}) collective-permute-start(bf16[192,1024]{1,0:T(8,128)(2,1)S(1)} %pad_maximum_fusion.31), channel_id=1, source_target_pairs={{0,8},{2,10},{4,12},{6,14},{8,0},{10,2},{12,4},{14,6},{16,24},{18,... | collective-permute-start | bytes 1179656 | tf_op jit(solution)/shard_map/ppermute | solution.py:461
  293.1 15.5 %collective-permute-start.55 = (bf16[128,1024]{1,0:T(8,128)(2,1)S(1)}, bf16[128,1024]{1,0:T(8,128)(2,1)S(1)}, u32[]{:S(2)}, u32[]{:S(2)}) collective-permute-start(bf16[128,1024]{1,0:T(8,128)(2,1)S(1)} %pad_maximum_fusion.34), channel_id=1, source_target_pairs={{0,16},{2,18},{4,20},{6,22},{8,24},{10,26},{12,28},{14,30},{16,0},... | collective-permute-start | bytes 786440 | tf_op jit(solution)/shard_map/ppermute | solution.py:461
  307.2 14.9 %collective-permute-start.62 = (bf16[256,1024]{1,0:T(8,128)(2,1)S(1)}, bf16[256,1024]{1,0:T(8,128)(2,1)S(1)}, u32[]{:S(2)}, u32[]{:S(2)}) collective-permute-start(bf16[256,1024]{1,0:T(8,128)(2,1)S(1)} %fusion.2), channel_id=1, source_target_pairs={{0,4},{2,6},{4,0},{6,2},{8,12},{10,14},{12,8},{14,10},{16,20},{18,... | collective-permute-start | bytes 1572872 | tf_op jit(solution)/shard_map/ppermute | solution.py:461
  308.8 30.1 %collective-permute-start.60 = (bf16[320,1024]{1,0:T(8,128)(2,1)S(1)}, bf16[320,1024]{1,0:T(8,128)(2,1)S(1)}, u32[]{:S(2)}, u32[]{:S(2)}) collective-permute-start(bf16[320,1024]{1,0:T(8,128)(2,1)S(1)} %get-tuple-element.549), channel_id=1, source_target_pairs={{0,8},{2,10},{4,12},{6,14},{8,0},{10,2},{12,4},{14,6},{16,24},{18,... | collective-permute-start | bytes 1966088 | tf_op jit(solution)/shard_map/ppermute | solution.py:461
  310.2 25.2 %collective-permute-start.63 = (bf16[256,1024]{1,0:T(8,128)(2,1)S(1)}, bf16[256,1024]{1,0:T(8,128)(2,1)S(1)}, u32[]{:S(2)}, u32[]{:S(2)}) collective-permute-start(bf16[256,1024]{1,0:T(8,128)(2,1)S(1)} %pad_maximum_fusion.19), channel_id=1, source_target_pairs={{0,8},{2,10},{4,12},{6,14},{8,0},{10,2},{12,4},{14,6},{16,24},{18,... | collective-permute-start | bytes 1572872 | tf_op jit(solution)/shard_map/ppermute | solution.py:461
  312.2 26.8 %collective-permute-start.59 = (bf16[256,1024]{1,0:T(8,128)(2,1)S(1)}, bf16[256,1024]{1,0:T(8,128)(2,1)S(1)}, u32[]{:S(2)}, u32[]{:S(2)}) collective-permute-start(bf16[256,1024]{1,0:T(8,128)(2,1)S(1)} %get-tuple-element.656), channel_id=1, source_target_pairs={{0,4},{2,6},{4,0},{6,2},{8,12},{10,14},{12,8},{14,10},{16,20},{18,... | collective-permute-start | bytes 1572872 | tf_op jit(solution)/shard_map/ppermute | solution.py:461
  322.1 16.5 %collective-permute-start.58 = (bf16[192,1024]{1,0:T(8,128)(2,1)S(1)}, bf16[192,1024]{1,0:T(8,128)(2,1)S(1)}, u32[]{:S(2)}, u32[]{:S(2)}) collective-permute-start(bf16[192,1024]{1,0:T(8,128)(2,1)S(1)} %pad_maximum_fusion.32), channel_id=1, source_target_pairs={{0,2},{2,0},{4,6},{6,4},{8,10},{10,8},{12,14},{14,12},{16,18},{18,... | collective-permute-start | bytes 1179656 | tf_op jit(solution)/shard_map/ppermute | solution.py:461
  322.5 22.8 %collective-permute-start.67 = (bf16[256,1024]{1,0:T(8,128)(2,1)S(1)}, bf16[256,1024]{1,0:T(8,128)(2,1)S(1)}, u32[]{:S(2)}, u32[]{:S(2)}) collective-permute-start(bf16[256,1024]{1,0:T(8,128)(2,1)S(1)} %pad_maximum_fusion.21), channel_id=1, source_target_pairs={{0,4},{2,6},{4,0},{6,2},{8,12},{10,14},{12,8},{14,10},{16,20},{18,... | collective-permute-start | bytes 1572872 | tf_op jit(solution)/shard_map/ppermute | solution.py:461
  335.4 14.9 %collective-permute-start.66 = (bf16[256,1024]{1,0:T(8,128)(2,1)S(1)}, bf16[256,1024]{1,0:T(8,128)(2,1)S(1)}, u32[]{:S(2)}, u32[]{:S(2)}) collective-permute-start(bf16[256,1024]{1,0:T(8,128)(2,1)S(1)} %pad_maximum_fusion.20), channel_id=1, source_target_pairs={{0,2},{2,0},{4,6},{6,4},{8,10},{10,8},{12,14},{14,12},{16,18},{18,... | collective-permute-start | bytes 1572872 | tf_op jit(solution)/shard_map/ppermute | solution.py:461
  339.1 25.2 %collective-permute-start.64 = (bf16[320,1024]{1,0:T(8,128)(2,1)S(1)}, bf16[320,1024]{1,0:T(8,128)(2,1)S(1)}, u32[]{:S(2)}, u32[]{:S(2)}) collective-permute-start(bf16[320,1024]{1,0:T(8,128)(2,1)S(1)} %get-tuple-element.609), channel_id=1, source_target_pairs={{0,2},{2,0},{4,6},{6,4},{8,10},{10,8},{12,14},{14,12},{16,18},{18,... | collective-permute-start | bytes 1966088 | tf_op jit(solution)/shard_map/ppermute | solution.py:461
  340.9 23.4 %collective-permute-start.65 = (bf16[320,1024]{1,0:T(8,128)(2,1)S(1)}, bf16[320,1024]{1,0:T(8,128)(2,1)S(1)}, u32[]{:S(2)}, u32[]{:S(2)}) collective-permute-start(bf16[320,1024]{1,0:T(8,128)(2,1)S(1)} %get-tuple-element.604), channel_id=1, source_target_pairs={{0,4},{2,6},{4,0},{6,2},{8,12},{10,14},{12,8},{14,10},{16,20},{18,... | collective-permute-start | bytes 1966088 | tf_op jit(solution)/shard_map/ppermute | solution.py:461
  345.3 20.2 %collective-permute-start.57 = (f32[4,1024]{1,0:T(4,128)S(1)}, f32[4,1024]{1,0:T(4,128)S(1)}, u32[]{:S(2)}, u32[]{:S(2)}) collective-permute-start(f32[4,1024]{1,0:T(4,128)S(1)} %add.378), channel_id=1, source_target_pairs={{0,16},{2,18},{4,20},{6,22},{8,24},{10,26},{12,28},{14,30},{16,0},... | collective-permute-start | bytes 49160 | tf_op jit(solution)/shard_map/ppermute | solution.py:461
  350.3 24.8 %collective-permute-start.72 = (bf16[256,1024]{1,0:T(8,128)(2,1)S(1)}, bf16[256,1024]{1,0:T(8,128)(2,1)S(1)}, u32[]{:S(2)}, u32[]{:S(2)}) collective-permute-start(bf16[256,1024]{1,0:T(8,128)(2,1)S(1)} %pad_maximum_fusion.23), channel_id=1, source_target_pairs={{0,2},{2,0},{4,6},{6,4},{8,10},{10,8},{12,14},{14,12},{16,18},{18,... | collective-permute-start | bytes 1572872 | tf_op jit(solution)/shard_map/ppermute | solution.py:461
  350.6 24.9 %collective-permute-start.73 = (bf16[384,1024]{1,0:T(8,128)(2,1)S(1)}, bf16[384,1024]{1,0:T(8,128)(2,1)S(1)}, u32[]{:S(2)}, u32[]{:S(2)}) collective-permute-start(bf16[384,1024]{1,0:T(8,128)(2,1)S(1)} %constant_dynamic-update-slice_fusion.64), channel_id=1, source_target_pairs={{0,4},{2,6},{4,0},{6,2},{8,12},{10,14},{12,8},{14,10},{16,20},{18,... | collective-permute-start | bytes 2359304 | tf_op jit(solution)/shard_map/ppermute | solution.py:461
  364.4 14.6 %collective-permute-start.70 = (bf16[128,1024]{1,0:T(8,128)(2,1)S(1)}, bf16[128,1024]{1,0:T(8,128)(2,1)S(1)}, u32[]{:S(2)}, u32[]{:S(2)}) collective-permute-start(bf16[128,1024]{1,0:T(8,128)(2,1)S(1)} %pad_maximum_fusion.36), channel_id=1, source_target_pairs={{0,4},{2,6},{4,0},{6,2},{8,12},{10,14},{12,8},{14,10},{16,20},{18,... | collective-permute-start | bytes 786440 | tf_op jit(solution)/shard_map/ppermute | solution.py:461
  365.2 13.8 %collective-permute-start.71 = (bf16[256,1024]{1,0:T(8,128)(2,1)S(1)}, bf16[256,1024]{1,0:T(8,128)(2,1)S(1)}, u32[]{:S(2)}, u32[]{:S(2)}) collective-permute-start(bf16[256,1024]{1,0:T(8,128)(2,1)S(1)} %get-tuple-element.600), channel_id=1, source_target_pairs={{0,8},{2,10},{4,12},{6,14},{8,0},{10,2},{12,4},{14,6},{16,24},{18,... | collective-permute-start | bytes 1572872 | tf_op jit(solution)/shard_map/ppermute | solution.py:461
  (95 other events, 621.7 us)
